TPU v7x, 256 devices: a whole 4x4x8 slice. The times are simulated.
256 devices in a mesh: wide: 64 (over x, z, core), narrow: 4 (over y).
Axes of the slice: x: 4, y: 4, z: 8, core: 2. Of those that a mesh axis runs over, the one named last changes fastest.
Arguments:
- node_features: bfloat16 [524288, 256], P(('wide', 'narrow'))
- query_weight: bfloat16 [256, 256], replicated, may hold values from -0.375 to 0.375
- key_weight: bfloat16 [256, 256], replicated, may hold values from -0.375 to 0.375
- value_weight: bfloat16 [256, 256], replicated, may hold values from -0.375 to 0.375
- graph_weight: bfloat16 [256, 256], replicated, may hold values from -0.375 to 0.375
- norm_gain: float32 [256], replicated, may hold values from 0.5 to 1.5
- tile_values: bfloat16 [24576, 128, 128], P(('wide', 'narrow')), may hold values from -0.21875 to 0.21875
- tile_rows: int32 [256, 96], P(('wide', 'narrow')), may hold values from 0 to 15
- tile_cols: int32 [256, 96], P(('wide', 'narrow')), may hold values from 0 to 127
- tile_count: int32 [256], P(('wide', 'narrow')), may hold values from 24 to 96, as said below
- send_list: int32 [256, 64], P(('wide', 'narrow')), may hold values from -1 to 15
Outputs:
- layer_out: bfloat16 [524288, 256], P(('wide', 'narrow'))
Inputs may be any that keep to these rules, and one draw needn't show every extreme that they name: `tile_count`: on one device some slots are live up to the full 96. `send_list`: entry [s, j] names one of device s's 16 row blocks, or -1. `tile_cols`: index into the 128 column blocks of the device's column space.
All inputs are finite; a program needn't handle non-finite values.
Results may differ from a plain program's by a relative error of at most 0.0055.
Values may be sent and summed in bfloat16 or wider, within the bound.
No kernel may reach another device: no remote copies, remote signals or barrier semaphores. Data moves between devices by JAX's collectives and lax.ppermute only.
A program may use at most 128 MiB of HBM per device.

v0:
```python
import jax
import jax.numpy as jnp
from jax import lax
from jax.sharding import PartitionSpec as P

D = 256


def shards(
    node_features,
    query_weight,
    key_weight,
    value_weight,
    graph_weight,
    norm_gain,
    tile_values,
    tile_rows,
    tile_cols,
    tile_count,
    send_list,
):
    highest = lax.Precision.HIGHEST
    rows_dev = node_features.shape[0]
    block = tile_values.shape[1]
    nblocks = rows_dev // block
    total = float(rows_dev * lax.axis_size("wide") * lax.axis_size("narrow"))
    width = float(D)
    query = jnp.dot(node_features, query_weight, preferred_element_type=jnp.float32)
    keys = jnp.dot(node_features, key_weight, preferred_element_type=jnp.float32)
    values = jnp.dot(node_features, value_weight, preferred_element_type=jnp.float32)
    query_sq, key_sq = lax.psum((jnp.sum(query * query), jnp.sum(keys * keys)), ("wide", "narrow"))
    key_feat = keys * keys * (total * width / key_sq)
    kv_total, ks_total = lax.psum(
        (jnp.dot(key_feat.T, values, precision=highest), jnp.sum(key_feat, 0)), ("wide", "narrow")
    )
    kv_mean = kv_total / total
    key_mean = ks_total / total
    query_feat = query * query * (total * width / query_sq)
    numer = jnp.dot(query_feat, kv_mean, precision=highest) + width * values
    denom = jnp.sum(query_feat * key_mean[None, :], 1, keepdims=True) + width
    attention = numer / denom
    send_index = send_list[0]
    live_send = send_index >= 0
    safe_send = jnp.maximum(send_index, 0)

    def spread_rows(blocks):
        group = lax.all_gather(blocks, "narrow", axis=0, tiled=True)
        chosen = jnp.take(blocks, safe_send, axis=0)
        outgoing = jnp.where(live_send[:, None, None], chosen, jnp.zeros_like(chosen))
        received = lax.all_to_all(outgoing, "wide", split_axis=0, concat_axis=0, tiled=True)
        return jnp.concatenate([group, received], 0)

    active = jnp.arange(tile_rows.shape[1], dtype=jnp.int32) < tile_count[0]
    onehot = (
        (tile_rows[0][None, :] == jnp.arange(nblocks, dtype=jnp.int32)[:, None]) & active[None, :]
    ).astype(jnp.float32)
    columns = tile_cols[0]

    def propagate(buffer):
        gathered = jnp.take(buffer, columns, axis=0)
        prod = jnp.einsum("tij,tjd->tid", tile_values, gathered, preferred_element_type=jnp.float32)
        out = jnp.einsum("rt,tid->rid", onehot, prod, precision=highest)
        return out.astype(jnp.bfloat16)

    hop_zero = jnp.dot(node_features, graph_weight, preferred_element_type=jnp.float32).astype(
        jnp.bfloat16
    )
    buffer = spread_rows(hop_zero.reshape(nblocks, block, D))
    hop_one = propagate(buffer)
    hop_two = propagate(spread_rows(hop_one))
    graph_part = (
        hop_zero.astype(jnp.float32)
        + hop_one.reshape(rows_dev, D).astype(jnp.float32)
        + hop_two.reshape(rows_dev, D).astype(jnp.float32)
    ) / 3.0
    mixed = attention + graph_part
    center = mixed - jnp.mean(mixed, 1, keepdims=True)
    scale = lax.rsqrt(jnp.mean(center * center, 1, keepdims=True) + 1e-05)
    return (norm_gain[None, :] * center * scale).astype(jnp.bfloat16)


def solution(mesh):
    return jax.shard_map(
        shards,
        mesh=mesh,
        in_specs=(
            P(("wide", "narrow"), None),
            P(),
            P(),
            P(),
            P(),
            P(),
            P(("wide", "narrow"), None, None),
            P(("wide", "narrow"), None),
            P(("wide", "narrow"), None),
            P(("wide", "narrow")),
            P(("wide", "narrow"), None),
        ),
        out_specs=P(("wide", "narrow"), None),
        check_vma=False,
    )
```

profile of v0, /device:TPU:1, one launch (start us, length us, event | category | flops | bytes accessed | tf_op | source)
XLA Modules:
  0.0 618.1 jit_solution(577113891096074729)
XLA Ops:
  14.0 4.0 gather_fusion
  21.9 13.3 %all-to-all-start = ((bf16[64,128,256]{2,1,0:T(8,128)(2,1)}), bf16[64,128,256]{2,1,0:T(8,128)(2,1)}, u32[]{:S(2)}, u32[]{:S(2)}) async-start(bf16[64,128,256]{2,1,0:T(8,128)(2,1)} %select_select_fusion.1), calls=%async_computation | async-start | bytes 8388608 | tf_op jit(solution)/shard_map/all_to_all | solution.py:50
  36.6 53.2 %all-gather.3.cloned.1.call-done = bf16[64,128,256]{2,1,0:T(8,128)(2,1)} async-done(((bf16[16,128,256]{2,1,0:T(8,128)(2,1)}), bf16[64,128,256]{2,1,0:T(8,128)(2,1)}) %all-gather.3.cloned.1.call-update) | async-done | bytes 4194320 | tf_op jit(solution)/shard_map/all_gather | solution.py:47
  89.9 41.2 %all-to-all-done = bf16[64,128,256]{2,1,0:T(8,128)(2,1)} async-done(((bf16[64,128,256]{2,1,0:T(8,128)(2,1)}), bf16[64,128,256]{2,1,0:T(8,128)(2,1)}, u32[]{:S(2)}, u32[]{:S(2)}) %all-to-all-start) | async-done | bytes 4194336 | tf_op jit(solution)/shard_map/all_to_all | solution.py:50
  131.1 7.4 %pad_maximum_fusion = bf16[128,128,256]{2,1,0:T(8,128)(2,1)} fusion(bf16[64,128,256]{2,1,0:T(8,128)(2,1)} %all-to-all-done, bf16[64,128,256]{2,1,0:T(8,128)(2,1)} %all-gather.3.cloned.1.call-done), kind=kLoop, calls=%fused_computation.4 | loop fusion | flops 4194304 | bytes 16777216 | tf_op jit(solution)/shard_map/concatenate | solution.py:51
  138.5 9.3 %gather_fusion.1 = bf16[96,128,256]{2,1,0:T(8,128)(2,1)} fusion(bf16[128,128,256]{2,1,0:T(8,128)(2,1)} %pad_maximum_fusion, s32[1024]{0:T(1024)S(1)} %pad_clamp_fusion), kind=kCustom, calls=%fused_computation.1.clone | custom fusion | bytes 12583296 | tf_op jit(solution)/shard_map/jit(_take)/gather | solution.py:60
  147.8 9.3 %fusion.6 = f32[96,128,256]{1,2,0:T(8,128)} fusion(bf16[96,128,128]{2,1,0:T(8,128)(2,1)S(1)} %copy-done, bf16[96,128,256]{2,1,0:T(8,128)(2,1)} %gather_fusion.1, pred[96]{0:T(512)(128)(4,1)S(1)} %compare_and_fusion), kind=kOutput, calls=%fused_computation.12 | convolution fusion | flops 808452096 | bytes 22020192 | tf_op jit(solution)/shard_map/tij,tjd->tid/dot_general | solution.py:61
  157.2 12.7 %copy.45 = f32[96,128,256]{2,0,1:T(8,128)} copy(f32[96,128,256]{1,2,0:T(8,128)} %fusion.6) | data formatting | bytes 25165824 | tf_op jit(solution)/shard_map/tij,tjd->tid/dot_general | solution.py:61
  169.9 7.9 %convolution_convert_fusion.2 = bf16[16,128,256]{2,0,1:T(8,128)(2,1)} fusion(f32[96,128,256]{2,0,1:T(8,128)} %copy.45, s32[96]{0:T(128)S(1)} %bitcast.54, pred[96]{0:T(512)(128)(4,1)S(1)} %iota_compare_fusion.1), kind=kOutput, calls=%fused_computation.36 | convolution fusion | flops 604507136 | bytes 13631968 | tf_op jit(solution)/shard_map/rt,tid->rid/dot_general | solution.py:62
  180.3 4.0 gather_fusion.2
  184.3 4.0 select_select_fusion
  188.3 18.5 %all-to-all-start.1 = ((bf16[64,128,256]{2,1,0:T(8,128)(2,1)}), bf16[64,128,256]{2,1,0:T(8,128)(2,1)}, u32[]{:S(2)}, u32[]{:S(2)}) async-start(bf16[64,128,256]{2,1,0:T(8,128)(2,1)} %select_select_fusion), calls=%async_computation.1 | async-start | bytes 8388608 | tf_op jit(solution)/shard_map/all_to_all | solution.py:50
  211.5 132.7 %psum.29 = f32[]{:T(128)} all-reduce(f32[]{:T(128)} %get-tuple-element.11), channel_id=1, replica_groups=mesh['wide'=64,'narrow'=4] {'wide','narrow'}, use_global_device_ids=true, to_apply=%region_3.0 | all-reduce | flops 1 | bytes 8 | tf_op jit(solution)/shard_map/psum | solution.py:31
  348.1 4.3 fusion.17
  357.9 75.6 %all-reduce = (f32[256]{0:T(256)S(1)}, f32[]{:T(128)}) all-reduce(f32[256]{0:T(256)S(1)} %multiply_reduce_fusion.2, f32[]{:T(128)} %get-tuple-element.13), channel_id=1, replica_groups=mesh['wide'=64,'narrow'=4] {'wide','narrow'}, use_global_device_ids=true, to_apply=%region_6.0 | all-reduce | flops 257 | bytes 2056 | tf_op jit(solution)/shard_map/psum | solution.py:33
  439.4 6.5 %copy.48 = bf16[64,128,256]{2,0,1:T(8,128)(2,1)} copy(bf16[64,128,256]{2,1,0:T(8,128)(2,1)} %all-to-all-done.1) | data formatting | bytes 8388608 | tf_op jit(solution)/shard_map/all_to_all | solution.py:50
  445.9 7.8 %pad_maximum_fusion.1 = bf16[128,128,256]{2,0,1:T(8,128)(2,1)} fusion(bf16[64,128,256]{2,0,1:T(8,128)(2,1)} %copy.48, bf16[64,128,256]{2,0,1:T(8,128)(2,1)} %all-gather.5.cloned.1.call-done), kind=kLoop, calls=%fused_computation.5 | loop fusion | flops 16777216 | bytes 16777216 | tf_op jit(solution)/shard_map/concatenate | solution.py:51
  453.7 11.4 %copy.49 = bf16[128,128,256]{2,1,0:T(8,128)(2,1)} copy(bf16[128,128,256]{2,0,1:T(8,128)(2,1)} %pad_maximum_fusion.1) | data formatting | bytes 16777216 | tf_op jit(solution)/shard_map/concatenate | solution.py:51
  465.1 9.4 %gather_fusion.3 = bf16[96,128,256]{2,1,0:T(8,128)(2,1)} fusion(bf16[128,128,256]{2,1,0:T(8,128)(2,1)} %copy.49, s32[1024]{0:T(1024)S(1)} %pad_clamp_fusion), kind=kCustom, calls=%fused_computation.3.clone | custom fusion | bytes 12583296 | tf_op jit(solution)/shard_map/jit(_take)/gather | solution.py:60
  474.5 9.3 %fusion.9 = f32[96,128,256]{1,2,0:T(8,128)} fusion(bf16[96,128,128]{2,1,0:T(8,128)(2,1)S(1)} %copy-done, bf16[96,128,256]{2,1,0:T(8,128)(2,1)} %gather_fusion.3, pred[96]{0:T(512)(128)(4,1)S(1)} %compare_and_fusion), kind=kOutput, calls=%fused_computation.13 | convolution fusion | flops 808452096 | bytes 22020192 | tf_op jit(solution)/shard_map/tij,tjd->tid/dot_general | solution.py:61
  483.8 12.7 %copy.51 = f32[96,128,256]{2,0,1:T(8,128)} copy(f32[96,128,256]{1,2,0:T(8,128)} %fusion.9) | data formatting | bytes 25165824 | tf_op jit(solution)/shard_map/tij,tjd->tid/dot_general | solution.py:61
  496.5 8.0 %fusion.20 = f32[16,128,256]{2,0,1:T(8,128)} fusion(f32[96,128,256]{2,0,1:T(8,128)} %copy.51, s32[96]{0:T(128)S(1)} %bitcast.55, pred[96]{0:T(512)(128)(4,1)S(1)} %iota_compare_fusion.1), kind=kOutput, calls=%fused_computation.35 | convolution fusion | flops 605031424 | bytes 14680544 | tf_op jit(solution)/shard_map/rt,tid->rid/dot_general | solution.py:62
  507.9 91.1 %all-reduce.3.cloned.1.call-done = f32[256,256]{1,0:T(8,128)} async-done(((f32[256,256]{1,0:T(8,128)}), f32[256,256]{1,0:T(8,128)}) %all-reduce.3.cloned.1.call-update) | async-done | bytes 262160 | tf_op jit(solution)/shard_map/psum | solution.py:33
  599.1 7.4 %fusion.38 = (f32[2048]{0:T(1024)S(1)}, f32[2048,256]{0,1:T(8,128)S(1)}) fusion(f32[32,8,16,128]{3,2,1,0:T(8,128)} %bitcast.53, f32[32,8,16,128]{3,2,1,0:T(8,128)} %bitcast.52, bf16[2048,256]{0,1:T(8,128)(2,1)} %convolution_convert_fusion, f32[2048]{0:T(1024)S(1)} %broadcast_add_fusion, f32[2048,256]{0,1:T(8,128)} %copy-done.2, ...), kind=kOutput, calls=%fused_computation.65 | convolution fusion | flops 1615919104 | bytes 11812868 | tf_op jit(solution)/shard_map/dot_general | solution.py:39
  (51 shorter events, 39.6 us)
Async XLA Ops:
  7.4 140.5 %copy-start = (bf16[96,128,128]{2,1,0:T(8,128)(2,1)S(1)}, bf16[96,128,128]{2,1,0:T(8,128)(2,1)}, u32[]{:S(2)}) copy-start(bf16[96,128,128]{2,1,0:T(8,128)(2,1)} %param.21) | copy-start | bytes 9437188
  21.9 14.7 %copy-start.8 = (s32[1,96]{1,0:T(1,128)S(1)}, s32[1,96]{1,0:T(1,128)}, u32[]{:S(2)}) copy-start(s32[1,96]{1,0:T(1,128)} %param.23) | copy-start | bytes 1156
  21.9 109.2 %all-to-all-start = ((bf16[64,128,256]{2,1,0:T(8,128)(2,1)}), bf16[64,128,256]{2,1,0:T(8,128)(2,1)}, u32[]{:S(2)}, u32[]{:S(2)}) async-start(bf16[64,128,256]{2,1,0:T(8,128)(2,1)} %select_select_fusion.1), calls=%async_computation | async-start | bytes 8388608 | tf_op jit(solution)/shard_map/all_to_all | solution.py:50
  35.2 54.7 %all-gather.3.cloned.1.call-start = ((), (), s32[]{:S(2)}) async-start(), calls=%async_computation.3 | async-start | bytes 5242880 | tf_op jit(solution)/shard_map/all_gather | solution.py:47
  157.2 12.7 %copy-start.6 = (s32[1,96]{1,0:T(1,128)S(1)}, s32[1,96]{1,0:T(1,128)}, u32[]{:S(2)}) copy-start(s32[1,96]{1,0:T(1,128)} %param.22) | copy-start | bytes 1156
  188.3 19.3 %copy-start.3 = (bf16[256,256]{1,0:T(8,128)(2,1)S(1)}, bf16[256,256]{1,0:T(8,128)(2,1)}, u32[]{:S(2)}) copy-start(bf16[256,256]{1,0:T(8,128)(2,1)} %param.17) | copy-start | bytes 393220
  188.3 251.1 %all-to-all-start.1 = ((bf16[64,128,256]{2,1,0:T(8,128)(2,1)}), bf16[64,128,256]{2,1,0:T(8,128)(2,1)}, u32[]{:S(2)}, u32[]{:S(2)}) async-start(bf16[64,128,256]{2,1,0:T(8,128)(2,1)} %select_select_fusion), calls=%async_computation.1 | async-start | bytes 8388608 | tf_op jit(solution)/shard_map/all_to_all | solution.py:50
  206.8 138.1 %copy-start.4 = (bf16[256,256]{1,0:T(8,128)(2,1)S(1)}, bf16[256,256]{1,0:T(8,128)(2,1)}, u32[]{:S(2)}) copy-start(bf16[256,256]{1,0:T(8,128)(2,1)} %param.18) | copy-start | bytes 393220
  206.8 239.1 %all-gather.5.cloned.1.call-start = ((), (), s32[]{:S(2)}) async-start(), calls=%async_computation.4 | async-start | bytes 5242880 | tf_op jit(solution)/shard_map/all_gather | solution.py:47
  207.5 391.5 %all-reduce.3.cloned.1.call-start = ((), (), s32[]{:S(2)}) async-start(), calls=%async_computation.2 | async-start | bytes 524288 | tf_op jit(solution)/shard_map/psum | solution.py:33
  344.9 3.3 copy-start.1
  346.7 1.4 copy-start.2
  348.1 6.2 copy-start.5
  599.1 7.7 %copy-start.7 = (f32[256]{0:T(256)S(1)}, f32[256]{0:T(256)}, u32[]{:S(2)}) copy-start(f32[256]{0:T(256)} %param.20) | copy-start | bytes 3076
Sparse Core Ops, SparseCore 0:
  37.8 51.9 all-gather.2
  209.4 52.4 all-gather.4
Sparse Core Ops, SparseCore 1:
  352.5 246.5 all-reduce.2
where the time goes:
time: 628 us; the launch traced here: 618 us
  blocking collectives  208 us (33%)
  waiting for transfers between devices  187 us (30%)
  local copies, waits for them, and re-layouts  85.2 us (14%)
  matrix products  58.3 us (9%)
  starting transfers between devices  31.9 us (5%)
  other arithmetic  30.1 us (5%)
  between operations  17.4 us (3%)
    psum x1, blocking collectives, shards(): lax.psum((jnp.sum(query * query), jnp.sum(keys * keys)), ('wide', 'narrow'))  133 us
    psum x1, waiting for transfers between devices, shards(): lax.psum((jnp.dot(key_feat.T, values, precision=highest), jnp.sum(key_fea...  91.1 us
    psum x1, blocking collectives, shards(): lax.psum((jnp.dot(key_feat.T, values, precision=highest), jnp.sum(key_fea...  75.6 us
    all_gather x2, waiting for transfers between devices, spread_rows(): group = lax.all_gather(blocks, 'narrow', axis=0, tiled=True)  53.2 us
    all_to_all x2, waiting for transfers between devices, spread_rows(): lax.all_to_all(outgoing, 'wide', split_axis=0, concat_axis=0, tiled=True)  41.2 us
    all_to_all x2, starting transfers between devices, spread_rows(): lax.all_to_all(outgoing, 'wide', split_axis=0, concat_axis=0, tiled=True)  31.8 us
    dot_general x2, local copies, waits for them, and re-layouts, propagate(): jnp.einsum('tij,tjd->tid', tile_values, gathered, preferred_element_type=...  25.4 us
    gather x2, local copies, waits for them, and re-layouts, propagate(): gathered = jnp.take(buffer, columns, axis=0)  18.8 us
  transfers between devices with their start and end apart: 5, of which 3 were waited for; matrix products, arithmetic and copies ran while one was open for 14% of the time, Pallas kernels for 0%

commit v1 on v0

v1 whole, which is shorter than its diff:
```python
import functools

import jax
import jax.numpy as jnp
from jax import lax
from jax.experimental import pallas as pl
from jax.experimental.pallas import tpu as pltpu
from jax.sharding import PartitionSpec as P

D = 256
BLOCK = 128
UNROLL = 8
CHUNK = 256
F32 = jnp.float32
BF16 = jnp.bfloat16
HIGHEST = lax.Precision.HIGHEST
SMEM = pl.BlockSpec(memory_space=pltpu.SMEM)
VMEM = pl.BlockSpec(memory_space=pltpu.VMEM)
ANY = pl.BlockSpec(memory_space=pl.ANY)


def params(mib):
    return pltpu.CompilerParams(vmem_limit_bytes=mib << 20)


def cost(flops, nbytes):
    return pl.CostEstimate(flops=flops, bytes_accessed=nbytes, transcendentals=0)


def send_blocks(send, src, zeros, out, sem):
    zeros[...] = jnp.zeros_like(zeros)

    def one(w, _):
        index = send[0, w]

        @pl.when(index >= 0)
        def _():
            pltpu.make_async_copy(src.at[jnp.maximum(index, 0)], out.at[w], sem).start()

        @pl.when(index < 0)
        def _():
            pltpu.make_async_copy(zeros, out.at[w], sem).start()

        return 0

    lax.fori_loop(0, out.shape[0], one, 0)
    pltpu.make_async_copy(out, out, sem).wait()


def start_kernel(send, x, weight, h_ref, out, zeros, sem):
    def one(b, _):
        rows = pl.ds(pl.multiple_of(b * BLOCK, BLOCK), BLOCK)
        h_ref[b] = jnp.dot(x[rows, :], weight[...], preferred_element_type=F32).astype(BF16)
        return 0

    lax.fori_loop(0, h_ref.shape[0], one, 0, unroll=True)
    send_blocks(send, h_ref, zeros, out, sem)


def start(send, x, weight, peers):
    nblocks = x.shape[0] // BLOCK
    return pl.pallas_call(
        start_kernel,
        out_shape=(
            jax.ShapeDtypeStruct((nblocks, BLOCK, D), BF16),
            jax.ShapeDtypeStruct((peers, BLOCK, D), BF16),
        ),
        in_specs=[SMEM, VMEM, VMEM],
        out_specs=(VMEM, ANY),
        scratch_shapes=[pltpu.VMEM((BLOCK, D), BF16), pltpu.SemaphoreType.DMA],
        compiler_params=params(16),
        name="project_send",
    )(send, x, weight)


def stats_kernel(x, qw, kw, vw, out, keys_sq, values, sums):
    steps = x.shape[0] // CHUNK
    ksum = jnp.zeros((1, D), F32)
    qsum = jnp.zeros((1, D), F32)
    for c in range(steps):
        rows = pl.ds(c * CHUNK, CHUNK)
        part = x[rows, :]
        query = jnp.dot(part, qw[...], preferred_element_type=F32)
        keys = jnp.dot(part, kw[...], preferred_element_type=F32)
        values[rows, :] = jnp.dot(part, vw[...], preferred_element_type=F32)
        keys_sq[rows, :] = keys * keys
        ksum = ksum + jnp.sum(keys * keys, 0, keepdims=True)
        qsum = qsum + jnp.sum(query * query, 0, keepdims=True)
    ktotal = jnp.sum(ksum, 1, keepdims=True)
    qtotal = jnp.sum(qsum, 1, keepdims=True)
    divisor = jnp.where(ktotal > 0, ktotal, 1.0)
    sums[...] = jnp.zeros_like(sums)

    def one(c, _):
        rows = pl.ds(pl.multiple_of(c * CHUNK, CHUNK), CHUNK)
        feat = keys_sq[rows, :] / divisor
        sums[...] += lax.dot_general(
            feat, values[rows, :], (((0,), (0,)), ((), ())),
            precision=HIGHEST, preferred_element_type=F32,
        )
        return 0

    lax.fori_loop(0, steps, one, 0)
    peers = out.shape[0]
    each = D // peers
    out[:, 4:5, :] = jnp.broadcast_to((ksum / divisor)[None], (peers, 1, D))
    out[:, 5:6, :] = jnp.broadcast_to(ktotal[None], (peers, 1, D))
    out[:, 6:7, :] = jnp.broadcast_to(qtotal[None], (peers, 1, D))
    out[:, 7:8, :] = jnp.zeros((peers, 1, D), F32)
    for w in range(peers):
        out[w, 0:each, :] = sums[w * each:(w + 1) * each, :]


def stats(x, qw, kw, vw, peers):
    rows = x.shape[0]
    return pl.pallas_call(
        stats_kernel,
        out_shape=jax.ShapeDtypeStruct((peers, 8, D), F32),
        in_specs=[VMEM] * 4,
        out_specs=VMEM,
        scratch_shapes=[pltpu.VMEM((rows, D), F32)] * 2 + [pltpu.VMEM((D, D), F32)],
        compiler_params=params(24),
        cost_estimate=cost(rows * D * D * 18, 2 << 20),
        name="attention_sums",
    )(x, qw, kw, vw)


def merge(parts):
    total = jnp.sum(parts[:, 5:6, :], 0, keepdims=True)
    weight = parts[:, 5:6, :] / jnp.where(total > 0, total, 1.0)
    means = jnp.sum(parts[:, :5, :] * weight, 0)
    return jnp.concatenate([means, total[0], jnp.sum(parts[:, 6:7, :], 0), jnp.zeros((1, D), F32)], 0)


def all_sums(parts):
    received = lax.all_to_all(parts, "wide", 0, 0, tiled=True)
    mine = merge(received)
    for step in (1, 2):
        other = lax.ppermute(mine, "narrow", [(i, i ^ step) for i in range(lax.axis_size("narrow"))])
        mine = merge(jnp.stack([mine, other]))
    return lax.all_to_all(jnp.broadcast_to(mine[None], parts.shape), "wide", 0, 0, tiled=True)


def collect(rows, cols, count, first, last, spare, lists):
    slots, places, targets = lists

    def one(t, n):
        c = cols[0, t]
        slots[n] = t
        places[n] = c - first
        targets[n] = rows[0, t]
        return n + ((c >= first) & (c < last)).astype(jnp.int32)

    n = lax.fori_loop(0, count[0], one, jnp.int32(0))
    for u in range(UNROLL):
        slots[n + u] = 0
        places[n + u] = 0
        targets[n + u] = spare
    return n


def add_tiles(n, lists, tiles, blocks, acc):
    slots, places, targets = lists

    def step(i, _):
        prods = [
            jnp.dot(tiles[slots[i * UNROLL + u]], blocks[places[i * UNROLL + u]], preferred_element_type=F32)
            for u in range(UNROLL)
        ]
        for u in range(UNROLL):
            r = targets[i * UNROLL + u]
            acc[r] = acc[r] + prods[u]
        return 0

    lax.fori_loop(0, (n + UNROLL - 1) // UNROLL, step, 0)


def local_kernel(rows, cols, count, tiles, blocks, acc, *lists):
    n = collect(rows, cols, count, 0, blocks.shape[0], acc.shape[0] - 1, lists)
    acc[...] = jnp.zeros_like(acc)
    add_tiles(n, lists, tiles, blocks, acc)


def lists_of(rows):
    return [pltpu.SMEM((rows.shape[1] + UNROLL,), jnp.int32)] * 3


def local_tiles(rows, cols, count, tiles, blocks, nblocks):
    return pl.pallas_call(
        local_kernel,
        out_shape=jax.ShapeDtypeStruct((nblocks + 1, BLOCK, D), F32),
        in_specs=[SMEM, SMEM, SMEM, VMEM, VMEM],
        out_specs=VMEM,
        scratch_shapes=lists_of(rows),
        compiler_params=params(24),
        cost_estimate=cost(48 * BLOCK * BLOCK * D * 2, 9 << 20),
        name="local_tiles",
    )(rows, cols, count, tiles, blocks)


def hop_kernel(first, send, rows, cols, count, tiles, blocks, part, h_ref, out, acc, zeros, sem, *lists):
    nblocks = h_ref.shape[0]
    n = collect(rows, cols, count, first, first + blocks.shape[0], nblocks, lists)
    acc[...] = part[...]
    add_tiles(n, lists, tiles, blocks, acc)
    h_ref[...] = acc[:nblocks].astype(BF16)
    send_blocks(send, h_ref, zeros, out, sem)


def hop(send, rows, cols, count, tiles, blocks, part, first):
    nblocks = part.shape[0] - 1
    return pl.pallas_call(
        functools.partial(hop_kernel, first),
        out_shape=(
            jax.ShapeDtypeStruct((nblocks, BLOCK, D), BF16),
            jax.ShapeDtypeStruct(blocks.shape, BF16),
        ),
        in_specs=[SMEM] * 4 + [VMEM] * 3,
        out_specs=(VMEM, ANY),
        scratch_shapes=[
            pltpu.VMEM(part.shape, F32),
            pltpu.VMEM((BLOCK, D), BF16),
            pltpu.SemaphoreType.DMA,
        ] + lists_of(rows),
        compiler_params=params(32),
        name="halo_tiles_send",
    )(send, rows, cols, count, tiles, blocks, part)


def attention_kernel(total, x, qw, vw, kv, key_mean, query_sq, hop_zero, hop_one, out):
    width = float(D)
    scale = total * width / query_sq[...]
    for c in range(x.shape[0] // CHUNK):
        rows = pl.ds(c * CHUNK, CHUNK)
        part = x[rows, :]
        query = jnp.dot(part, qw[...], preferred_element_type=F32)
        values = jnp.dot(part, vw[...], preferred_element_type=F32)
        feat = query * query * scale
        numer = jnp.dot(feat, kv[...], precision=HIGHEST, preferred_element_type=F32) + width * values
        denom = jnp.sum(feat * key_mean[...], 1, keepdims=True) + width
        graph = hop_zero[rows, :].astype(F32) + hop_one[rows, :].astype(F32)
        out[rows, :] = numer / denom + graph / 3.0


def attention(total, x, qw, vw, kv, key_mean, query_sq, hop_zero, hop_one):
    rows = x.shape[0]
    return pl.pallas_call(
        functools.partial(attention_kernel, total),
        out_shape=jax.ShapeDtypeStruct((rows, D), F32),
        in_specs=[VMEM] * 8,
        out_specs=VMEM,
        compiler_params=params(24),
        cost_estimate=cost(rows * D * D * 18, 6 << 20),
        name="attention",
    )(x, qw, vw, kv, key_mean, query_sq, hop_zero, hop_one)


def finish_kernel(first, rows, cols, count, tiles, blocks, part, base, gain, out, acc, *lists):
    nblocks = part.shape[0] - 1
    n = collect(rows, cols, count, first, first + blocks.shape[0], nblocks, lists)
    acc[...] = part[...]
    add_tiles(n, lists, tiles, blocks, acc)
    for b in range(nblocks):
        mixed = base[b] + acc[b].astype(BF16).astype(F32) / 3.0
        center = mixed - jnp.mean(mixed, 1, keepdims=True)
        scale = lax.rsqrt(jnp.mean(center * center, 1, keepdims=True) + 1e-05)
        out[b] = (gain[...] * center * scale).astype(BF16)


def finish(rows, cols, count, tiles, blocks, part, base, gain, first):
    nblocks = part.shape[0] - 1
    return pl.pallas_call(
        functools.partial(finish_kernel, first),
        out_shape=jax.ShapeDtypeStruct((nblocks, BLOCK, D), BF16),
        in_specs=[SMEM] * 3 + [VMEM] * 5,
        out_specs=VMEM,
        scratch_shapes=[pltpu.VMEM(part.shape, F32)] + lists_of(rows),
        compiler_params=params(32),
        name="halo_tiles_norm",
    )(rows, cols, count, tiles, blocks, part, base, gain)


def shards(x, qw, kw, vw, gw, gain, tiles, tile_rows, tile_cols, tile_count, send_list):
    rows_dev = x.shape[0]
    nblocks = rows_dev // BLOCK
    peers, groups = lax.axis_size("wide"), lax.axis_size("narrow")
    total = float(rows_dev * peers * groups)
    first = groups * nblocks

    hop_zero, outgoing = start(send_list, x, gw, peers)
    received = lax.all_to_all(outgoing, "wide", 0, 0, tiled=True)
    group = lax.all_gather(hop_zero, "narrow", axis=0, tiled=True)
    parts = stats(x, qw, kw, vw, peers)
    part = local_tiles(tile_rows, tile_cols, tile_count, tiles, group, nblocks)
    hop_one, outgoing = hop(
        send_list, tile_rows, tile_cols, tile_count, tiles, received, part, first
    )
    received = lax.all_to_all(outgoing, "wide", 0, 0, tiled=True)
    group = lax.all_gather(hop_one, "narrow", axis=0, tiled=True)
    part = local_tiles(tile_rows, tile_cols, tile_count, tiles, group, nblocks)
    sums = all_sums(parts)
    width = float(D)
    kv_mean = sums[:, :D // peers, :].reshape(D, D) * width
    key_mean = sums[0, 4:5, :] * width
    query_sq = sums[0, 6:7, :]
    base = attention(
        total, x, qw, vw, kv_mean, key_mean, query_sq,
        hop_zero.reshape(rows_dev, D), hop_one.reshape(rows_dev, D),
    )
    out = finish(
        tile_rows, tile_cols, tile_count, tiles, received, part,
        base.reshape(nblocks, BLOCK, D), gain[None, :], first,
    )
    return out.reshape(rows_dev, D)


def solution(mesh):
    return jax.shard_map(
        shards,
        mesh=mesh,
        in_specs=(
            P(("wide", "narrow"), None),
            P(),
            P(),
            P(),
            P(),
            P(),
            P(("wide", "narrow"), None, None),
            P(("wide", "narrow"), None),
            P(("wide", "narrow"), None),
            P(("wide", "narrow")),
            P(("wide", "narrow"), None),
        ),
        out_specs=P(("wide", "narrow"), None),
        check_vma=False,
    )
```

time: 628 us -> 301 us (0.48); the launches traced: 618 us -> 301 us
  blocking collectives: 208 us -> 0 us
  matrix products: 58.3 us -> 0 us
  local copies, waits for them, and re-layouts: 85.2 us -> 27.6 us
  Pallas kernels: 0 us -> 40.1 us
  other arithmetic: 30.1 us -> 6.67 us
  waiting for transfers between devices: 187 us -> 171 us
  starting transfers between devices: 31.9 us -> 41 us
    psum x2 -> x0, blocking collectives: 208 us -> none  [the longest x1 133 us: shards(): lax.psum((jnp.sum(query * query), jnp.sum(keys * keys)), ('wide', 'narrow'))]
    psum x1 -> x0, waiting for transfers between devices: 91.1 us -> none  [shards(): lax.psum((jnp.dot(key_feat.T, values, precision=highest), jnp.sum(key_fea...]
    all_to_all x2 -> x4, waiting for transfers between devices: 41.2 us -> 126 us  [the longest x2 119 us: shards(): received = lax.all_to_all(outgoing, 'wide', 0, 0, tiled=True)]
    dot_general x10 -> x0, matrix products: 58.3 us -> none  [the longest x2 18.7 us: propagate(): jnp.einsum('tij,tjd->tid', tile_values, gathered, preferred_element_type=...]
    pallas_call x0 -> x7, Pallas kernels: none -> 40.1 us  [the longest x1 11.7 us: hop(): pl.pallas_call(functools.partial(hop_kernel, first), out_shape=(jax.Shape...]
    gather x4 -> x0, local copies, waits for them, and re-layouts: 26.7 us -> none  [the longest x2 18.8 us: propagate(): gathered = jnp.take(buffer, columns, axis=0)]
    dot_general x2 -> x0, local copies, waits for them, and re-layouts: 25.4 us -> none  [propagate(): jnp.einsum('tij,tjd->tid', tile_values, gathered, preferred_element_type=...]
    unnamed x18 -> x54, local copies, waits for them, and re-layouts: 1.42 us -> 25.7 us
  transfers between devices with their start and end apart: 5 -> 8, of which waited for: 3 -> 6; matrix products, arithmetic and copies ran while one was open for 14% -> 3% of each run, Pallas kernels for 0% -> 9%
where the time goes in v1:
time: 301 us
  waiting for transfers between devices  171 us (57%)
  starting transfers between devices  41 us (14%)
  Pallas kernels  40.1 us (13%)
  local copies, waits for them, and re-layouts  27.6 us (9%)
  between operations  14.3 us (5%)
  other arithmetic  6.67 us (2%)
    all_to_all x2, waiting for transfers between devices, shards(): received = lax.all_to_all(outgoing, 'wide', 0, 0, tiled=True)  119 us
    all_gather x1, waiting for transfers between devices, shards(): group = lax.all_gather(hop_one, 'narrow', axis=0, tiled=True)  41 us
    unnamed x54, local copies, waits for them, and re-layouts  25.7 us
    all_to_all x2, starting transfers between devices, shards(): received = lax.all_to_all(outgoing, 'wide', 0, 0, tiled=True)  17.5 us
    all_to_all x1, starting transfers between devices, all_sums(): received = lax.all_to_all(parts, 'wide', 0, 0, tiled=True)  13 us
    pallas_call x1, Pallas kernels, hop(): pl.pallas_call(functools.partial(hop_kernel, first), out_shape=(jax.Shape...  11.7 us
    pallas_call x1, Pallas kernels, start(): pl.pallas_call(start_kernel, out_shape=(jax.ShapeDtypeStruct((nblocks, BL...  7.55 us
    pallas_call x1, Pallas kernels, finish(): pl.pallas_call(functools.partial(finish_kernel, first), out_shape=jax.Sha...  7.38 us
  transfers between devices with their start and end apart: 8, of which 6 were waited for; matrix products, arithmetic and copies ran while one was open for 3% of the time, Pallas kernels for 9%

profile of v1, /device:TPU:1, one launch (start us, length us, event | category | flops | bytes accessed | tf_op | source)
XLA Modules:
  0.0 300.8 jit_solution(2190256463378888812)
XLA Ops:
  10.5 5.5 %attention_sums.1 = f32[64,8,256]{2,1,0:T(8,128)} custom-call(bf16[2048,256]{1,0:T(8,128)(2,1)S(1)} %copy-done.9, bf16[256,256]{1,0:T(8,128)(2,1)S(1)} %copy-done.21, bf16[256,256]{1,0:T(8,128)(2,1)S(1)} %copy-done.20, bf16[256,256]{1,0:T(8,128)(2,1)S(1)} %copy-done.23), custom_call_target="tpu_custom_call" | custom-call | flops 2415919104 | bytes 2097152 | tf_op jit(solution)/shard_map/attention_sums/pallas_call | solution.py:116
  15.9 13.0 %all-to-all-start.2 = ((f32[64,8,256]{2,1,0:T(8,128)}), f32[64,8,256]{2,1,0:T(8,128)S(1)}, u32[]{:S(2)}, u32[]{:S(2)}) async-start(f32[64,8,256]{2,1,0:T(8,128)} %attention_sums.1), calls=%async_computation.2 | async-start | bytes 1048576 | tf_op jit(solution)/shard_map/all_to_all | solution.py:136
  29.0 7.5 %project_send.1 = (bf16[16,128,256]{2,1,0:T(8,128)(2,1)S(1)}, bf16[64,128,256]{2,1,0:T(8,128)(2,1)S(1)}) custom-call(s32[1,64]{1,0:T(1,128)S(1)} %copy-done.18, bf16[2048,256]{1,0:T(8,128)(2,1)S(1)} %copy-done.9, bf16[256,256]{1,0:T(8,128)(2,1)S(1)} %copy-done.15), custom_call_target="tpu_custom_call" | custom-call | tf_op jit(solution)/shard_map/project_send/pallas_call | solution.py:62
  36.5 2.0 copy-done.5
  39.5 6.8 %all-to-all-done.2 = f32[64,8,256]{2,1,0:T(8,128)S(1)} async-done(((f32[64,8,256]{2,1,0:T(8,128)}), f32[64,8,256]{2,1,0:T(8,128)S(1)}, u32[]{:S(2)}, u32[]{:S(2)}) %all-to-all-start.2) | async-done | bytes 524320 | tf_op jit(solution)/shard_map/all_to_all | solution.py:136
  47.1 6.7 %all-to-all-start = ((bf16[64,128,256]{2,1,0:T(8,128)(2,1)}), bf16[64,128,256]{2,1,0:T(8,128)(2,1)}, u32[]{:S(2)}, u32[]{:S(2)}) async-start(bf16[64,128,256]{2,1,0:T(8,128)(2,1)} %copy-done.5), calls=%async_computation | async-start | bytes 8388608 | tf_op jit(solution)/shard_map/all_to_all | solution.py:291
  59.8 1.5 collective-permute-done
  61.5 2.9 collective-permute-start.1
  66.1 83.7 %all-to-all-done.blocks = bf16[64,128,256]{2,1,0:T(8,128)(2,1)} async-done(((bf16[64,128,256]{2,1,0:T(8,128)(2,1)}), bf16[64,128,256]{2,1,0:T(8,128)(2,1)}, u32[]{:S(2)}, u32[]{:S(2)}) %all-to-all-start) | async-done | bytes 4194336 | tf_op jit(solution)/shard_map/all_to_all | solution.py:291
  150.6 5.9 %all-to-all-start.3 = ((f32[64,8,256]{2,1,0:T(8,128)}), f32[64,8,256]{2,1,0:T(8,128)}, u32[]{:S(2)}, u32[]{:S(2)}) async-start(f32[64,8,256]{2,1,0:T(8,128)} %broadcast_in_dim.19), calls=%async_computation.3 | async-start | bytes 1048576 | tf_op jit(solution)/shard_map/all_to_all | solution.py:141
  157.2 2.2 copy-done.3
  159.4 2.5 local_tiles.2.part
  161.9 11.7 %halo_tiles_send.1 = (bf16[16,128,256]{2,1,0:T(8,128)(2,1)S(1)}, bf16[64,128,256]{2,1,0:T(8,128)(2,1)S(1)}) custom-call(s32[1,64]{1,0:T(1,128)S(1)} %copy-done.18, s32[1,96]{1,0:T(1,128)S(1)} %copy-done.16, s32[1,96]{1,0:T(1,128)S(1)} %copy-done.17, s32[1]{0:T(128)S(6)} %copy.25.count, bf16[96,128,128]{2,1,0:T(8,128)(2,1)S(1)} %copy-done, ...), custom_call_target="tpu_custom_call" | custom-call | tf_op jit(solution)/shard_map/halo_tiles_send/pallas_call | solution.py:212
  173.7 2.0 copy-done.6
  176.7 10.8 %all-to-all-start.1 = ((bf16[64,128,256]{2,1,0:T(8,128)(2,1)}), bf16[64,128,256]{2,1,0:T(8,128)(2,1)}, u32[]{:S(2)}, u32[]{:S(2)}) async-start(bf16[64,128,256]{2,1,0:T(8,128)(2,1)} %copy-done.6), calls=%async_computation.1 | async-start | bytes 8388608 | tf_op jit(solution)/shard_map/all_to_all | solution.py:298
  188.2 1.8 slice_multiply_fusion.1
  196.4 3.0 attention.1
  200.7 41.0 %all-gather.5.cloned.1.call-done.blocks = bf16[64,128,256]{2,1,0:T(8,128)(2,1)} async-done(((bf16[16,128,256]{2,1,0:T(8,128)(2,1)}), bf16[64,128,256]{2,1,0:T(8,128)(2,1)}) %all-gather.5.cloned.1.call-update) | async-done | bytes 4194320 | tf_op jit(solution)/shard_map/all_gather | solution.py:299
  241.8 2.2 copy-done.4
  244.0 2.5 local_tiles.3.part
  247.9 35.4 %all-to-all-done.1.blocks = bf16[64,128,256]{2,1,0:T(8,128)(2,1)} async-done(((bf16[64,128,256]{2,1,0:T(8,128)(2,1)}), bf16[64,128,256]{2,1,0:T(8,128)(2,1)}, u32[]{:S(2)}, u32[]{:S(2)}) %all-to-all-start.1) | async-done | bytes 4194336 | tf_op jit(solution)/shard_map/all_to_all | solution.py:298
  283.4 1.6 copy-done.2
  285.0 1.6 copy-done.8
  286.6 7.4 %halo_tiles_norm.1 = bf16[16,128,256]{2,1,0:T(8,128)(2,1)} custom-call(s32[1,96]{1,0:T(1,128)S(1)} %copy-done.16, s32[1,96]{1,0:T(1,128)S(1)} %copy-done.17, s32[1]{0:T(128)S(6)} %copy.25.count, bf16[96,128,128]{2,1,0:T(8,128)(2,1)S(1)} %copy-done, bf16[64,128,256]{2,1,0:T(8,128)(2,1)} %all-to-all-done.1.blocks, f32[17,128,256]{2,1,0:T(8,128)S(1)} %copy-done.2, ...), custom_call_target="tpu_custom_call" | custom-call | tf_op jit(solution)/shard_map/halo_tiles_norm/pallas_call | solution.py:272
  (79 shorter events, 25.2 us)
Async XLA Ops:
  10.5 18.5 %copy-start.15 = (bf16[256,256]{1,0:T(8,128)(2,1)S(1)}, bf16[256,256]{1,0:T(8,128)(2,1)}, u32[]{:S(2)}) copy-start(bf16[256,256]{1,0:T(8,128)(2,1)} %weight.1) | copy-start | bytes 393220
  10.5 18.5 %copy-start.18 = (s32[1,64]{1,0:T(1,128)S(1)}, s32[1,64]{1,0:T(1,128)}, u32[]{:S(2)}) copy-start(s32[1,64]{1,0:T(1,128)} %send.3) | copy-start | bytes 772
  15.9 30.3 %all-to-all-start.2 = ((f32[64,8,256]{2,1,0:T(8,128)}), f32[64,8,256]{2,1,0:T(8,128)S(1)}, u32[]{:S(2)}, u32[]{:S(2)}) async-start(f32[64,8,256]{2,1,0:T(8,128)} %attention_sums.1), calls=%async_computation.2 | async-start | bytes 1048576 | tf_op jit(solution)/shard_map/all_to_all | solution.py:136
  36.5 2.0 copy-start.5
  47.1 110.1 %copy-start = (bf16[96,128,128]{2,1,0:T(8,128)(2,1)S(1)}, bf16[96,128,128]{2,1,0:T(8,128)(2,1)}, u32[]{:S(2)}) copy-start(bf16[96,128,128]{2,1,0:T(8,128)(2,1)} %tiles.7) | copy-start | bytes 9437188
  47.1 110.1 %copy-start.16 = (s32[1,96]{1,0:T(1,128)S(1)}, s32[1,96]{1,0:T(1,128)}, u32[]{:S(2)}) copy-start(s32[1,96]{1,0:T(1,128)} %rows.7) | copy-start | bytes 1156
  47.1 110.1 %copy-start.17 = (s32[1,96]{1,0:T(1,128)S(1)}, s32[1,96]{1,0:T(1,128)}, u32[]{:S(2)}) copy-start(s32[1,96]{1,0:T(1,128)} %cols.7) | copy-start | bytes 1156
  47.1 102.6 %all-to-all-start = ((bf16[64,128,256]{2,1,0:T(8,128)(2,1)}), bf16[64,128,256]{2,1,0:T(8,128)(2,1)}, u32[]{:S(2)}, u32[]{:S(2)}) async-start(bf16[64,128,256]{2,1,0:T(8,128)(2,1)} %copy-done.5), calls=%async_computation | async-start | bytes 8388608 | tf_op jit(solution)/shard_map/all_to_all | solution.py:291
  53.9 103.3 %all-gather.3.cloned.1.call-start = ((), (), s32[]{:S(2)}) async-start(), calls=%async_computation.4 | async-start | bytes 5242880 | tf_op jit(solution)/shard_map/all_gather | solution.py:292
  58.4 2.9 collective-permute-start
  61.5 4.4 %collective-permute-start.1 = (f32[8,256]{1,0:T(8,128)S(1)}, f32[8,256]{1,0:T(8,128)S(1)}, u32[]{:S(2)}, u32[]{:S(2)}) collective-permute-start(f32[8,256]{1,0:T(8,128)S(1)} %maximum_maximum_fusion.1), channel_id=1, source_target_pairs={{0,2},{1,3},{2,0},{3,1},{4,6},{5,7},{6,4},{7,5},{8,10},{9,11},{10,... | collective-permute-start | bytes 24584 | tf_op jit(solution)/shard_map/ppermute | solution.py:139
  150.6 26.1 %all-to-all-start.3 = ((f32[64,8,256]{2,1,0:T(8,128)}), f32[64,8,256]{2,1,0:T(8,128)}, u32[]{:S(2)}, u32[]{:S(2)}) async-start(f32[64,8,256]{2,1,0:T(8,128)} %broadcast_in_dim.19), calls=%async_computation.3 | async-start | bytes 1048576 | tf_op jit(solution)/shard_map/all_to_all | solution.py:141
  157.2 2.2 copy-start.3
  173.7 2.0 copy-start.6
  176.7 15.2 %copy-start.22 = (bf16[256,256]{1,0:T(8,128)(2,1)S(1)}, bf16[256,256]{1,0:T(8,128)(2,1)}, u32[]{:S(2)}) copy-start(bf16[256,256]{1,0:T(8,128)(2,1)} %qw.3) | copy-start | bytes 393220
  176.7 106.7 %all-to-all-start.1 = ((bf16[64,128,256]{2,1,0:T(8,128)(2,1)}), bf16[64,128,256]{2,1,0:T(8,128)(2,1)}, u32[]{:S(2)}, u32[]{:S(2)}) async-start(bf16[64,128,256]{2,1,0:T(8,128)(2,1)} %copy-done.6), calls=%async_computation.1 | async-start | bytes 8388608 | tf_op jit(solution)/shard_map/all_to_all | solution.py:298
  187.5 54.3 %all-gather.5.cloned.1.call-start = ((), (), s32[]{:S(2)}) async-start(), calls=%async_computation.5 | async-start | bytes 5242880 | tf_op jit(solution)/shard_map/all_gather | solution.py:299
  191.8 1.2 copy-start.10
  199.4 1.3 copy-start.7
  241.8 2.2 copy-start.4
  244.0 39.4 %copy-start.19 = (f32[256]{0:T(256)S(1)}, f32[256]{0:T(256)}, u32[]{:S(2)}) copy-start(f32[256]{0:T(256)} %param.16) | copy-start | bytes 3076
  246.5 1.4 copy-start.1
  283.4 1.6 copy-start.2
  285.0 1.6 copy-start.8
  (10 other events, 10.1 us)
Sparse Core Ops, SparseCore 0:
  56.5 51.9 all-gather.2
  190.1 51.6 all-gather.4

commit v2 on v1

v2 whole, which is shorter than its diff:
```python
import functools

import jax
import jax.numpy as jnp
from jax import lax
from jax.experimental import pallas as pl
from jax.experimental.pallas import tpu as pltpu
from jax.sharding import PartitionSpec as P

D = 256
BLOCK = 128
UNROLL = 8
CHUNK = 256
EXTRA = 8
CORE = ("wide", 0)
HALVE = (("wide", 4), ("wide", 5), ("narrow", 0), ("narrow", 1))
DEPTH = 8
F32 = jnp.float32
BF16 = jnp.bfloat16
HIGHEST = lax.Precision.HIGHEST
SMEM = pl.BlockSpec(memory_space=pltpu.SMEM)
VMEM = pl.BlockSpec(memory_space=pltpu.VMEM)
HBM = pl.BlockSpec(memory_space=pltpu.HBM)


def in_hbm(x):
    return pltpu.with_memory_space_constraint(x, pltpu.HBM)


def params(mib):
    return pltpu.CompilerParams(vmem_limit_bytes=mib << 20)


def cost(flops, nbytes):
    return pl.CostEstimate(flops=flops, bytes_accessed=nbytes, transcendentals=0)


def send_blocks(send, src, zeros, h_out, out, sems):
    own = pltpu.make_async_copy(src, h_out, sems.at[0])
    own.start()
    zeros[...] = jnp.zeros_like(zeros)

    def one(w, _):
        index = send[0, w]

        @pl.when(index >= 0)
        def _():
            pltpu.make_async_copy(src.at[jnp.maximum(index, 0)], out.at[w], sems.at[1]).start()

        @pl.when(index < 0)
        def _():
            pltpu.make_async_copy(zeros, out.at[w], sems.at[1]).start()

        return 0

    lax.fori_loop(0, out.shape[0], one, 0, unroll=8)
    own.wait()
    pltpu.make_async_copy(out, out, sems.at[1]).wait()


def start_kernel(send, x, weight, h_out, out, h_own, zeros, sems):
    def one(b, _):
        rows = pl.ds(pl.multiple_of(b * BLOCK, BLOCK), BLOCK)
        h_own[b] = jnp.dot(x[rows, :], weight[...], preferred_element_type=F32).astype(BF16)
        return 0

    lax.fori_loop(0, h_own.shape[0], one, 0, unroll=4)
    send_blocks(send, h_own, zeros, h_out, out, sems)


def start(send, x, weight, peers):
    nblocks = x.shape[0] // BLOCK
    return pl.pallas_call(
        start_kernel,
        out_shape=(pltpu.HBM((nblocks, BLOCK, D), BF16), pltpu.HBM((peers, BLOCK, D), BF16)),
        in_specs=[SMEM, VMEM, VMEM],
        out_specs=(HBM, HBM),
        scratch_shapes=[
            pltpu.VMEM((nblocks, BLOCK, D), BF16),
            pltpu.VMEM((BLOCK, D), BF16),
            pltpu.SemaphoreType.DMA((2,)),
        ],
        compiler_params=params(16),
        name="project_send",
    )(send, x, weight)


def stats_kernel(x, qw, kw, vw, after, out, keys_sq, values, sums):
    steps = x.shape[0] // CHUNK

    def project(c, carry):
        ksum, qsum = carry
        rows = pl.ds(pl.multiple_of(c * CHUNK, CHUNK), CHUNK)
        part = x[rows, :]
        query = jnp.dot(part, qw[...], preferred_element_type=F32)
        keys = jnp.dot(part, kw[...], preferred_element_type=F32)
        values[rows, :] = jnp.dot(part, vw[...], preferred_element_type=F32)
        keys_sq[rows, :] = keys * keys
        ksum = ksum + jnp.sum(keys * keys, 0, keepdims=True)
        return ksum, qsum + jnp.sum(query * query, 0, keepdims=True)

    zero = jnp.zeros((1, D), F32)
    ksum, qsum = lax.fori_loop(0, steps, project, (zero, zero))
    ktotal = jnp.sum(ksum, 1, keepdims=True)
    qtotal = jnp.sum(qsum, 1, keepdims=True)
    divisor = jnp.where(ktotal > 0, ktotal, 1.0)
    sums[...] = jnp.zeros_like(sums)

    def one(c, _):
        rows = pl.ds(pl.multiple_of(c * CHUNK, CHUNK), CHUNK)
        feat = keys_sq[rows, :] / divisor
        sums[...] += lax.dot_general(
            feat, values[rows, :], (((0,), (0,)), ((), ())),
            precision=HIGHEST, preferred_element_type=F32,
        )
        return 0

    lax.fori_loop(0, steps, one, 0)
    row = lax.broadcasted_iota(jnp.int32, (EXTRA, D), 0)
    extra = jnp.where(row == 0, ksum / divisor, jnp.where(row == 1, ktotal, qtotal))
    out[0:D, :] = sums[...]
    out[D:, :] = extra


def bit_of(step):
    axis, bit = step
    return lax.axis_index(axis) >> bit & 1


def split(rows, extra, bit, keep, away):
    half = rows.shape[0] // 2
    keep[0:half, :] = rows[pl.ds(pl.multiple_of(bit * half, 8), half), :]
    away[0:half, :] = rows[pl.ds(pl.multiple_of((1 - bit) * half, 8), half), :]
    keep[half:half + EXTRA, :] = extra
    away[half:half + EXTRA, :] = extra


def stats(x, qw, kw, vw, after):
    rows = x.shape[0]
    return pl.pallas_call(
        stats_kernel,
        out_shape=jax.ShapeDtypeStruct((D + EXTRA, D), F32),
        in_specs=[VMEM] * 4 + [HBM],
        out_specs=VMEM,
        scratch_shapes=[pltpu.VMEM((rows, D), F32)] * 2 + [pltpu.VMEM((D, D), F32)],
        compiler_params=params(16),
        cost_estimate=cost(rows * D * D * 18, 2 << 20),
        name="attention_sums",
    )(x, qw, kw, vw, after)


def merged(parts):
    rows = parts[0].shape[0] - EXTRA
    extras = [p[rows:, :] for p in parts]
    added = functools.reduce(jnp.add, extras)
    total = added[1:2, :]
    weights = [e[1:2, :] / jnp.where(total > 0, total, 1.0) for e in extras]
    row = lax.broadcasted_iota(jnp.int32, (EXTRA, D), 0)
    extra = jnp.where(row == 0, functools.reduce(jnp.add, [e * w for e, w in zip(extras, weights)]), added)
    return functools.reduce(jnp.add, [p[0:rows, :] * w for p, w in zip(parts, weights)]), extra


def halve_kernel(step, mine, other, keep, away, scratch):
    sums, extra = merged((mine, other))
    scratch[...] = sums
    split(scratch, extra, bit_of(step), keep, away)


def halve(mine, other, step):
    rows = mine.shape[0] - EXTRA
    return pl.pallas_call(
        functools.partial(halve_kernel, step),
        out_shape=(jax.ShapeDtypeStruct((rows // 2 + EXTRA, D), F32),) * 2,
        in_specs=[VMEM, VMEM],
        out_specs=(VMEM, VMEM),
        scratch_shapes=[pltpu.VMEM((rows, D), F32)],
        name="halve_sums",
    )(mine, other)


def merge_kernel(core, *refs):
    out = refs[-1]
    parts = [ref[...] for ref in refs[:-1]]
    if core:
        parts[0] = jnp.where(bit_of(CORE) == 0, parts[0], 0.0)
    sums, extra = merged(parts)
    rows = sums.shape[0]
    out[0:rows, :] = sums
    out[rows:, :] = extra


def merge(*parts, core=False):
    return pl.pallas_call(
        functools.partial(merge_kernel, core),
        out_shape=jax.ShapeDtypeStruct(parts[0].shape, F32),
        in_specs=[VMEM] * len(parts),
        out_specs=VMEM,
        name="merge_sums",
    )(*parts)


def join_kernel(step, mine, other, out):
    rows = mine.shape[0]
    at = bit_of(step)
    out[pl.ds(pl.multiple_of(at * rows, 8), rows), :] = mine[...]
    out[pl.ds(pl.multiple_of((1 - at) * rows, 8), rows), :] = other[...]


def join(mine, other, step):
    return pl.pallas_call(
        functools.partial(join_kernel, step),
        out_shape=jax.ShapeDtypeStruct((2 * mine.shape[0], D), F32),
        in_specs=[VMEM, VMEM],
        out_specs=VMEM,
        name="join_sums",
    )(mine, other)


def swap(x, step):
    axis, bit = step
    return lax.ppermute(x, axis, [(i, i ^ 1 << bit) for i in range(lax.axis_size(axis))])


def partial_sums(mine):
    keep, away = halve(mine, swap(mine, CORE), HALVE[0])
    for done, step in zip(HALVE, HALVE[1:]):
        keep, away = halve(keep, swap(away, done), step)
    return merge(keep, swap(away, HALVE[-1]))


def along_depth(mine):
    span, reach = 2 * DEPTH, DEPTH // 2

    def shift(by):
        return [
            (i, i // span * span + (i + 2 * (by + reach * (i % 2))) % span)
            for i in range(lax.axis_size("wide"))
            if by + reach * (i % 2) < DEPTH
        ]

    return [lax.ppermute(mine, "wide", shift(by)) for by in range(1, reach + 1)]


def whole_sums(mine, others):
    mine = merge(mine, *others, core=True)
    mine = merge(mine, swap(mine, CORE))
    rows, extra = mine[:-EXTRA], mine[-EXTRA:]
    for step in HALVE[::-1]:
        rows = join(rows, swap(rows, step), step)
    return rows, extra


def collect(rows, cols, count, first, last, spare, lists):
    slots, places, targets = lists

    def one(t, n):
        c = cols[0, t]
        slots[n] = t
        places[n] = c - first
        targets[n] = rows[0, t]
        return n + ((c >= first) & (c < last)).astype(jnp.int32)

    n = lax.fori_loop(0, count[0], one, jnp.int32(0))
    for u in range(UNROLL):
        slots[n + u] = 0
        places[n + u] = 0
        targets[n + u] = spare
    return n


def add_tiles(n, lists, tiles, blocks, acc):
    slots, places, targets = lists

    def step(i, _):
        prods = [
            jnp.dot(tiles[slots[i * UNROLL + u]], blocks[places[i * UNROLL + u]], preferred_element_type=F32)
            for u in range(UNROLL)
        ]
        for u in range(UNROLL):
            r = targets[i * UNROLL + u]
            acc[r] = acc[r] + prods[u]
        return 0

    lax.fori_loop(0, (n + UNROLL - 1) // UNROLL, step, 0)


def local_kernel(rows, cols, count, tiles, blocks, after, acc, *lists):
    n = collect(rows, cols, count, 0, blocks.shape[0], acc.shape[0] - 1, lists)
    acc[...] = jnp.zeros_like(acc)
    add_tiles(n, lists, tiles, blocks, acc)


def lists_of(rows):
    return [pltpu.SMEM((rows.shape[1] + UNROLL,), jnp.int32)] * 3


def local_tiles(rows, cols, count, tiles, blocks, after, nblocks):
    return pl.pallas_call(
        local_kernel,
        out_shape=pltpu.HBM((nblocks + 1, BLOCK, D), F32),
        in_specs=[SMEM, SMEM, SMEM, VMEM, VMEM, HBM],
        out_specs=VMEM,
        scratch_shapes=lists_of(rows),
        compiler_params=params(16),
        cost_estimate=cost(48 * BLOCK * BLOCK * D * 2, 9 << 20),
        name="local_tiles",
    )(rows, cols, count, tiles, blocks, after)


def hop_kernel(first, send, rows, cols, count, tiles, blocks, part, *refs):
    h_out, out, got, acc, h_own, zeros, sems, *lists = refs[DEPTH // 2:]
    loads = [pltpu.make_async_copy(blocks, got, sems.at[2]), pltpu.make_async_copy(part, acc, sems.at[3])]
    for load in loads:
        load.start()
    n = collect(rows, cols, count, first, first + blocks.shape[0], h_own.shape[0], lists)
    for load in loads:
        load.wait()
    add_tiles(n, lists, tiles, got, acc)
    h_own[...] = acc[:h_own.shape[0]].astype(BF16)
    send_blocks(send, h_own, zeros, h_out, out, sems)


def hop(send, rows, cols, count, tiles, blocks, part, after, first):
    nblocks = part.shape[0] - 1
    return pl.pallas_call(
        functools.partial(hop_kernel, first),
        out_shape=(pltpu.HBM((nblocks, BLOCK, D), BF16), pltpu.HBM(blocks.shape, BF16)),
        in_specs=[SMEM] * 4 + [VMEM, HBM, HBM] + [HBM] * len(after),
        out_specs=(HBM, HBM),
        scratch_shapes=[
            pltpu.VMEM(blocks.shape, BF16),
            pltpu.VMEM(part.shape, F32),
            pltpu.VMEM((nblocks, BLOCK, D), BF16),
            pltpu.VMEM((BLOCK, D), BF16),
            pltpu.SemaphoreType.DMA((4,)),
        ] + lists_of(rows),
        compiler_params=params(24),
        name="halo_tiles_send",
    )(send, rows, cols, count, tiles, in_hbm(blocks), in_hbm(part), *after)


def attention_kernel(total, x, qw, vw, kv_sums, extra, hop_zero, hop_one, out, kv):
    width = float(D)
    kv[...] = kv_sums[...] * width
    key_mean = extra[0:1, :] * width
    scale = total * width / extra[2:3, :]

    def one(c, _):
        rows = pl.ds(pl.multiple_of(c * CHUNK, CHUNK), CHUNK)
        part = x[rows, :]
        query = jnp.dot(part, qw[...], preferred_element_type=F32)
        values = jnp.dot(part, vw[...], preferred_element_type=F32)
        feat = query * query * scale
        numer = jnp.dot(feat, kv[...], precision=HIGHEST, preferred_element_type=F32) + width * values
        denom = jnp.sum(feat * key_mean, 1, keepdims=True) + width
        graph = hop_zero[rows, :].astype(F32) + hop_one[rows, :].astype(F32)
        out[rows, :] = numer / denom + graph / 3.0
        return 0

    lax.fori_loop(0, x.shape[0] // CHUNK, one, 0)


def attention(total, x, qw, vw, kv_sums, extra, hop_zero, hop_one):
    rows = x.shape[0]
    return pl.pallas_call(
        functools.partial(attention_kernel, total),
        out_shape=pltpu.HBM((rows, D), F32),
        in_specs=[VMEM] * 7,
        out_specs=VMEM,
        scratch_shapes=[pltpu.VMEM((D, D), F32)],
        compiler_params=params(16),
        cost_estimate=cost(rows * D * D * 18, 6 << 20),
        name="attention",
    )(x, qw, vw, kv_sums, extra, hop_zero, hop_one)


def finish_kernel(first, rows, cols, count, tiles, blocks, part, base, gain, out, got, acc, mixing, done, sems, *lists):
    nblocks = part.shape[0] - 1
    loads = [
        pltpu.make_async_copy(blocks, got, sems.at[0]),
        pltpu.make_async_copy(part, acc, sems.at[1]),
        pltpu.make_async_copy(base, mixing, sems.at[2]),
    ]
    for load in loads:
        load.start()
    n = collect(rows, cols, count, first, first + blocks.shape[0], nblocks, lists)
    loads[0].wait()
    loads[1].wait()
    add_tiles(n, lists, tiles, got, acc)
    loads[2].wait()

    def one(b, _):
        mixed = mixing[b] + acc[b].astype(BF16).astype(F32) / 3.0
        center = mixed - jnp.mean(mixed, 1, keepdims=True)
        scale = lax.rsqrt(jnp.mean(center * center, 1, keepdims=True) + 1e-05)
        done[b] = (gain[...] * center * scale).astype(BF16)
        pltpu.make_async_copy(done.at[b], out.at[b], sems.at[3]).start()
        return 0

    lax.fori_loop(0, nblocks, one, 0)
    pltpu.make_async_copy(done, out, sems.at[3]).wait()


def finish(rows, cols, count, tiles, blocks, part, base, gain, first):
    nblocks = part.shape[0] - 1
    return pl.pallas_call(
        functools.partial(finish_kernel, first),
        out_shape=jax.ShapeDtypeStruct((nblocks, BLOCK, D), BF16),
        in_specs=[SMEM] * 3 + [VMEM, HBM, HBM, HBM, VMEM],
        out_specs=HBM,
        scratch_shapes=[
            pltpu.VMEM(blocks.shape, BF16),
            pltpu.VMEM(part.shape, F32),
            pltpu.VMEM(base.shape, F32),
            pltpu.VMEM((nblocks, BLOCK, D), BF16),
            pltpu.SemaphoreType.DMA((4,)),
        ] + lists_of(rows),
        compiler_params=params(24),
        name="halo_tiles_norm",
    )(rows, cols, count, tiles, in_hbm(blocks), in_hbm(part), in_hbm(base), gain)


def shards(x, qw, kw, vw, gw, gain, tiles, tile_rows, tile_cols, tile_count, send_list):
    rows_dev = x.shape[0]
    nblocks = rows_dev // BLOCK
    peers, groups = lax.axis_size("wide"), lax.axis_size("narrow")
    total = float(rows_dev * peers * groups)
    first = groups * nblocks
    slots = (tile_rows, tile_cols, tile_count, tiles)

    hop_zero, outgoing = start(send_list, x, gw, peers)
    received = lax.all_to_all(outgoing, "wide", 0, 0, tiled=True)
    group = lax.all_gather(hop_zero, "narrow", axis=0, tiled=True)
    mine = partial_sums(stats(x, qw, kw, vw, hop_zero))
    others = along_depth(mine)
    part = local_tiles(*slots, group, mine, nblocks)
    hop_one, outgoing = hop(send_list, *slots, received, part, others, first)
    received = lax.all_to_all(outgoing, "wide", 0, 0, tiled=True)
    group = lax.all_gather(hop_one, "narrow", axis=0, tiled=True)
    kv_sums, extra = whole_sums(mine, others)
    base = attention(
        total, x, qw, vw, kv_sums, extra, hop_zero.reshape(rows_dev, D), hop_one.reshape(rows_dev, D)
    )
    part = local_tiles(*slots, group, base, nblocks)
    out = finish(*slots, received, part, base.reshape(nblocks, BLOCK, D), gain[None, :], first)
    return out.reshape(rows_dev, D)


def solution(mesh):
    return jax.shard_map(
        shards,
        mesh=mesh,
        in_specs=(
            P(("wide", "narrow"), None),
            P(),
            P(),
            P(),
            P(),
            P(),
            P(("wide", "narrow"), None, None),
            P(("wide", "narrow"), None),
            P(("wide", "narrow"), None),
            P(("wide", "narrow")),
            P(("wide", "narrow"), None),
        ),
        out_specs=P(("wide", "narrow"), None),
        check_vma=False,
    )
```

time: 301 us -> 251 us (0.83)
  waiting for transfers between devices: 171 us -> 105 us
  Pallas kernels: 40.1 us -> 53.4 us
  starting transfers between devices: 41 us -> 50.4 us
  other arithmetic: 6.67 us -> 0 us
    all_to_all x2, waiting for transfers between devices: 119 us -> 35.4 us  [shards(): received = lax.all_to_all(outgoing, 'wide', 0, 0, tiled=True)]
    ppermute x2 -> x14, waiting for transfers between devices: 2.94 us -> 60.5 us  [the longest x4 31.2 us: along_depth(): return [lax.ppermute(mine, 'wide', shift(by)) for by in range(1, reach + 1)]]
    all_gather x1, waiting for transfers between devices: 41 us -> 7.8 us  [shards(): group = lax.all_gather(hop_one, 'narrow', axis=0, tiled=True)]
    ppermute x2 -> x14, starting transfers between devices: 4.27 us -> 28.2 us  [the longest x10 17.4 us: swap(): lax.ppermute(x, axis, [(i, i ^ 1 << bit) for i in range(lax.axis_size(axi...]
    all_to_all x2 -> x0, starting transfers between devices: 18.9 us -> none  [the longest x1 13 us: all_sums(): received = lax.all_to_all(parts, 'wide', 0, 0, tiled=True)]
    pallas_call x6 -> x17, Pallas kernels: 32.7 us -> 45.4 us  [the longest x1 6.83 us: hop(): pl.pallas_call(functools.partial(hop_kernel, first), out_shape=(pltpu.HBM...]
    all_to_all x2 -> x0, waiting for transfers between devices: 6.78 us -> none  [the longest x1 6.78 us: all_sums(): received = lax.all_to_all(parts, 'wide', 0, 0, tiled=True)]
    all_to_all x2, starting transfers between devices: 17.5 us -> 22.1 us  [shards(): received = lax.all_to_all(outgoing, 'wide', 0, 0, tiled=True)]
  transfers between devices with their start and end apart: 8 -> 18, of which waited for: 6 -> 16; matrix products, arithmetic and copies ran while one was open for 3% -> 1% of each run, Pallas kernels for 9% -> 14%
where the time goes in v2:
time: 251 us; the launch traced here: 249 us
  waiting for transfers between devices  105 us (42%)
  Pallas kernels  53.4 us (21%)
  starting transfers between devices  50.4 us (20%)
  local copies, waits for them, and re-layouts  25.4 us (10%)
  between operations  14.3 us (6%)
    all_to_all x2, waiting for transfers between devices, shards(): received = lax.all_to_all(outgoing, 'wide', 0, 0, tiled=True)  35.4 us
    ppermute x4, waiting for transfers between devices, along_depth(): return [lax.ppermute(mine, 'wide', shift(by)) for by in range(1, reach + 1)]  31.2 us
    ppermute x10, waiting for transfers between devices, swap(): lax.ppermute(x, axis, [(i, i ^ 1 << bit) for i in range(lax.axis_size(axi...  29.3 us
    unnamed x76, local copies, waits for them, and re-layouts  24 us
    all_to_all x2, starting transfers between devices, shards(): received = lax.all_to_all(outgoing, 'wide', 0, 0, tiled=True)  22.1 us
    ppermute x10, starting transfers between devices, swap(): lax.ppermute(x, axis, [(i, i ^ 1 << bit) for i in range(lax.axis_size(axi...  17.4 us
    ppermute x4, starting transfers between devices, along_depth(): return [lax.ppermute(mine, 'wide', shift(by)) for by in range(1, reach + 1)]  10.8 us
    pallas_call x1, Pallas kernels, finish(): pl.pallas_call(functools.partial(finish_kernel, first), out_shape=jax.Sha...  8.05 us
  transfers between devices with their start and end apart: 18, of which 16 were waited for; matrix products, arithmetic and copies ran while one was open for 1% of the time, Pallas kernels for 14%

profile of v2, /device:TPU:1, one launch (start us, length us, event | category | flops | bytes accessed | tf_op | source)
XLA Modules:
  0.0 248.7 jit_solution(10714687655864407776)
XLA Ops:
  9.3 3.8 %project_send.1 = (bf16[16,128,256]{2,1,0:T(8,128)(2,1)}, bf16[64,128,256]{2,1,0:T(8,128)(2,1)}) custom-call(s32[1,64]{1,0:T(1,128)S(1)} %copy-done.20, bf16[2048,256]{1,0:T(8,128)(2,1)S(1)} %copy-done.4, bf16[256,256]{1,0:T(8,128)(2,1)S(1)} %copy-done.13), custom_call_target="tpu_custom_call" | custom-call | tf_op jit(solution)/shard_map/project_send/pallas_call | solution.py:73
  13.1 13.3 %all-to-all-start = ((bf16[64,128,256]{2,1,0:T(8,128)(2,1)}), bf16[64,128,256]{2,1,0:T(8,128)(2,1)}, u32[]{:S(2)}, u32[]{:S(2)}) async-start(bf16[64,128,256]{2,1,0:T(8,128)(2,1)} %get-tuple-element.17), calls=%async_computation | async-start | bytes 8388608 | tf_op jit(solution)/shard_map/all_to_all | solution.py:432
  31.4 5.8 %attention_sums.1.mine = f32[264,256]{1,0:T(8,128)S(1)} custom-call(bf16[2048,256]{1,0:T(8,128)(2,1)S(1)} %copy-done.5, bf16[256,256]{1,0:T(8,128)(2,1)S(1)} %copy-done.24, bf16[256,256]{1,0:T(8,128)(2,1)S(1)} %copy-done.23, bf16[256,256]{1,0:T(8,128)(2,1)S(1)} %copy-done.26, bf16[16,128,256]{2,1,0:T(8,128)(2,1)S(1)} %copy-done.7), custom_call_target="tpu_custom_call" | custom-call | flops 2415919104 | bytes 2097152 | tf_op jit(solution)/shard_map/attention_sums/pallas_call | solution.py:140
  42.2 6.4 %collective-permute-done.1.other = f32[136,256]{1,0:T(8,128)S(1)} collective-permute-done((f32[136,256]{1,0:T(8,128)}, f32[136,256]{1,0:T(8,128)S(1)}, u32[]{:S(2)}, u32[]{:S(2)}) %collective-permute-start.1) | collective-permute-done | bytes 139296 | tf_op jit(solution)/shard_map/ppermute | solution.py:221
  51.0 3.1 %collective-permute-start.2 = (f32[72,256]{1,0:T(8,128)}, f32[72,256]{1,0:T(8,128)S(1)}, u32[]{:S(2)}, u32[]{:S(2)}) collective-permute-start(f32[72,256]{1,0:T(8,128)} %get-tuple-element.22), channel_id=1, source_target_pairs={{0,128},{4,132},{8,136},{12,140},{16,144},{20,148},{24,152},{28,15... | collective-permute-start | bytes 221192 | tf_op jit(solution)/shard_map/ppermute | solution.py:221
  54.1 2.5 %collective-permute-done.2.other = f32[72,256]{1,0:T(8,128)S(1)} collective-permute-done((f32[72,256]{1,0:T(8,128)}, f32[72,256]{1,0:T(8,128)S(1)}, u32[]{:S(2)}, u32[]{:S(2)}) %collective-permute-start.2) | collective-permute-done | bytes 73760 | tf_op jit(solution)/shard_map/ppermute | solution.py:221
  60.1 3.0 %collective-permute-done.3.other = f32[40,256]{1,0:T(8,128)S(1)} collective-permute-done((f32[40,256]{1,0:T(8,128)}, f32[40,256]{1,0:T(8,128)S(1)}, u32[]{:S(2)}, u32[]{:S(2)}) %collective-permute-start.3) | collective-permute-done | bytes 40992 | tf_op jit(solution)/shard_map/ppermute | solution.py:221
  65.2 2.9 %collective-permute-start.4 = (f32[24,256]{1,0:T(8,128)}, f32[24,256]{1,0:T(8,128)S(1)}, u32[]{:S(2)}, u32[]{:S(2)}) collective-permute-start(f32[24,256]{1,0:T(8,128)} %get-tuple-element.26), channel_id=1, source_target_pairs={{0,2},{1,3},{2,0},{3,1},{4,6},{5,7},{6,4},{7,5},{8,10},{9,11},{10,... | collective-permute-start | bytes 73736 | tf_op jit(solution)/shard_map/ppermute | solution.py:221
  72.5 2.6 %collective-permute-start.5 = (f32[24,256]{1,0:T(8,128)}, f32[24,256]{1,0:T(8,128)S(1)}, u32[]{:S(2)}, u32[]{:S(2)}) collective-permute-start(f32[24,256]{1,0:T(8,128)} %merge_sums.3.after.refs_0_), channel_id=1, source_target_pairs={{0,8},{4,44},{8,16},{12,52},{16,24},{20,60},{24,32},{28,4},{32,40}... | collective-permute-start | bytes 73736 | tf_op jit(solution)/shard_map/ppermute | solution.py:241
  75.1 3.2 %collective-permute-start.6 = (f32[24,256]{1,0:T(8,128)}, f32[24,256]{1,0:T(8,128)S(1)}, u32[]{:S(2)}, u32[]{:S(2)}) collective-permute-start(f32[24,256]{1,0:T(8,128)} %merge_sums.3.after.refs_0_), channel_id=1, source_target_pairs={{0,16},{4,52},{8,24},{12,60},{16,32},{20,4},{24,40},{28,12},{32,48... | collective-permute-start | bytes 73736 | tf_op jit(solution)/shard_map/ppermute | solution.py:241
  78.3 4.4 %collective-permute-start.7 = (f32[24,256]{1,0:T(8,128)}, f32[24,256]{1,0:T(8,128)S(1)}, u32[]{:S(2)}, u32[]{:S(2)}) collective-permute-start(f32[24,256]{1,0:T(8,128)} %merge_sums.3.after.refs_0_), channel_id=1, source_target_pairs={{0,24},{4,60},{8,32},{12,4},{16,40},{20,12},{24,48},{28,20},{32,56... | collective-permute-start | bytes 73736 | tf_op jit(solution)/shard_map/ppermute | solution.py:241
  86.3 3.3 %local_tiles.2.part = f32[17,128,256]{2,1,0:T(8,128)} custom-call(s32[1,96]{1,0:T(1,128)S(1)} %copy-done.18, s32[1,96]{1,0:T(1,128)S(1)} %copy-done.19, s32[1]{0:T(128)S(6)} %copy.12.count, bf16[96,128,128]{2,1,0:T(8,128)(2,1)S(1)} %copy-done, bf16[64,128,256]{2,1,0:T(8,128)(2,1)S(1)} %copy-done.2, f32[24,256]{1,0:T(8,128)S(1)} %copy-done.12), custom_call_target="tpu_custom_call" | custom-call | flops 402653184 | bytes 9437184 | tf_op jit(solution)/shard_map/local_tiles/pallas_call | solution.py:298
  89.6 28.2 %collective-permute-done.5.refs_0_.refs_1_ = f32[24,256]{1,0:T(8,128)S(1)} collective-permute-done((f32[24,256]{1,0:T(8,128)}, f32[24,256]{1,0:T(8,128)S(1)}, u32[]{:S(2)}, u32[]{:S(2)}) %collective-permute-start.5) | collective-permute-done | bytes 24608 | tf_op jit(solution)/shard_map/ppermute | solution.py:241
  117.8 2.4 collective-permute-done.6.refs_1_.refs_2_
  122.3 6.8 %halo_tiles_send.1 = (bf16[16,128,256]{2,1,0:T(8,128)(2,1)}, bf16[64,128,256]{2,1,0:T(8,128)(2,1)}) custom-call(s32[1,64]{1,0:T(1,128)S(1)} %copy-done.21, s32[1,96]{1,0:T(1,128)S(1)} %copy-done.18, s32[1,96]{1,0:T(1,128)S(1)} %copy-done.19, s32[1]{0:T(128)S(6)} %copy.12.count, bf16[96,128,128]{2,1,0:T(8,128)(2,1)S(1)} %copy-done, ...), custom_call_target="tpu_custom_call" | custom-call | tf_op jit(solution)/shard_map/halo_tiles_send/pallas_call | solution.py:325
  129.2 8.8 %all-to-all-start.1 = ((bf16[64,128,256]{2,1,0:T(8,128)(2,1)}), bf16[64,128,256]{2,1,0:T(8,128)(2,1)}, u32[]{:S(2)}, u32[]{:S(2)}) async-start(bf16[64,128,256]{2,1,0:T(8,128)(2,1)} %get-tuple-element.27), calls=%async_computation.1 | async-start | bytes 8388608 | tf_op jit(solution)/shard_map/all_to_all | solution.py:438
  144.4 3.1 %collective-permute-start.10 = (f32[16,256]{1,0:T(8,128)S(1)}, f32[16,256]{1,0:T(8,128)S(1)}, u32[]{:S(2)}, u32[]{:S(2)}) collective-permute-start(f32[16,256]{1,0:T(8,128)S(1)} %slice.8.mine), channel_id=1, source_target_pairs={{0,2},{1,3},{2,0},{3,1},{4,6},{5,7},{6,4},{7,5},{8,10},{9,11},{10,... | collective-permute-start | bytes 49160 | tf_op jit(solution)/shard_map/ppermute | solution.py:221
  158.8 4.0 %collective-permute-done.12.other = f32[64,256]{1,0:T(8,128)S(1)} collective-permute-done((f32[64,256]{1,0:T(8,128)}, f32[64,256]{1,0:T(8,128)S(1)}, u32[]{:S(2)}, u32[]{:S(2)}) %collective-permute-start.12) | collective-permute-done | bytes 65568 | tf_op jit(solution)/shard_map/ppermute | solution.py:221
  166.5 5.6 %collective-permute-done.13.other = f32[128,256]{1,0:T(8,128)S(1)} collective-permute-done((f32[128,256]{1,0:T(8,128)}, f32[128,256]{1,0:T(8,128)S(1)}, u32[]{:S(2)}, u32[]{:S(2)}) %collective-permute-start.13) | collective-permute-done | bytes 131104 | tf_op jit(solution)/shard_map/ppermute | solution.py:221
  179.2 5.8 %attention.1.after = f32[2048,256]{1,0:T(8,128)} custom-call(bf16[2048,256]{1,0:T(8,128)(2,1)S(1)} %copy-done.6, bf16[256,256]{1,0:T(8,128)(2,1)S(1)} %copy-done.25, bf16[256,256]{1,0:T(8,128)(2,1)S(1)} %copy-done.27, f32[256,256]{1,0:T(8,128)S(1)} %copy-done.11, f32[8,256]{1,0:T(8,128)S(1)} %slice.9.extra, bf16[2048,256]{1,0:T(8,128)(2,1)S(1)} %bitcast.6, ...), custom_call_target="tpu_custom_call" | custom-call | flops 2415919104 | bytes 6291456 | tf_op jit(solution)/shard_map/attention/pallas_call | solution.py:365
  185.0 7.8 %all-gather.5.cloned.1.call-done.blocks = bf16[64,128,256]{2,1,0:T(8,128)(2,1)} async-done(((bf16[16,128,256]{2,1,0:T(8,128)(2,1)}), bf16[64,128,256]{2,1,0:T(8,128)(2,1)}) %all-gather.5.cloned.1.call-update) | async-done | bytes 4194320 | tf_op jit(solution)/shard_map/all_gather | solution.py:439
  196.6 3.3 %local_tiles.3.part = f32[17,128,256]{2,1,0:T(8,128)} custom-call(s32[1,96]{1,0:T(1,128)S(1)} %copy-done.18, s32[1,96]{1,0:T(1,128)S(1)} %copy-done.19, s32[1]{0:T(128)S(6)} %copy.12.count, bf16[96,128,128]{2,1,0:T(8,128)(2,1)S(1)} %copy-done, bf16[64,128,256]{2,1,0:T(8,128)(2,1)S(1)} %copy-done.3, f32[2048,256]{1,0:T(8,128)S(1)} %copy-done.1), custom_call_target="tpu_custom_call" | custom-call | flops 402653184 | bytes 9437184 | tf_op jit(solution)/shard_map/local_tiles/pallas_call | solution.py:298
  199.8 34.0 %all-to-all-done.1.blocks = bf16[64,128,256]{2,1,0:T(8,128)(2,1)} async-done(((bf16[64,128,256]{2,1,0:T(8,128)(2,1)}), bf16[64,128,256]{2,1,0:T(8,128)(2,1)}, u32[]{:S(2)}, u32[]{:S(2)}) %all-to-all-start.1) | async-done | bytes 4194336 | tf_op jit(solution)/shard_map/all_to_all | solution.py:438
  233.8 8.1 %halo_tiles_norm.1 = bf16[16,128,256]{2,1,0:T(8,128)(2,1)} custom-call(s32[1,96]{1,0:T(1,128)S(1)} %copy-done.18, s32[1,96]{1,0:T(1,128)S(1)} %copy-done.19, s32[1]{0:T(128)S(6)} %copy.12.count, bf16[96,128,128]{2,1,0:T(8,128)(2,1)S(1)} %copy-done, bf16[64,128,256]{2,1,0:T(8,128)(2,1)} %all-to-all-done.1.blocks, f32[17,128,256]{2,1,0:T(8,128)} %local_tiles.3.part, ...), custom_call_target="tpu_custom_call" | custom-call | tf_op jit(solution)/shard_map/halo_tiles_norm/pallas_call | solution.py:406
  (110 shorter events, 62.3 us)
Async XLA Ops:
  13.1 109.1 %all-to-all-start = ((bf16[64,128,256]{2,1,0:T(8,128)(2,1)}), bf16[64,128,256]{2,1,0:T(8,128)(2,1)}, u32[]{:S(2)}, u32[]{:S(2)}) async-start(bf16[64,128,256]{2,1,0:T(8,128)(2,1)} %get-tuple-element.17), calls=%async_computation | async-start | bytes 8388608 | tf_op jit(solution)/shard_map/all_to_all | solution.py:432
  26.4 56.9 %all-gather.3.cloned.1.call-start = ((), (), s32[]{:S(2)}) async-start(), calls=%async_computation.2 | async-start | bytes 5242880 | tf_op jit(solution)/shard_map/all_gather | solution.py:433
  31.4 51.9 %copy-start = (bf16[96,128,128]{2,1,0:T(8,128)(2,1)S(1)}, bf16[96,128,128]{2,1,0:T(8,128)(2,1)}, u32[]{:S(2)}) copy-start(bf16[96,128,128]{2,1,0:T(8,128)(2,1)} %tiles.7) | copy-start | bytes 9437188
  31.4 51.9 %copy-start.18 = (s32[1,96]{1,0:T(1,128)S(1)}, s32[1,96]{1,0:T(1,128)}, u32[]{:S(2)}) copy-start(s32[1,96]{1,0:T(1,128)} %rows.7) | copy-start | bytes 1156
  31.4 51.9 %copy-start.19 = (s32[1,96]{1,0:T(1,128)S(1)}, s32[1,96]{1,0:T(1,128)}, u32[]{:S(2)}) copy-start(s32[1,96]{1,0:T(1,128)} %cols.7) | copy-start | bytes 1156
  37.3 1.9 collective-permute-start
  41.0 7.6 %collective-permute-start.1 = (f32[136,256]{1,0:T(8,128)}, f32[136,256]{1,0:T(8,128)S(1)}, u32[]{:S(2)}, u32[]{:S(2)}) collective-permute-start(f32[136,256]{1,0:T(8,128)} %get-tuple-element.20), channel_id=1, source_target_pairs={{0,64},{4,68},{8,72},{12,76},{16,80},{20,84},{24,88},{28,92},{32,9... | collective-permute-start | bytes 417800 | tf_op jit(solution)/shard_map/ppermute | solution.py:221
  51.0 5.6 %collective-permute-start.2 = (f32[72,256]{1,0:T(8,128)}, f32[72,256]{1,0:T(8,128)S(1)}, u32[]{:S(2)}, u32[]{:S(2)}) collective-permute-start(f32[72,256]{1,0:T(8,128)} %get-tuple-element.22), channel_id=1, source_target_pairs={{0,128},{4,132},{8,136},{12,140},{16,144},{20,148},{24,152},{28,15... | collective-permute-start | bytes 221192 | tf_op jit(solution)/shard_map/ppermute | solution.py:221
  58.8 4.3 %collective-permute-start.3 = (f32[40,256]{1,0:T(8,128)}, f32[40,256]{1,0:T(8,128)S(1)}, u32[]{:S(2)}, u32[]{:S(2)}) collective-permute-start(f32[40,256]{1,0:T(8,128)} %get-tuple-element.24), channel_id=1, source_target_pairs={{0,1},{1,0},{2,3},{3,2},{4,5},{5,4},{6,7},{7,6},{8,9},{9,8},{10,11... | collective-permute-start | bytes 122888 | tf_op jit(solution)/shard_map/ppermute | solution.py:221
  65.2 5.3 %collective-permute-start.4 = (f32[24,256]{1,0:T(8,128)}, f32[24,256]{1,0:T(8,128)S(1)}, u32[]{:S(2)}, u32[]{:S(2)}) collective-permute-start(f32[24,256]{1,0:T(8,128)} %get-tuple-element.26), channel_id=1, source_target_pairs={{0,2},{1,3},{2,0},{3,1},{4,6},{5,7},{6,4},{7,5},{8,10},{9,11},{10,... | collective-permute-start | bytes 73736 | tf_op jit(solution)/shard_map/ppermute | solution.py:221
  71.1 51.1 %copy-start.21 = (s32[1,64]{1,0:T(1,128)S(1)}, s32[1,64]{1,0:T(1,128)}, u32[]{:S(2)}) copy-start(s32[1,64]{1,0:T(1,128)} %send.3) | copy-start | bytes 772
  72.5 45.3 %collective-permute-start.5 = (f32[24,256]{1,0:T(8,128)}, f32[24,256]{1,0:T(8,128)S(1)}, u32[]{:S(2)}, u32[]{:S(2)}) collective-permute-start(f32[24,256]{1,0:T(8,128)} %merge_sums.3.after.refs_0_), channel_id=1, source_target_pairs={{0,8},{4,44},{8,16},{12,52},{16,24},{20,60},{24,32},{28,4},{32,40}... | collective-permute-start | bytes 73736 | tf_op jit(solution)/shard_map/ppermute | solution.py:241
  75.1 45.1 %collective-permute-start.6 = (f32[24,256]{1,0:T(8,128)}, f32[24,256]{1,0:T(8,128)S(1)}, u32[]{:S(2)}, u32[]{:S(2)}) collective-permute-start(f32[24,256]{1,0:T(8,128)} %merge_sums.3.after.refs_0_), channel_id=1, source_target_pairs={{0,16},{4,52},{8,24},{12,60},{16,32},{20,4},{24,40},{28,12},{32,48... | collective-permute-start | bytes 73736 | tf_op jit(solution)/shard_map/ppermute | solution.py:241
  78.3 42.5 %collective-permute-start.7 = (f32[24,256]{1,0:T(8,128)}, f32[24,256]{1,0:T(8,128)S(1)}, u32[]{:S(2)}, u32[]{:S(2)}) collective-permute-start(f32[24,256]{1,0:T(8,128)} %merge_sums.3.after.refs_0_), channel_id=1, source_target_pairs={{0,24},{4,60},{8,32},{12,4},{16,40},{20,12},{24,48},{28,20},{32,56... | collective-permute-start | bytes 73736 | tf_op jit(solution)/shard_map/ppermute | solution.py:241
  82.7 38.1 %collective-permute-start.8 = (f32[24,256]{1,0:T(8,128)}, f32[24,256]{1,0:T(8,128)S(1)}, u32[]{:S(2)}, u32[]{:S(2)}) collective-permute-start(f32[24,256]{1,0:T(8,128)} %merge_sums.3.after.refs_0_), channel_id=1, source_target_pairs={{0,32},{8,40},{16,48},{24,56},{32,0},{40,8},{48,16},{56,24},{64,96... | collective-permute-start | bytes 73736 | tf_op jit(solution)/shard_map/ppermute | solution.py:241
  129.1 45.4 %copy-start.25 = (bf16[256,256]{1,0:T(8,128)(2,1)S(1)}, bf16[256,256]{1,0:T(8,128)(2,1)}, u32[]{:S(2)}) copy-start(bf16[256,256]{1,0:T(8,128)(2,1)} %qw.3) | copy-start | bytes 393220
  129.1 45.4 %copy-start.27 = (bf16[256,256]{1,0:T(8,128)(2,1)S(1)}, bf16[256,256]{1,0:T(8,128)(2,1)}, u32[]{:S(2)}) copy-start(bf16[256,256]{1,0:T(8,128)(2,1)} %vw.3) | copy-start | bytes 393220
  129.2 104.7 %all-to-all-start.1 = ((bf16[64,128,256]{2,1,0:T(8,128)(2,1)}), bf16[64,128,256]{2,1,0:T(8,128)(2,1)}, u32[]{:S(2)}, u32[]{:S(2)}) async-start(bf16[64,128,256]{2,1,0:T(8,128)(2,1)} %get-tuple-element.27), calls=%async_computation.1 | async-start | bytes 8388608 | tf_op jit(solution)/shard_map/all_to_all | solution.py:438
  137.9 54.8 %all-gather.5.cloned.1.call-start = ((), (), s32[]{:S(2)}) async-start(), calls=%async_computation.3 | async-start | bytes 5242880 | tf_op jit(solution)/shard_map/all_gather | solution.py:439
  140.1 1.6 collective-permute-start.9
  144.4 4.6 %collective-permute-start.10 = (f32[16,256]{1,0:T(8,128)S(1)}, f32[16,256]{1,0:T(8,128)S(1)}, u32[]{:S(2)}, u32[]{:S(2)}) collective-permute-start(f32[16,256]{1,0:T(8,128)S(1)} %slice.8.mine), channel_id=1, source_target_pairs={{0,2},{1,3},{2,0},{3,1},{4,6},{5,7},{6,4},{7,5},{8,10},{9,11},{10,... | collective-permute-start | bytes 49160 | tf_op jit(solution)/shard_map/ppermute | solution.py:221
  151.0 3.4 %collective-permute-start.11 = (f32[32,256]{1,0:T(8,128)}, f32[32,256]{1,0:T(8,128)S(1)}, u32[]{:S(2)}, u32[]{:S(2)}) collective-permute-start(f32[32,256]{1,0:T(8,128)} %join_sums.4.mine), channel_id=1, source_target_pairs={{0,1},{1,0},{2,3},{3,2},{4,5},{5,4},{6,7},{7,6},{8,9},{9,8},{10,11... | collective-permute-start | bytes 98312 | tf_op jit(solution)/shard_map/ppermute | solution.py:221
  156.4 6.4 %collective-permute-start.12 = (f32[64,256]{1,0:T(8,128)}, f32[64,256]{1,0:T(8,128)S(1)}, u32[]{:S(2)}, u32[]{:S(2)}) collective-permute-start(f32[64,256]{1,0:T(8,128)} %join_sums.5.mine), channel_id=1, source_target_pairs={{0,128},{4,132},{8,136},{12,140},{16,144},{20,148},{24,152},{28,15... | collective-permute-start | bytes 196616 | tf_op jit(solution)/shard_map/ppermute | solution.py:221
  164.9 7.2 %collective-permute-start.13 = (f32[128,256]{1,0:T(8,128)}, f32[128,256]{1,0:T(8,128)S(1)}, u32[]{:S(2)}, u32[]{:S(2)}) collective-permute-start(f32[128,256]{1,0:T(8,128)} %join_sums.6.mine), channel_id=1, source_target_pairs={{0,64},{4,68},{8,72},{12,76},{16,80},{20,84},{24,88},{28,92},{32,9... | collective-permute-start | bytes 393224 | tf_op jit(solution)/shard_map/ppermute | solution.py:221
  (32 other events, 118.7 us)
Sparse Core Ops, SparseCore 0:
  29.1 52.7 all-gather.2
  140.6 52.1 all-gather.4

commit v3 on v2

--- a/solution.py
+++ b/solution.py
@@ -11,10 +11,12 @@
 BLOCK = 128
 UNROLL = 8
 CHUNK = 256
+NORM = 4
 EXTRA = 8
 CORE = ("wide", 0)
 HALVE = (("wide", 4), ("wide", 5), ("narrow", 0), ("narrow", 1))
 DEPTH = 8
+JOIN = (("wide", 5), ("wide", 4), ("narrow", 1), ("narrow", 0))
 F32 = jnp.float32
 BF16 = jnp.bfloat16
 HIGHEST = lax.Precision.HIGHEST
@@ -35,54 +37,103 @@
     return pl.CostEstimate(flops=flops, bytes_accessed=nbytes, transcendentals=0)
 
 
-def send_blocks(send, src, zeros, h_out, out, sems):
-    own = pltpu.make_async_copy(src, h_out, sems.at[0])
-    own.start()
+def send_order(send, heads, nexts, zeros, out, sem):
     zeros[...] = jnp.zeros_like(zeros)
+
+    def clear(b, _):
+        heads[b] = -1
+        return 0
+
+    lax.fori_loop(0, heads.shape[0], clear, 0)
 
     def one(w, _):
         index = send[0, w]
+        block = jnp.maximum(index, 0)
 
         @pl.when(index >= 0)
         def _():
-            pltpu.make_async_copy(src.at[jnp.maximum(index, 0)], out.at[w], sems.at[1]).start()
+            nexts[w] = heads[block]
+            heads[block] = w
 
         @pl.when(index < 0)
         def _():
-            pltpu.make_async_copy(zeros, out.at[w], sems.at[1]).start()
-
-        return 0
-
-    lax.fori_loop(0, out.shape[0], one, 0, unroll=8)
-    own.wait()
+            pltpu.make_async_copy(zeros, out.at[w], sem).start()
+
+        return 0
+
+    lax.fori_loop(0, nexts.shape[0], one, 0)
+
+
+def send_block(b, src, heads, nexts, h_out, out, sems):
+    pltpu.make_async_copy(src.at[b], h_out.at[b], sems.at[0]).start()
+
+    def one(w):
+        pltpu.make_async_copy(src.at[b], out.at[w], sems.at[1]).start()
+        return nexts[w]
+
+    lax.while_loop(lambda w: w >= 0, one, heads[b])
+
+
+def wait_sent(src, h_out, out, sems):
+    pltpu.make_async_copy(src, h_out, sems.at[0]).wait()
     pltpu.make_async_copy(out, out, sems.at[1]).wait()
 
 
-def start_kernel(send, x, weight, h_out, out, h_own, zeros, sems):
-    def one(b, _):
-        rows = pl.ds(pl.multiple_of(b * BLOCK, BLOCK), BLOCK)
-        h_own[b] = jnp.dot(x[rows, :], weight[...], preferred_element_type=F32).astype(BF16)
-        return 0
-
-    lax.fori_loop(0, h_own.shape[0], one, 0, unroll=4)
-    send_blocks(send, h_own, zeros, h_out, out, sems)
+def send_scratch(nblocks, peers):
+    return [
+        pltpu.VMEM((nblocks, BLOCK, D), BF16),
+        pltpu.VMEM((BLOCK, D), BF16),
+        pltpu.SMEM((nblocks,), jnp.int32),
+        pltpu.SMEM((peers,), jnp.int32),
+        pltpu.SemaphoreType.DMA((2,)),
+    ]
+
+
+def start_kernel(send, x, weight, h_out, out, h_own, zeros, heads, nexts, sems, send_own, x_own, weight_own, loads):
+    pieces = loads.shape[0] - 2
+    rows = x.shape[0] // pieces
+    per = rows // BLOCK
+    sends = pltpu.make_async_copy(send, send_own, loads.at[0])
+    weights = pltpu.make_async_copy(weight, weight_own, loads.at[1])
+    sends.start()
+    weights.start()
+    parts = [
+        pltpu.make_async_copy(x.at[pl.ds(p * rows, rows)], x_own.at[pl.ds(p * rows, rows)], loads.at[2 + p])
+        for p in range(pieces)
+    ]
+    for part in parts:
+        part.start()
+    sends.wait()
+    send_order(send_own, heads, nexts, zeros, out, sems.at[1])
+    weights.wait()
+    for p in range(pieces):
+        parts[p].wait()
+        for b in range(p * per, (p + 1) * per):
+            h_own[b] = jnp.dot(
+                x_own[b * BLOCK:(b + 1) * BLOCK, :], weight_own[...], preferred_element_type=F32
+            ).astype(BF16)
+        for b in range(p * per, (p + 1) * per):
+            send_block(b, h_own, heads, nexts, h_out, out, sems)
+    wait_sent(h_own, h_out, out, sems)
 
 
 def start(send, x, weight, peers):
     nblocks = x.shape[0] // BLOCK
+    pieces = 4
     return pl.pallas_call(
         start_kernel,
         out_shape=(pltpu.HBM((nblocks, BLOCK, D), BF16), pltpu.HBM((peers, BLOCK, D), BF16)),
-        in_specs=[SMEM, VMEM, VMEM],
+        in_specs=[HBM] * 3,
         out_specs=(HBM, HBM),
-        scratch_shapes=[
-            pltpu.VMEM((nblocks, BLOCK, D), BF16),
-            pltpu.VMEM((BLOCK, D), BF16),
-            pltpu.SemaphoreType.DMA((2,)),
+        scratch_shapes=send_scratch(nblocks, peers) + [
+            pltpu.SMEM(send.shape, jnp.int32),
+            pltpu.VMEM(x.shape, BF16),
+            pltpu.VMEM(weight.shape, BF16),
+            pltpu.SemaphoreType.DMA((pieces + 2,)),
         ],
         compiler_params=params(16),
         name="project_send",
-    )(send, x, weight)
+    )(in_hbm(send), in_hbm(x), in_hbm(weight))
 
 
 def stats_kernel(x, qw, kw, vw, after, out, keys_sq, values, sums):
@@ -245,7 +296,7 @@
     mine = merge(mine, *others, core=True)
     mine = merge(mine, swap(mine, CORE))
     rows, extra = mine[:-EXTRA], mine[-EXTRA:]
-    for step in HALVE[::-1]:
+    for step in JOIN:
         rows = join(rows, swap(rows, step), step)
     return rows, extra
 
@@ -284,9 +335,58 @@
     lax.fori_loop(0, (n + UNROLL - 1) // UNROLL, step, 0)
 
 
-def local_kernel(rows, cols, count, tiles, blocks, after, acc, *lists):
-    n = collect(rows, cols, count, 0, blocks.shape[0], acc.shape[0] - 1, lists)
+def load_halo(n, places, blocks, got, sems):
+    def one(i, _):
+        for u in range(UNROLL):
+            j = i * UNROLL + u
+            pltpu.make_async_copy(blocks.at[places[j]], got.at[j], sems.at[i]).start()
+        return 0
+
+    lax.fori_loop(0, (n + UNROLL - 1) // UNROLL, one, 0)
+
+
+def add_halo(n, lists, tiles, got, acc, sems):
+    slots, places, targets = lists
+
+    def step(i, _):
+        at = pl.ds(i * UNROLL, UNROLL)
+        pltpu.make_async_copy(got.at[at], got.at[at], sems.at[i]).wait()
+        prods = [
+            jnp.dot(tiles[slots[i * UNROLL + u]], got[i * UNROLL + u], preferred_element_type=F32)
+            for u in range(UNROLL)
+        ]
+        for u in range(UNROLL):
+            r = targets[i * UNROLL + u]
+            acc[r] = acc[r] + prods[u]
+        return 0
+
+    lax.fori_loop(0, (n + UNROLL - 1) // UNROLL, step, 0)
+
+
+def halo_scratch(rows, part):
+    steps = -(-rows.shape[1] // UNROLL)
+    return [
+        pltpu.VMEM((steps * UNROLL, BLOCK, D), BF16),
+        pltpu.VMEM(part.shape, F32),
+        pltpu.VMEM(part.shape, F32),
+        pltpu.SemaphoreType.DMA((steps + 1,)),
+    ] + lists_of(rows)
+
+
+def local_kernel(rows, cols, count, tiles, *refs):
+    parts, after, acc, blocks, sems, lists = refs[:-7], refs[-7], refs[-6], refs[-5], refs[-4], refs[-3:]
+    groups, nblocks = len(parts), parts[0].shape[0]
+    me = lax.axis_index("narrow")
+    loads = []
+    for by, part in enumerate(parts):
+        owner = lax.rem(me + groups - by, groups)
+        place = blocks.at[pl.ds(owner * nblocks, nblocks)]
+        loads.append(pltpu.make_async_copy(part, place, sems.at[by]))
+        loads[-1].start()
+    n = collect(rows, cols, count, 0, blocks.shape[0], nblocks, lists)
     acc[...] = jnp.zeros_like(acc)
+    for load in loads:
+        load.wait()
     add_tiles(n, lists, tiles, blocks, acc)
 
 
@@ -294,30 +394,43 @@
     return [pltpu.SMEM((rows.shape[1] + UNROLL,), jnp.int32)] * 3
 
 
-def local_tiles(rows, cols, count, tiles, blocks, after, nblocks):
+def local_tiles(rows, cols, count, tiles, parts, after):
+    nblocks = parts[0].shape[0]
     return pl.pallas_call(
         local_kernel,
         out_shape=pltpu.HBM((nblocks + 1, BLOCK, D), F32),
-        in_specs=[SMEM, SMEM, SMEM, VMEM, VMEM, HBM],
+        in_specs=[SMEM, SMEM, SMEM, VMEM] + [HBM] * (len(parts) + 1),
         out_specs=VMEM,
-        scratch_shapes=lists_of(rows),
+        scratch_shapes=[
+            pltpu.VMEM((len(parts) * nblocks, BLOCK, D), BF16),
+            pltpu.SemaphoreType.DMA((len(parts),)),
+        ] + lists_of(rows),
         compiler_params=params(16),
         cost_estimate=cost(48 * BLOCK * BLOCK * D * 2, 9 << 20),
         name="local_tiles",
-    )(rows, cols, count, tiles, blocks, after)
+    )(rows, cols, count, tiles, *map(in_hbm, parts), after)
 
 
 def hop_kernel(first, send, rows, cols, count, tiles, blocks, part, *refs):
-    h_out, out, got, acc, h_own, zeros, sems, *lists = refs[DEPTH // 2:]
-    loads = [pltpu.make_async_copy(blocks, got, sems.at[2]), pltpu.make_async_copy(part, acc, sems.at[3])]
-    for load in loads:
-        load.start()
-    n = collect(rows, cols, count, first, first + blocks.shape[0], h_own.shape[0], lists)
-    for load in loads:
-        load.wait()
-    add_tiles(n, lists, tiles, got, acc)
-    h_own[...] = acc[:h_own.shape[0]].astype(BF16)
-    send_blocks(send, h_own, zeros, h_out, out, sems)
+    h_out, out, got, acc, local, loads, *rest = refs[DEPTH // 2:]
+    lists, (h_own, zeros, heads, nexts, sems) = rest[:3], rest[3:]
+    nblocks = h_own.shape[0]
+    n = collect(rows, cols, count, first, first + blocks.shape[0], nblocks, lists)
+    load_halo(n, lists[1], blocks, got, loads)
+    load = pltpu.make_async_copy(part, local, loads.at[loads.shape[0] - 1])
+    load.start()
+    send_order(send, heads, nexts, zeros, out, sems.at[1])
+    acc[...] = jnp.zeros_like(acc)
+    add_halo(n, lists, tiles, got, acc, loads)
+    load.wait()
+
+    def one(b, _):
+        h_own[b] = (acc[b] + local[b]).astype(BF16)
+        send_block(b, h_own, heads, nexts, h_out, out, sems)
+        return 0
+
+    lax.fori_loop(0, nblocks, one, 0)
+    wait_sent(h_own, h_out, out, sems)
 
 
 def hop(send, rows, cols, count, tiles, blocks, part, after, first):
@@ -327,21 +440,19 @@
         out_shape=(pltpu.HBM((nblocks, BLOCK, D), BF16), pltpu.HBM(blocks.shape, BF16)),
         in_specs=[SMEM] * 4 + [VMEM, HBM, HBM] + [HBM] * len(after),
         out_specs=(HBM, HBM),
-        scratch_shapes=[
-            pltpu.VMEM(blocks.shape, BF16),
-            pltpu.VMEM(part.shape, F32),
-            pltpu.VMEM((nblocks, BLOCK, D), BF16),
-            pltpu.VMEM((BLOCK, D), BF16),
-            pltpu.SemaphoreType.DMA((4,)),
-        ] + lists_of(rows),
-        compiler_params=params(24),
+        scratch_shapes=halo_scratch(rows, part) + send_scratch(nblocks, blocks.shape[0]),
+        compiler_params=params(20),
         name="halo_tiles_send",
     )(send, rows, cols, count, tiles, in_hbm(blocks), in_hbm(part), *after)
 
 
 def attention_kernel(total, x, qw, vw, kv_sums, extra, hop_zero, hop_one, out, kv):
     width = float(D)
-    kv[...] = kv_sums[...] * width
+    each = D >> len(HALVE)
+    for place in range(1 << len(HALVE)):
+        bits = {step: place >> at & 1 for at, step in enumerate(HALVE[::-1])}
+        came = sum(bits[step] << at for at, step in enumerate(JOIN))
+        kv[place * each:(place + 1) * each, :] = kv_sums[came * each:(came + 1) * each, :] * width
     key_mean = extra[0:1, :] * width
     scale = total * width / extra[2:3, :]
 
@@ -374,31 +485,35 @@
     )(x, qw, vw, kv_sums, extra, hop_zero, hop_one)
 
 
-def finish_kernel(first, rows, cols, count, tiles, blocks, part, base, gain, out, got, acc, mixing, done, sems, *lists):
+def finish_kernel(first, rows, cols, count, tiles, blocks, part, base, gain, out, got, acc, local, loads, *rest):
+    lists, (mixing, base_sem, done, sem) = rest[:3], rest[3:]
     nblocks = part.shape[0] - 1
-    loads = [
-        pltpu.make_async_copy(blocks, got, sems.at[0]),
-        pltpu.make_async_copy(part, acc, sems.at[1]),
-        pltpu.make_async_copy(base, mixing, sems.at[2]),
+    n = collect(rows, cols, count, first, first + blocks.shape[0], nblocks, lists)
+    load_halo(n, lists[1], blocks, got, loads)
+    late = [
+        pltpu.make_async_copy(part, local, loads.at[loads.shape[0] - 1]),
+        pltpu.make_async_copy(base, mixing, base_sem),
     ]
-    for load in loads:
+    for load in late:
         load.start()
-    n = collect(rows, cols, count, first, first + blocks.shape[0], nblocks, lists)
-    loads[0].wait()
-    loads[1].wait()
-    add_tiles(n, lists, tiles, got, acc)
-    loads[2].wait()
-
-    def one(b, _):
-        mixed = mixing[b] + acc[b].astype(BF16).astype(F32) / 3.0
-        center = mixed - jnp.mean(mixed, 1, keepdims=True)
-        scale = lax.rsqrt(jnp.mean(center * center, 1, keepdims=True) + 1e-05)
-        done[b] = (gain[...] * center * scale).astype(BF16)
-        pltpu.make_async_copy(done.at[b], out.at[b], sems.at[3]).start()
-        return 0
-
-    lax.fori_loop(0, nblocks, one, 0)
-    pltpu.make_async_copy(done, out, sems.at[3]).wait()
+    acc[...] = jnp.zeros_like(acc)
+    add_halo(n, lists, tiles, got, acc, loads)
+    for load in late:
+        load.wait()
+
+    def some(i, _):
+        for u in range(NORM):
+            b = i * NORM + u
+            mixed = mixing[b] + (acc[b] + local[b]).astype(BF16).astype(F32) / 3.0
+            center = mixed - jnp.mean(mixed, 1, keepdims=True)
+            scale = lax.rsqrt(jnp.mean(center * center, 1, keepdims=True) + 1e-05)
+            done[b] = (gain[...] * center * scale).astype(BF16)
+        at = pl.ds(i * NORM, NORM)
+        pltpu.make_async_copy(done.at[at], out.at[at], sem).start()
+        return 0
+
+    lax.fori_loop(0, nblocks // NORM, some, 0)
+    pltpu.make_async_copy(done, out, sem).wait()
 
 
 def finish(rows, cols, count, tiles, blocks, part, base, gain, first):
@@ -408,16 +523,21 @@
         out_shape=jax.ShapeDtypeStruct((nblocks, BLOCK, D), BF16),
         in_specs=[SMEM] * 3 + [VMEM, HBM, HBM, HBM, VMEM],
         out_specs=HBM,
-        scratch_shapes=[
-            pltpu.VMEM(blocks.shape, BF16),
-            pltpu.VMEM(part.shape, F32),
-            pltpu.VMEM(base.shape, F32),
-            pltpu.VMEM((nblocks, BLOCK, D), BF16),
-            pltpu.SemaphoreType.DMA((4,)),
-        ] + lists_of(rows),
-        compiler_params=params(24),
+        scratch_shapes=halo_scratch(rows, part) + [
+            pltpu.VMEM(base.shape, F32), pltpu.SemaphoreType.DMA,
+            pltpu.VMEM((nblocks, BLOCK, D), BF16), pltpu.SemaphoreType.DMA,
+        ],
+        compiler_params=params(20),
         name="halo_tiles_norm",
     )(rows, cols, count, tiles, in_hbm(blocks), in_hbm(part), in_hbm(base), gain)
+
+
+def group_blocks(own):
+    groups = lax.axis_size("narrow")
+    return [own] + [
+        lax.ppermute(own, "narrow", [(i, (i + by) % groups) for i in range(groups)])
+        for by in range(1, groups)
+    ]
 
 
 def shards(x, qw, kw, vw, gw, gain, tiles, tile_rows, tile_cols, tile_count, send_list):
@@ -430,18 +550,18 @@
 
     hop_zero, outgoing = start(send_list, x, gw, peers)
     received = lax.all_to_all(outgoing, "wide", 0, 0, tiled=True)
-    group = lax.all_gather(hop_zero, "narrow", axis=0, tiled=True)
+    group = group_blocks(hop_zero)
     mine = partial_sums(stats(x, qw, kw, vw, hop_zero))
     others = along_depth(mine)
-    part = local_tiles(*slots, group, mine, nblocks)
+    part = local_tiles(*slots, group, mine)
     hop_one, outgoing = hop(send_list, *slots, received, part, others, first)
     received = lax.all_to_all(outgoing, "wide", 0, 0, tiled=True)
-    group = lax.all_gather(hop_one, "narrow", axis=0, tiled=True)
+    group = group_blocks(hop_one)
     kv_sums, extra = whole_sums(mine, others)
     base = attention(
         total, x, qw, vw, kv_sums, extra, hop_zero.reshape(rows_dev, D), hop_one.reshape(rows_dev, D)
     )
-    part = local_tiles(*slots, group, base, nblocks)
+    part = local_tiles(*slots, group, base)
     out = finish(*slots, received, part, base.reshape(nblocks, BLOCK, D), gain[None, :], first)
     return out.reshape(rows_dev, D)
 

time: 251 us -> 232 us (0.924)
  between operations: 14.3 us -> 1.07 us
  local copies, waits for them, and re-layouts: 25.4 us -> 17.6 us
  starting transfers between devices: 50.4 us -> 55.2 us
    ppermute x10, waiting for transfers between devices: 29.3 us -> 58.3 us  [swap(): lax.ppermute(x, axis, [(i, i ^ 1 << bit) for i in range(lax.axis_size(axi...]
    all_to_all x2, waiting for transfers between devices: 35.4 us -> 21.4 us  [shards(): received = lax.all_to_all(outgoing, 'wide', 0, 0, tiled=True)]
    ppermute x0 -> x6, starting transfers between devices: none -> 10.4 us  [group_blocks(): lax.ppermute(own, 'narrow', [(i, (i + by) % groups) for i in range(groups)])]
    all_gather x2 -> x0, waiting for transfers between devices: 7.82 us -> none  [the longest x1 7.8 us: shards(): group = lax.all_gather(hop_one, 'narrow', axis=0, tiled=True)]
    unnamed x76 -> x64, local copies, waits for them, and re-layouts: 24 us -> 16.2 us
    ppermute x4, waiting for transfers between devices: 31.2 us -> 23.9 us  [along_depth(): return [lax.ppermute(mine, 'wide', shift(by)) for by in range(1, reach + 1)]]
    ppermute x4, starting transfers between devices: 10.8 us -> 6.83 us  [along_depth(): return [lax.ppermute(mine, 'wide', shift(by)) for by in range(1, reach + 1)]]
    pallas_call x1, Pallas kernels: 8.05 us -> 5.5 us  [finish(): pl.pallas_call(functools.partial(finish_kernel, first), out_shape=jax.Sha...]
  transfers between devices with their start and end apart: 18 -> 22, of which waited for: 16 -> 15; matrix products, arithmetic and copies ran while one was open for 1% -> 1% of each run, Pallas kernels for 14% -> 16%
where the time goes in v3:
time: 232 us; the launch traced here: 230 us
  waiting for transfers between devices  104 us (45%)
  starting transfers between devices  55.2 us (24%)
  Pallas kernels  52.1 us (22%)
  local copies, waits for them, and re-layouts  17.6 us (8%)
    ppermute x10, waiting for transfers between devices, swap(): lax.ppermute(x, axis, [(i, i ^ 1 << bit) for i in range(lax.axis_size(axi...  58.3 us
    ppermute x4, waiting for transfers between devices, along_depth(): return [lax.ppermute(mine, 'wide', shift(by)) for by in range(1, reach + 1)]  23.9 us
    all_to_all x2, starting transfers between devices, shards(): received = lax.all_to_all(outgoing, 'wide', 0, 0, tiled=True)  22.6 us
    all_to_all x2, waiting for transfers between devices, shards(): received = lax.all_to_all(outgoing, 'wide', 0, 0, tiled=True)  21.4 us
    unnamed x64, local copies, waits for them, and re-layouts  16.2 us
    ppermute x10, starting transfers between devices, swap(): lax.ppermute(x, axis, [(i, i ^ 1 << bit) for i in range(lax.axis_size(axi...  15.3 us
    ppermute x6, starting transfers between devices, group_blocks(): lax.ppermute(own, 'narrow', [(i, (i + by) % groups) for i in range(groups)])  10.4 us
    pallas_call x2, Pallas kernels, local_tiles(): pl.pallas_call(local_kernel, out_shape=pltpu.HBM((nblocks + 1, BLOCK, D),...  8.81 us
  transfers between devices with their start and end apart: 22, of which 15 were waited for; matrix products, arithmetic and copies ran while one was open for 1% of the time, Pallas kernels for 16%

profile of v3, /device:TPU:1, one launch (start us, length us, event | category | flops | bytes accessed | tf_op | source)
XLA Modules:
  0.0 229.6 jit_solution(4474762090230143643)
XLA Ops:
  0.0 4.0 %project_send.1 = (bf16[16,128,256]{2,1,0:T(8,128)(2,1)}, bf16[64,128,256]{2,1,0:T(8,128)(2,1)}) custom-call(s32[1,64]{1,0:T(1,128)} %send.3, bf16[2048,256]{1,0:T(8,128)(2,1)} %x.5, bf16[256,256]{1,0:T(8,128)(2,1)} %weight.1), custom_call_target="tpu_custom_call" | custom-call | tf_op jit(solution)/shard_map/project_send/pallas_call | solution.py:123
  4.0 13.4 %all-to-all-start = ((bf16[64,128,256]{2,1,0:T(8,128)(2,1)}), bf16[64,128,256]{2,1,0:T(8,128)(2,1)}, u32[]{:S(2)}, u32[]{:S(2)}) async-start(bf16[64,128,256]{2,1,0:T(8,128)(2,1)} %get-tuple-element.17), calls=%async_computation | async-start | bytes 8388608 | tf_op jit(solution)/shard_map/all_to_all | solution.py:552
  18.7 2.7 %collective-permute-start.1 = (bf16[16,128,256]{2,1,0:T(8,128)(2,1)}, bf16[16,128,256]{2,1,0:T(8,128)(2,1)}, u32[]{:S(2)}, u32[]{:S(2)}) collective-permute-start(bf16[16,128,256]{2,1,0:T(8,128)(2,1)} %get-tuple-element.18.after.refs_0_), channel_id=1, source_target_pairs={{0,2},{1,3},{2,0},{3,1},{4,6},{5,7},{6,4},{7,5},{8,10},{9,11},{10,... | collective-permute-start | bytes 3145736 | tf_op jit(solution)/shard_map/ppermute | solution.py:538
  26.9 5.8 %attention_sums.1.mine = f32[264,256]{1,0:T(8,128)S(1)} custom-call(bf16[2048,256]{1,0:T(8,128)(2,1)S(1)} %copy-done.5, bf16[256,256]{1,0:T(8,128)(2,1)S(1)} %copy-done.19, bf16[256,256]{1,0:T(8,128)(2,1)S(1)} %copy-done.18, bf16[256,256]{1,0:T(8,128)(2,1)S(1)} %copy-done.21, bf16[16,128,256]{2,1,0:T(8,128)(2,1)S(1)} %copy-done.2), custom_call_target="tpu_custom_call" | custom-call | flops 2415919104 | bytes 2097152 | tf_op jit(solution)/shard_map/attention_sums/pallas_call | solution.py:191
  38.5 6.7 %collective-permute-done.4.other = f32[136,256]{1,0:T(8,128)S(1)} collective-permute-done((f32[136,256]{1,0:T(8,128)}, f32[136,256]{1,0:T(8,128)S(1)}, u32[]{:S(2)}, u32[]{:S(2)}) %collective-permute-start.4) | collective-permute-done | bytes 139296 | tf_op jit(solution)/shard_map/ppermute | solution.py:272
  47.5 2.8 %collective-permute-start.5 = (f32[72,256]{1,0:T(8,128)}, f32[72,256]{1,0:T(8,128)S(1)}, u32[]{:S(2)}, u32[]{:S(2)}) collective-permute-start(f32[72,256]{1,0:T(8,128)} %get-tuple-element.22), channel_id=1, source_target_pairs={{0,128},{4,132},{8,136},{12,140},{16,144},{20,148},{24,152},{28,15... | collective-permute-start | bytes 221192 | tf_op jit(solution)/shard_map/ppermute | solution.py:272
  50.4 3.1 %collective-permute-done.5.other = f32[72,256]{1,0:T(8,128)S(1)} collective-permute-done((f32[72,256]{1,0:T(8,128)}, f32[72,256]{1,0:T(8,128)S(1)}, u32[]{:S(2)}, u32[]{:S(2)}) %collective-permute-start.5) | collective-permute-done | bytes 73760 | tf_op jit(solution)/shard_map/ppermute | solution.py:272
  56.1 11.1 %collective-permute-done.6.other = f32[40,256]{1,0:T(8,128)S(1)} collective-permute-done((f32[40,256]{1,0:T(8,128)}, f32[40,256]{1,0:T(8,128)S(1)}, u32[]{:S(2)}, u32[]{:S(2)}) %collective-permute-start.6) | collective-permute-done | bytes 40992 | tf_op jit(solution)/shard_map/ppermute | solution.py:272
  69.3 2.7 %collective-permute-start.7 = (f32[24,256]{1,0:T(8,128)}, f32[24,256]{1,0:T(8,128)S(1)}, u32[]{:S(2)}, u32[]{:S(2)}) collective-permute-start(f32[24,256]{1,0:T(8,128)} %get-tuple-element.26), channel_id=1, source_target_pairs={{0,2},{1,3},{2,0},{3,1},{4,6},{5,7},{6,4},{7,5},{8,10},{9,11},{10,... | collective-permute-start | bytes 73736 | tf_op jit(solution)/shard_map/ppermute | solution.py:272
  75.9 4.7 %collective-permute-start.8 = (f32[24,256]{1,0:T(8,128)}, f32[24,256]{1,0:T(8,128)S(1)}, u32[]{:S(2)}, u32[]{:S(2)}) collective-permute-start(f32[24,256]{1,0:T(8,128)} %merge_sums.3.refs_4_.refs_0_), channel_id=1, source_target_pairs={{0,8},{4,44},{8,16},{12,52},{16,24},{20,60},{24,32},{28,4},{32,40}... | collective-permute-start | bytes 73736 | tf_op jit(solution)/shard_map/ppermute | solution.py:292
  83.5 4.4 %local_tiles.2.part = f32[17,128,256]{2,1,0:T(8,128)} custom-call(s32[1,96]{1,0:T(1,128)S(1)} %copy-done.14, s32[1,96]{1,0:T(1,128)S(1)} %copy-done.15, s32[1]{0:T(128)S(6)} %copy.12.count, bf16[96,128,128]{2,1,0:T(8,128)(2,1)S(1)} %copy-done, bf16[16,128,256]{2,1,0:T(8,128)(2,1)} %get-tuple-element.18.after.refs_0_, ...), custom_call_target="tpu_custom_call" | custom-call | flops 402653184 | bytes 9437184 | tf_op jit(solution)/shard_map/local_tiles/pallas_call | solution.py:399
  88.0 20.9 %collective-permute-done.8.refs_0_.refs_1_ = f32[24,256]{1,0:T(8,128)S(1)} collective-permute-done((f32[24,256]{1,0:T(8,128)}, f32[24,256]{1,0:T(8,128)S(1)}, u32[]{:S(2)}, u32[]{:S(2)}) %collective-permute-start.8) | collective-permute-done | bytes 24608 | tf_op jit(solution)/shard_map/ppermute | solution.py:292
  108.8 2.4 %collective-permute-done.9.refs_1_.refs_2_ = f32[24,256]{1,0:T(8,128)S(1)} collective-permute-done((f32[24,256]{1,0:T(8,128)}, f32[24,256]{1,0:T(8,128)S(1)}, u32[]{:S(2)}, u32[]{:S(2)}) %collective-permute-start.9) | collective-permute-done | bytes 24608 | tf_op jit(solution)/shard_map/ppermute | solution.py:292
  113.3 5.5 %halo_tiles_send.1 = (bf16[16,128,256]{2,1,0:T(8,128)(2,1)}, bf16[64,128,256]{2,1,0:T(8,128)(2,1)}) custom-call(s32[1,64]{1,0:T(1,128)S(1)} %copy-done.16, s32[1,96]{1,0:T(1,128)S(1)} %copy-done.14, s32[1,96]{1,0:T(1,128)S(1)} %copy-done.15, s32[1]{0:T(128)S(6)} %copy.12.count, bf16[96,128,128]{2,1,0:T(8,128)(2,1)S(1)} %copy-done, ...), custom_call_target="tpu_custom_call" | custom-call | tf_op jit(solution)/shard_map/halo_tiles_send/pallas_call | solution.py:438
  118.8 9.2 %all-to-all-start.1 = ((bf16[64,128,256]{2,1,0:T(8,128)(2,1)}), bf16[64,128,256]{2,1,0:T(8,128)(2,1)}, u32[]{:S(2)}, u32[]{:S(2)}) async-start(bf16[64,128,256]{2,1,0:T(8,128)(2,1)} %get-tuple-element.27), calls=%async_computation.1 | async-start | bytes 8388608 | tf_op jit(solution)/shard_map/all_to_all | solution.py:558
  129.8 2.4 %collective-permute-start.13 = (bf16[16,128,256]{2,1,0:T(8,128)(2,1)}, bf16[16,128,256]{2,1,0:T(8,128)(2,1)}, u32[]{:S(2)}, u32[]{:S(2)}) collective-permute-start(bf16[16,128,256]{2,1,0:T(8,128)(2,1)} %get-tuple-element.28.refs_0_), channel_id=1, source_target_pairs={{0,2},{1,3},{2,0},{3,1},{4,6},{5,7},{6,4},{7,5},{8,10},{9,11},{10,... | collective-permute-start | bytes 3145736 | tf_op jit(solution)/shard_map/ppermute | solution.py:538
  139.9 2.8 %collective-permute-start.16 = (f32[16,256]{1,0:T(8,128)S(1)}, f32[16,256]{1,0:T(8,128)S(1)}, u32[]{:S(2)}, u32[]{:S(2)}) collective-permute-start(f32[16,256]{1,0:T(8,128)S(1)} %slice.8.mine), channel_id=1, source_target_pairs={{0,128},{4,132},{8,136},{12,140},{16,144},{20,148},{24,152},{28,15... | collective-permute-start | bytes 49160 | tf_op jit(solution)/shard_map/ppermute | solution.py:272
  147.8 2.9 %collective-permute-done.17.other = f32[32,256]{1,0:T(8,128)S(1)} collective-permute-done((f32[32,256]{1,0:T(8,128)}, f32[32,256]{1,0:T(8,128)S(1)}, u32[]{:S(2)}, u32[]{:S(2)}) %collective-permute-start.17) | collective-permute-done | bytes 32800 | tf_op jit(solution)/shard_map/ppermute | solution.py:272
  152.7 26.5 %collective-permute-done.18.other = f32[64,256]{1,0:T(8,128)S(1)} collective-permute-done((f32[64,256]{1,0:T(8,128)}, f32[64,256]{1,0:T(8,128)S(1)}, u32[]{:S(2)}, u32[]{:S(2)}) %collective-permute-start.18) | collective-permute-done | bytes 65568 | tf_op jit(solution)/shard_map/ppermute | solution.py:272
  183.5 2.3 collective-permute-done.19.other
  192.1 5.8 %attention.1.refs_4_ = f32[2048,256]{1,0:T(8,128)} custom-call(bf16[2048,256]{1,0:T(8,128)(2,1)S(1)} %copy-done.6, bf16[256,256]{1,0:T(8,128)(2,1)S(1)} %copy-done.20, bf16[256,256]{1,0:T(8,128)(2,1)S(1)} %copy-done.22, f32[256,256]{1,0:T(8,128)S(1)} %copy-done.8, f32[8,256]{1,0:T(8,128)S(1)} %slice.9.extra, bf16[2048,256]{1,0:T(8,128)(2,1)S(1)} %bitcast.6, ...), custom_call_target="tpu_custom_call" | custom-call | flops 2415919104 | bytes 6291456 | tf_op jit(solution)/shard_map/attention/pallas_call | solution.py:476
  199.5 4.4 %local_tiles.3.part = f32[17,128,256]{2,1,0:T(8,128)} custom-call(s32[1,96]{1,0:T(1,128)S(1)} %copy-done.14, s32[1,96]{1,0:T(1,128)S(1)} %copy-done.15, s32[1]{0:T(128)S(6)} %copy.12.count, bf16[96,128,128]{2,1,0:T(8,128)(2,1)S(1)} %copy-done, bf16[16,128,256]{2,1,0:T(8,128)(2,1)} %get-tuple-element.28.refs_0_, ...), custom_call_target="tpu_custom_call" | custom-call | flops 402653184 | bytes 9437184 | tf_op jit(solution)/shard_map/local_tiles/pallas_call | solution.py:399
  203.9 20.0 %all-to-all-done.1.blocks = bf16[64,128,256]{2,1,0:T(8,128)(2,1)} async-done(((bf16[64,128,256]{2,1,0:T(8,128)(2,1)}), bf16[64,128,256]{2,1,0:T(8,128)(2,1)}, u32[]{:S(2)}, u32[]{:S(2)}) %all-to-all-start.1) | async-done | bytes 4194336 | tf_op jit(solution)/shard_map/all_to_all | solution.py:558
  223.9 5.5 %halo_tiles_norm.1 = bf16[16,128,256]{2,1,0:T(8,128)(2,1)} custom-call(s32[1,96]{1,0:T(1,128)S(1)} %copy-done.14, s32[1,96]{1,0:T(1,128)S(1)} %copy-done.15, s32[1]{0:T(128)S(6)} %copy.12.count, bf16[96,128,128]{2,1,0:T(8,128)(2,1)S(1)} %copy-done, bf16[64,128,256]{2,1,0:T(8,128)(2,1)} %all-to-all-done.1.blocks, f32[17,128,256]{2,1,0:T(8,128)} %local_tiles.3.part, ...), custom_call_target="tpu_custom_call" | custom-call | tf_op jit(solution)/shard_map/halo_tiles_norm/pallas_call | solution.py:521
  (104 shorter events, 56.4 us)
Async XLA Ops:
  4.0 109.3 %all-to-all-start = ((bf16[64,128,256]{2,1,0:T(8,128)(2,1)}), bf16[64,128,256]{2,1,0:T(8,128)(2,1)}, u32[]{:S(2)}, u32[]{:S(2)}) async-start(bf16[64,128,256]{2,1,0:T(8,128)(2,1)} %get-tuple-element.17), calls=%async_computation | async-start | bytes 8388608 | tf_op jit(solution)/shard_map/all_to_all | solution.py:552
  17.5 64.3 %collective-permute-start = (bf16[16,128,256]{2,1,0:T(8,128)(2,1)}, bf16[16,128,256]{2,1,0:T(8,128)(2,1)}, u32[]{:S(2)}, u32[]{:S(2)}) collective-permute-start(bf16[16,128,256]{2,1,0:T(8,128)(2,1)} %get-tuple-element.18.after.refs_0_), channel_id=1, source_target_pairs={{0,1},{1,2},{2,3},{3,0},{4,5},{5,6},{6,7},{7,4},{8,9},{9,10},{10,1... | collective-permute-start | bytes 3145736 | tf_op jit(solution)/shard_map/ppermute | solution.py:538
  18.7 63.4 %collective-permute-start.1 = (bf16[16,128,256]{2,1,0:T(8,128)(2,1)}, bf16[16,128,256]{2,1,0:T(8,128)(2,1)}, u32[]{:S(2)}, u32[]{:S(2)}) collective-permute-start(bf16[16,128,256]{2,1,0:T(8,128)(2,1)} %get-tuple-element.18.after.refs_0_), channel_id=1, source_target_pairs={{0,2},{1,3},{2,0},{3,1},{4,6},{5,7},{6,4},{7,5},{8,10},{9,11},{10,... | collective-permute-start | bytes 3145736 | tf_op jit(solution)/shard_map/ppermute | solution.py:538
  21.5 61.3 %collective-permute-start.2 = (bf16[16,128,256]{2,1,0:T(8,128)(2,1)}, bf16[16,128,256]{2,1,0:T(8,128)(2,1)}, u32[]{:S(2)}, u32[]{:S(2)}) collective-permute-start(bf16[16,128,256]{2,1,0:T(8,128)(2,1)} %get-tuple-element.18.after.refs_0_), channel_id=1, source_target_pairs={{0,3},{1,0},{2,1},{3,2},{4,7},{5,4},{6,5},{7,6},{8,11},{9,8},{10,9... | collective-permute-start | bytes 3145736 | tf_op jit(solution)/shard_map/ppermute | solution.py:538
  32.7 2.8 %collective-permute-start.3 = (f32[264,256]{1,0:T(8,128)S(1)}, f32[264,256]{1,0:T(8,128)}, u32[]{:S(2)}, u32[]{:S(2)}) collective-permute-start(f32[264,256]{1,0:T(8,128)S(1)} %attention_sums.1.mine), channel_id=1, source_target_pairs={{0,4},{4,0},{8,12},{12,8},{16,20},{20,16},{24,28},{28,24},{32,36},... | collective-permute-start | bytes 811016 | tf_op jit(solution)/shard_map/ppermute | solution.py:272
  37.3 7.9 %collective-permute-start.4 = (f32[136,256]{1,0:T(8,128)}, f32[136,256]{1,0:T(8,128)S(1)}, u32[]{:S(2)}, u32[]{:S(2)}) collective-permute-start(f32[136,256]{1,0:T(8,128)} %get-tuple-element.20), channel_id=1, source_target_pairs={{0,64},{4,68},{8,72},{12,76},{16,80},{20,84},{24,88},{28,92},{32,9... | collective-permute-start | bytes 417800 | tf_op jit(solution)/shard_map/ppermute | solution.py:272
  47.5 6.0 %collective-permute-start.5 = (f32[72,256]{1,0:T(8,128)}, f32[72,256]{1,0:T(8,128)S(1)}, u32[]{:S(2)}, u32[]{:S(2)}) collective-permute-start(f32[72,256]{1,0:T(8,128)} %get-tuple-element.22), channel_id=1, source_target_pairs={{0,128},{4,132},{8,136},{12,140},{16,144},{20,148},{24,152},{28,15... | collective-permute-start | bytes 221192 | tf_op jit(solution)/shard_map/ppermute | solution.py:272
  55.7 11.5 %collective-permute-start.6 = (f32[40,256]{1,0:T(8,128)}, f32[40,256]{1,0:T(8,128)S(1)}, u32[]{:S(2)}, u32[]{:S(2)}) collective-permute-start(f32[40,256]{1,0:T(8,128)} %get-tuple-element.24), channel_id=1, source_target_pairs={{0,1},{1,0},{2,3},{3,2},{4,5},{5,4},{6,7},{7,6},{8,9},{9,8},{10,11... | collective-permute-start | bytes 122888 | tf_op jit(solution)/shard_map/ppermute | solution.py:272
  69.3 4.7 %collective-permute-start.7 = (f32[24,256]{1,0:T(8,128)}, f32[24,256]{1,0:T(8,128)S(1)}, u32[]{:S(2)}, u32[]{:S(2)}) collective-permute-start(f32[24,256]{1,0:T(8,128)} %get-tuple-element.26), channel_id=1, source_target_pairs={{0,2},{1,3},{2,0},{3,1},{4,6},{5,7},{6,4},{7,5},{8,10},{9,11},{10,... | collective-permute-start | bytes 73736 | tf_op jit(solution)/shard_map/ppermute | solution.py:272
  75.9 32.9 %collective-permute-start.8 = (f32[24,256]{1,0:T(8,128)}, f32[24,256]{1,0:T(8,128)S(1)}, u32[]{:S(2)}, u32[]{:S(2)}) collective-permute-start(f32[24,256]{1,0:T(8,128)} %merge_sums.3.refs_4_.refs_0_), channel_id=1, source_target_pairs={{0,8},{4,44},{8,16},{12,52},{16,24},{20,60},{24,32},{28,4},{32,40}... | collective-permute-start | bytes 73736 | tf_op jit(solution)/shard_map/ppermute | solution.py:292
  80.6 30.6 %collective-permute-start.9 = (f32[24,256]{1,0:T(8,128)}, f32[24,256]{1,0:T(8,128)S(1)}, u32[]{:S(2)}, u32[]{:S(2)}) collective-permute-start(f32[24,256]{1,0:T(8,128)} %merge_sums.3.refs_4_.refs_0_), channel_id=1, source_target_pairs={{0,16},{4,52},{8,24},{12,60},{16,32},{20,4},{24,40},{28,12},{32,48... | collective-permute-start | bytes 73736 | tf_op jit(solution)/shard_map/ppermute | solution.py:292
  81.8 30.0 %collective-permute-start.10 = (f32[24,256]{1,0:T(8,128)}, f32[24,256]{1,0:T(8,128)S(1)}, u32[]{:S(2)}, u32[]{:S(2)}) collective-permute-start(f32[24,256]{1,0:T(8,128)} %merge_sums.3.refs_4_.refs_0_), channel_id=1, source_target_pairs={{0,24},{4,60},{8,32},{12,4},{16,40},{20,12},{24,48},{28,20},{32,56... | collective-permute-start | bytes 73736 | tf_op jit(solution)/shard_map/ppermute | solution.py:292
  82.1 29.7 %collective-permute-start.11 = (f32[24,256]{1,0:T(8,128)}, f32[24,256]{1,0:T(8,128)S(1)}, u32[]{:S(2)}, u32[]{:S(2)}) collective-permute-start(f32[24,256]{1,0:T(8,128)} %merge_sums.3.refs_4_.refs_0_), channel_id=1, source_target_pairs={{0,32},{8,40},{16,48},{24,56},{32,0},{40,8},{48,16},{56,24},{64,96... | collective-permute-start | bytes 73736 | tf_op jit(solution)/shard_map/ppermute | solution.py:292
  118.8 68.6 %copy-start.20 = (bf16[256,256]{1,0:T(8,128)(2,1)S(1)}, bf16[256,256]{1,0:T(8,128)(2,1)}, u32[]{:S(2)}) copy-start(bf16[256,256]{1,0:T(8,128)(2,1)} %qw.3) | copy-start | bytes 393220
  118.8 68.6 %copy-start.22 = (bf16[256,256]{1,0:T(8,128)(2,1)S(1)}, bf16[256,256]{1,0:T(8,128)(2,1)}, u32[]{:S(2)}) copy-start(bf16[256,256]{1,0:T(8,128)(2,1)} %vw.3) | copy-start | bytes 393220
  118.8 105.1 %all-to-all-start.1 = ((bf16[64,128,256]{2,1,0:T(8,128)(2,1)}), bf16[64,128,256]{2,1,0:T(8,128)(2,1)}, u32[]{:S(2)}, u32[]{:S(2)}) async-start(bf16[64,128,256]{2,1,0:T(8,128)(2,1)} %get-tuple-element.27), calls=%async_computation.1 | async-start | bytes 8388608 | tf_op jit(solution)/shard_map/all_to_all | solution.py:558
  128.0 69.9 %collective-permute-start.12 = (bf16[16,128,256]{2,1,0:T(8,128)(2,1)}, bf16[16,128,256]{2,1,0:T(8,128)(2,1)}, u32[]{:S(2)}, u32[]{:S(2)}) collective-permute-start(bf16[16,128,256]{2,1,0:T(8,128)(2,1)} %get-tuple-element.28.refs_0_), channel_id=1, source_target_pairs={{0,1},{1,2},{2,3},{3,0},{4,5},{5,6},{6,7},{7,4},{8,9},{9,10},{10,1... | collective-permute-start | bytes 3145736 | tf_op jit(solution)/shard_map/ppermute | solution.py:538
  129.8 68.0 %collective-permute-start.13 = (bf16[16,128,256]{2,1,0:T(8,128)(2,1)}, bf16[16,128,256]{2,1,0:T(8,128)(2,1)}, u32[]{:S(2)}, u32[]{:S(2)}) collective-permute-start(bf16[16,128,256]{2,1,0:T(8,128)(2,1)} %get-tuple-element.28.refs_0_), channel_id=1, source_target_pairs={{0,2},{1,3},{2,0},{3,1},{4,6},{5,7},{6,4},{7,5},{8,10},{9,11},{10,... | collective-permute-start | bytes 3145736 | tf_op jit(solution)/shard_map/ppermute | solution.py:538
  132.2 65.6 %collective-permute-start.14 = (bf16[16,128,256]{2,1,0:T(8,128)(2,1)}, bf16[16,128,256]{2,1,0:T(8,128)(2,1)}, u32[]{:S(2)}, u32[]{:S(2)}) collective-permute-start(bf16[16,128,256]{2,1,0:T(8,128)(2,1)} %get-tuple-element.28.refs_0_), channel_id=1, source_target_pairs={{0,3},{1,0},{2,1},{3,2},{4,7},{5,4},{6,5},{7,6},{8,11},{9,8},{10,9... | collective-permute-start | bytes 3145736 | tf_op jit(solution)/shard_map/ppermute | solution.py:538
  134.8 2.4 %collective-permute-start.15 = (f32[24,256]{1,0:T(8,128)}, f32[24,256]{1,0:T(8,128)S(1)}, u32[]{:S(2)}, u32[]{:S(2)}) collective-permute-start(f32[24,256]{1,0:T(8,128)} %merge_sums.4.refs_0_), channel_id=1, source_target_pairs={{0,4},{4,0},{8,12},{12,8},{16,20},{20,16},{24,28},{28,24},{32,36},... | collective-permute-start | bytes 73736 | tf_op jit(solution)/shard_map/ppermute | solution.py:272
  139.9 4.9 %collective-permute-start.16 = (f32[16,256]{1,0:T(8,128)S(1)}, f32[16,256]{1,0:T(8,128)S(1)}, u32[]{:S(2)}, u32[]{:S(2)}) collective-permute-start(f32[16,256]{1,0:T(8,128)S(1)} %slice.8.mine), channel_id=1, source_target_pairs={{0,128},{4,132},{8,136},{12,140},{16,144},{20,148},{24,152},{28,15... | collective-permute-start | bytes 49160 | tf_op jit(solution)/shard_map/ppermute | solution.py:272
  146.8 3.9 %collective-permute-start.17 = (f32[32,256]{1,0:T(8,128)}, f32[32,256]{1,0:T(8,128)S(1)}, u32[]{:S(2)}, u32[]{:S(2)}) collective-permute-start(f32[32,256]{1,0:T(8,128)} %join_sums.4.mine), channel_id=1, source_target_pairs={{0,64},{4,68},{8,72},{12,76},{16,80},{20,84},{24,88},{28,92},{32,9... | collective-permute-start | bytes 98312 | tf_op jit(solution)/shard_map/ppermute | solution.py:272
  152.7 26.5 %collective-permute-start.18 = (f32[64,256]{1,0:T(8,128)}, f32[64,256]{1,0:T(8,128)S(1)}, u32[]{:S(2)}, u32[]{:S(2)}) collective-permute-start(f32[64,256]{1,0:T(8,128)} %join_sums.5.mine), channel_id=1, source_target_pairs={{0,2},{1,3},{2,0},{3,1},{4,6},{5,7},{6,4},{7,5},{8,10},{9,11},{10,... | collective-permute-start | bytes 196616 | tf_op jit(solution)/shard_map/ppermute | solution.py:272
  181.3 4.4 %collective-permute-start.19 = (f32[128,256]{1,0:T(8,128)}, f32[128,256]{1,0:T(8,128)}, u32[]{:S(2)}, u32[]{:S(2)}) collective-permute-start(f32[128,256]{1,0:T(8,128)} %join_sums.6.mine), channel_id=1, source_target_pairs={{0,1},{1,0},{2,3},{3,2},{4,5},{5,4},{6,7},{7,6},{8,9},{9,8},{10,11... | collective-permute-start | bytes 393224 | tf_op jit(solution)/shard_map/ppermute | solution.py:272
  (30 other events, 340.4 us)

commit v4 on v3

--- a/solution.py
+++ b/solution.py
@@ -9,13 +9,14 @@
 
 D = 256
 BLOCK = 128
-UNROLL = 8
+PAIRS = 4
 CHUNK = 256
 NORM = 4
 EXTRA = 8
 CORE = ("wide", 0)
 HALVE = (("wide", 4), ("wide", 5), ("narrow", 0), ("narrow", 1))
 DEPTH = 8
+AROUND = ((2, 4), (6, 3), (1, 5), (7, 0))
 JOIN = (("wide", 5), ("wide", 4), ("narrow", 1), ("narrow", 0))
 F32 = jnp.float32
 BF16 = jnp.bfloat16
@@ -280,16 +281,16 @@
 
 
 def along_depth(mine):
-    span, reach = 2 * DEPTH, DEPTH // 2
+    span = 2 * DEPTH
 
     def shift(by):
         return [
-            (i, i // span * span + (i + 2 * (by + reach * (i % 2))) % span)
+            (i, i // span * span + (i + 2 * by[i % 2]) % span)
             for i in range(lax.axis_size("wide"))
-            if by + reach * (i % 2) < DEPTH
+            if by[i % 2]
         ]
 
-    return [lax.ppermute(mine, "wide", shift(by)) for by in range(1, reach + 1)]
+    return [lax.ppermute(mine, "wide", shift(by)) for by in AROUND]
 
 
 def whole_sums(mine, others):
@@ -301,127 +302,173 @@
     return rows, extra
 
 
-def collect(rows, cols, count, first, last, spare, lists):
-    slots, places, targets = lists
-
-    def one(t, n):
-        c = cols[0, t]
-        slots[n] = t
-        places[n] = c - first
-        targets[n] = rows[0, t]
-        return n + ((c >= first) & (c < last)).astype(jnp.int32)
-
-    n = lax.fori_loop(0, count[0], one, jnp.int32(0))
-    for u in range(UNROLL):
-        slots[n + u] = 0
-        places[n + u] = 0
-        targets[n + u] = spare
-    return n
-
-
-def add_tiles(n, lists, tiles, blocks, acc):
-    slots, places, targets = lists
-
+def plan_kernel(nblocks, first, last, rows, cols, count, local, halo, heads, nexts):
+    for out, low, high in ((local, 0, first), (halo, first, last)):
+        def clear(r, _):
+            heads[r] = -1
+            return 0
+
+        lax.fori_loop(0, nblocks, clear, 0)
+
+        def one(t, _):
+            c, r = cols[0, t], rows[0, t]
+
+            @pl.when((c >= low) & (c < high))
+            def _():
+                nexts[t] = heads[r]
+                heads[r] = t
+
+            return 0
+
+        lax.fori_loop(0, count[0], one, 0)
+
+        def place(r, n):
+            def pair(at):
+                t, n = at
+                other = nexts[t]
+                both = other >= 0
+                second = jnp.where(both, other, t)
+                out[0, n] = t
+                out[1, n] = second
+                out[2, n] = cols[0, t] - low
+                out[3, n] = cols[0, second] - low
+                out[4, n] = both.astype(jnp.int32)
+                out[5, n] = r
+                return jnp.where(both, nexts[second], -1), n + 1
+
+            return lax.while_loop(lambda at: at[0] >= 0, pair, (heads[r], n))[1]
+
+        n = lax.fori_loop(0, nblocks, place, jnp.int32(0))
+        for u in range(PAIRS):
+            for line in range(5):
+                out[line, n + u] = 0
+            out[5, n + u] = nblocks
+        out[6, 0] = (n + PAIRS - 1) // PAIRS
+
+
+def plan(rows, cols, count, nblocks, first, last, after):
+    slots = rows.shape[1]
+    width = -(-((slots + nblocks) // 2 + PAIRS) // PAIRS) * PAIRS
+    shape = jax.ShapeDtypeStruct((8, width), jnp.int32)
+
+    def kernel(rows, cols, count, after, *refs):
+        plan_kernel(nblocks, first, last, rows, cols, count, *refs)
+
+    return pl.pallas_call(
+        kernel,
+        out_shape=(shape, shape),
+        in_specs=[SMEM] * 3 + [HBM],
+        out_specs=(SMEM, SMEM),
+        scratch_shapes=[pltpu.SMEM((nblocks,), jnp.int32), pltpu.SMEM((slots,), jnp.int32)],
+        name="plan_tiles",
+    )(rows, cols, count, after)
+
+
+def add_pairs(steps, tiles, two_blocks, acc, before):
     def step(i, _):
-        prods = [
-            jnp.dot(tiles[slots[i * UNROLL + u]], blocks[places[i * UNROLL + u]], preferred_element_type=F32)
-            for u in range(UNROLL)
-        ]
-        for u in range(UNROLL):
-            r = targets[i * UNROLL + u]
+        before(i)
+        prods = []
+        for u in range(PAIRS):
+            j = i * PAIRS + u
+            second = tiles[steps[1, j]]
+            second = jnp.where(steps[4, j] > 0, second, jnp.zeros_like(second))
+            both = jnp.concatenate([tiles[steps[0, j]], second], 1)
+            prods.append(jnp.dot(both, two_blocks(j), preferred_element_type=F32))
+        for u in range(PAIRS):
+            r = steps[5, i * PAIRS + u]
             acc[r] = acc[r] + prods[u]
         return 0
 
-    lax.fori_loop(0, (n + UNROLL - 1) // UNROLL, step, 0)
-
-
-def load_halo(n, places, blocks, got, sems):
-    def one(i, _):
-        for u in range(UNROLL):
-            j = i * UNROLL + u
-            pltpu.make_async_copy(blocks.at[places[j]], got.at[j], sems.at[i]).start()
-        return 0
-
-    lax.fori_loop(0, (n + UNROLL - 1) // UNROLL, one, 0)
-
-
-def add_halo(n, lists, tiles, got, acc, sems):
-    slots, places, targets = lists
-
-    def step(i, _):
-        at = pl.ds(i * UNROLL, UNROLL)
-        pltpu.make_async_copy(got.at[at], got.at[at], sems.at[i]).wait()
-        prods = [
-            jnp.dot(tiles[slots[i * UNROLL + u]], got[i * UNROLL + u], preferred_element_type=F32)
-            for u in range(UNROLL)
-        ]
-        for u in range(UNROLL):
-            r = targets[i * UNROLL + u]
-            acc[r] = acc[r] + prods[u]
-        return 0
-
-    lax.fori_loop(0, (n + UNROLL - 1) // UNROLL, step, 0)
-
-
-def halo_scratch(rows, part):
-    steps = -(-rows.shape[1] // UNROLL)
-    return [
-        pltpu.VMEM((steps * UNROLL, BLOCK, D), BF16),
-        pltpu.VMEM(part.shape, F32),
-        pltpu.VMEM(part.shape, F32),
-        pltpu.SemaphoreType.DMA((steps + 1,)),
-    ] + lists_of(rows)
-
-
-def local_kernel(rows, cols, count, tiles, *refs):
-    parts, after, acc, blocks, sems, lists = refs[:-7], refs[-7], refs[-6], refs[-5], refs[-4], refs[-3:]
-    groups, nblocks = len(parts), parts[0].shape[0]
+    lax.fori_loop(0, steps[6, 0], step, 0)
+
+
+def local_kernel(nparts, steps, tiles, *refs):
+    parts, (base, out, blocks, acc, result, sems) = refs[:nparts], refs[nparts:]
+    nblocks = parts[0].shape[0]
     me = lax.axis_index("narrow")
     loads = []
     for by, part in enumerate(parts):
-        owner = lax.rem(me + groups - by, groups)
+        owner = lax.rem(me + nparts - by, nparts)
         place = blocks.at[pl.ds(owner * nblocks, nblocks)]
         loads.append(pltpu.make_async_copy(part, place, sems.at[by]))
-        loads[-1].start()
-    n = collect(rows, cols, count, 0, blocks.shape[0], nblocks, lists)
+    with_base = base.shape == result.shape
+    if with_base:
+        loads.append(pltpu.make_async_copy(base, result, sems.at[nparts]))
+    for load in loads:
+        load.start()
     acc[...] = jnp.zeros_like(acc)
     for load in loads:
         load.wait()
-    add_tiles(n, lists, tiles, blocks, acc)
-
-
-def lists_of(rows):
-    return [pltpu.SMEM((rows.shape[1] + UNROLL,), jnp.int32)] * 3
-
-
-def local_tiles(rows, cols, count, tiles, parts, after):
+    add_pairs(
+        steps, tiles, lambda j: jnp.concatenate([blocks[steps[2, j]], blocks[steps[3, j]]], 0), acc, lambda i: None
+    )
+    if with_base:
+        result[...] = result[...] + acc[:nblocks] / 3.0
+    else:
+        result[...] = acc[:nblocks]
+    store = pltpu.make_async_copy(result, out, sems.at[nparts + 1])
+    store.start()
+    store.wait()
+
+
+def local_tiles(steps, tiles, parts, base):
     nblocks = parts[0].shape[0]
     return pl.pallas_call(
-        local_kernel,
-        out_shape=pltpu.HBM((nblocks + 1, BLOCK, D), F32),
-        in_specs=[SMEM, SMEM, SMEM, VMEM] + [HBM] * (len(parts) + 1),
-        out_specs=VMEM,
+        functools.partial(local_kernel, len(parts)),
+        out_shape=pltpu.HBM((nblocks, BLOCK, D), F32),
+        in_specs=[SMEM, VMEM] + [HBM] * (len(parts) + 1),
+        out_specs=HBM,
         scratch_shapes=[
             pltpu.VMEM((len(parts) * nblocks, BLOCK, D), BF16),
-            pltpu.SemaphoreType.DMA((len(parts),)),
-        ] + lists_of(rows),
-        compiler_params=params(16),
+            pltpu.VMEM((nblocks + 1, BLOCK, D), F32),
+            pltpu.VMEM((nblocks, BLOCK, D), F32),
+            pltpu.SemaphoreType.DMA((len(parts) + 2,)),
+        ],
+        compiler_params=params(20),
         cost_estimate=cost(48 * BLOCK * BLOCK * D * 2, 9 << 20),
         name="local_tiles",
-    )(rows, cols, count, tiles, *map(in_hbm, parts), after)
-
-
-def hop_kernel(first, send, rows, cols, count, tiles, blocks, part, *refs):
-    h_out, out, got, acc, local, loads, *rest = refs[DEPTH // 2:]
-    lists, (h_own, zeros, heads, nexts, sems) = rest[:3], rest[3:]
+    )(steps, tiles, *map(in_hbm, parts), in_hbm(base))
+
+
+def load_halo(steps, blocks, got, sems):
+    def one(i, _):
+        for u in range(PAIRS):
+            j = i * PAIRS + u
+            for half in range(2):
+                place = got.at[j, pl.ds(half * BLOCK, BLOCK)]
+                pltpu.make_async_copy(blocks.at[steps[2 + half, j]], place, sems.at[i]).start()
+        return 0
+
+    lax.fori_loop(0, steps[6, 0], one, 0)
+
+
+def add_halo(steps, tiles, got, acc, sems):
+    def before(i):
+        at = pl.ds(i * PAIRS, PAIRS)
+        pltpu.make_async_copy(got.at[at], got.at[at], sems.at[i]).wait()
+
+    add_pairs(steps, tiles, lambda j: got[j], acc, before)
+
+
+def halo_scratch(steps, part):
+    nblocks = part.shape[0]
+    return [
+        pltpu.VMEM((steps.shape[1], 2 * BLOCK, D), BF16),
+        pltpu.VMEM((nblocks + 1, BLOCK, D), F32),
+        pltpu.VMEM(part.shape, F32),
+        pltpu.SemaphoreType.DMA((steps.shape[1] // PAIRS + 1,)),
+    ]
+
+
+def hop_kernel(send, steps, tiles, blocks, part, *refs):
+    h_out, out, got, acc, local, loads, h_own, zeros, heads, nexts, sems = refs[len(AROUND):]
     nblocks = h_own.shape[0]
-    n = collect(rows, cols, count, first, first + blocks.shape[0], nblocks, lists)
-    load_halo(n, lists[1], blocks, got, loads)
+    load_halo(steps, blocks, got, loads)
     load = pltpu.make_async_copy(part, local, loads.at[loads.shape[0] - 1])
     load.start()
     send_order(send, heads, nexts, zeros, out, sems.at[1])
     acc[...] = jnp.zeros_like(acc)
-    add_halo(n, lists, tiles, got, acc, loads)
+    add_halo(steps, tiles, got, acc, loads)
     load.wait()
 
     def one(b, _):
@@ -433,17 +480,17 @@
     wait_sent(h_own, h_out, out, sems)
 
 
-def hop(send, rows, cols, count, tiles, blocks, part, after, first):
-    nblocks = part.shape[0] - 1
-    return pl.pallas_call(
-        functools.partial(hop_kernel, first),
+def hop(send, steps, tiles, blocks, part, after):
+    nblocks = part.shape[0]
+    return pl.pallas_call(
+        hop_kernel,
         out_shape=(pltpu.HBM((nblocks, BLOCK, D), BF16), pltpu.HBM(blocks.shape, BF16)),
-        in_specs=[SMEM] * 4 + [VMEM, HBM, HBM] + [HBM] * len(after),
+        in_specs=[SMEM, SMEM, VMEM, HBM, HBM] + [HBM] * len(after),
         out_specs=(HBM, HBM),
-        scratch_shapes=halo_scratch(rows, part) + send_scratch(nblocks, blocks.shape[0]),
+        scratch_shapes=halo_scratch(steps, part) + send_scratch(nblocks, blocks.shape[0]),
         compiler_params=params(20),
         name="halo_tiles_send",
-    )(send, rows, cols, count, tiles, in_hbm(blocks), in_hbm(part), *after)
+    )(send, steps, tiles, in_hbm(blocks), in_hbm(part), *after)
 
 
 def attention_kernel(total, x, qw, vw, kv_sums, extra, hop_zero, hop_one, out, kv):
@@ -485,26 +532,19 @@
     )(x, qw, vw, kv_sums, extra, hop_zero, hop_one)
 
 
-def finish_kernel(first, rows, cols, count, tiles, blocks, part, base, gain, out, got, acc, local, loads, *rest):
-    lists, (mixing, base_sem, done, sem) = rest[:3], rest[3:]
-    nblocks = part.shape[0] - 1
-    n = collect(rows, cols, count, first, first + blocks.shape[0], nblocks, lists)
-    load_halo(n, lists[1], blocks, got, loads)
-    late = [
-        pltpu.make_async_copy(part, local, loads.at[loads.shape[0] - 1]),
-        pltpu.make_async_copy(base, mixing, base_sem),
-    ]
-    for load in late:
-        load.start()
+def finish_kernel(steps, tiles, blocks, base, gain, out, got, acc, mixing, loads, done, sem):
+    nblocks = base.shape[0]
+    load_halo(steps, blocks, got, loads)
+    load = pltpu.make_async_copy(base, mixing, loads.at[loads.shape[0] - 1])
+    load.start()
     acc[...] = jnp.zeros_like(acc)
-    add_halo(n, lists, tiles, got, acc, loads)
-    for load in late:
-        load.wait()
+    add_halo(steps, tiles, got, acc, loads)
+    load.wait()
 
     def some(i, _):
         for u in range(NORM):
             b = i * NORM + u
-            mixed = mixing[b] + (acc[b] + local[b]).astype(BF16).astype(F32) / 3.0
+            mixed = mixing[b] + acc[b] / 3.0
             center = mixed - jnp.mean(mixed, 1, keepdims=True)
             scale = lax.rsqrt(jnp.mean(center * center, 1, keepdims=True) + 1e-05)
             done[b] = (gain[...] * center * scale).astype(BF16)
@@ -516,20 +556,19 @@
     pltpu.make_async_copy(done, out, sem).wait()
 
 
-def finish(rows, cols, count, tiles, blocks, part, base, gain, first):
-    nblocks = part.shape[0] - 1
-    return pl.pallas_call(
-        functools.partial(finish_kernel, first),
+def finish(steps, tiles, blocks, base, gain):
+    nblocks = base.shape[0]
+    return pl.pallas_call(
+        finish_kernel,
         out_shape=jax.ShapeDtypeStruct((nblocks, BLOCK, D), BF16),
-        in_specs=[SMEM] * 3 + [VMEM, HBM, HBM, HBM, VMEM],
+        in_specs=[SMEM, VMEM, HBM, HBM, VMEM],
         out_specs=HBM,
-        scratch_shapes=halo_scratch(rows, part) + [
-            pltpu.VMEM(base.shape, F32), pltpu.SemaphoreType.DMA,
+        scratch_shapes=halo_scratch(steps, base) + [
             pltpu.VMEM((nblocks, BLOCK, D), BF16), pltpu.SemaphoreType.DMA,
         ],
         compiler_params=params(20),
         name="halo_tiles_norm",
-    )(rows, cols, count, tiles, in_hbm(blocks), in_hbm(part), in_hbm(base), gain)
+    )(steps, tiles, in_hbm(blocks), in_hbm(base), gain)
 
 
 def group_blocks(own):
@@ -546,23 +585,23 @@
     peers, groups = lax.axis_size("wide"), lax.axis_size("narrow")
     total = float(rows_dev * peers * groups)
     first = groups * nblocks
-    slots = (tile_rows, tile_cols, tile_count, tiles)
 
     hop_zero, outgoing = start(send_list, x, gw, peers)
     received = lax.all_to_all(outgoing, "wide", 0, 0, tiled=True)
     group = group_blocks(hop_zero)
     mine = partial_sums(stats(x, qw, kw, vw, hop_zero))
     others = along_depth(mine)
-    part = local_tiles(*slots, group, mine)
-    hop_one, outgoing = hop(send_list, *slots, received, part, others, first)
+    local, halo = plan(tile_rows, tile_cols, tile_count, nblocks, first, first + peers, hop_zero)
+    part = local_tiles(local, tiles, group, mine)
+    hop_one, outgoing = hop(send_list, halo, tiles, received, part, others)
     received = lax.all_to_all(outgoing, "wide", 0, 0, tiled=True)
     group = group_blocks(hop_one)
     kv_sums, extra = whole_sums(mine, others)
     base = attention(
         total, x, qw, vw, kv_sums, extra, hop_zero.reshape(rows_dev, D), hop_one.reshape(rows_dev, D)
     )
-    part = local_tiles(*slots, group, base)
-    out = finish(*slots, received, part, base.reshape(nblocks, BLOCK, D), gain[None, :], first)
+    base = local_tiles(local, tiles, group, base.reshape(nblocks, BLOCK, D))
+    out = finish(halo, tiles, received, base, gain[None, :])
     return out.reshape(rows_dev, D)
 
 

time: 232 us -> 230 us (level)
  waiting for transfers between devices: 104 us -> 97.1 us
  Pallas kernels: 52.1 us -> 55.6 us
    ppermute x4, waiting for transfers between devices: 23.9 us -> 19.9 us  [along_depth(): return [lax.ppermute(mine, 'wide', shift(by)) for by in AROUND]]
    ppermute x4, starting transfers between devices: 6.83 us -> 10.7 us  [along_depth(): return [lax.ppermute(mine, 'wide', shift(by)) for by in AROUND]]
    pallas_call x4 -> x5, Pallas kernels: 19.8 us -> 23.3 us  [the longest x2 10.8 us: local_tiles(): pl.pallas_call(functools.partial(local_kernel, len(parts)), out_shape=plt...]
  transfers between devices with their start and end apart: 22 -> 22, of which waited for: 15 -> 12; matrix products, arithmetic and copies ran while one was open for 1% -> 1% of each run, Pallas kernels for 16% -> 18%
where the time goes in v4:
time: 230 us; the launch traced here: 228 us
  waiting for transfers between devices  97.1 us (42%)
  starting transfers between devices  57.5 us (25%)
  Pallas kernels  55.6 us (24%)
  local copies, waits for them, and re-layouts  16.7 us (7%)
    ppermute x10, waiting for transfers between devices, swap(): lax.ppermute(x, axis, [(i, i ^ 1 << bit) for i in range(lax.axis_size(axi...  57.4 us
    all_to_all x2, starting transfers between devices, shards(): received = lax.all_to_all(outgoing, 'wide', 0, 0, tiled=True)  21.5 us
    ppermute x4, waiting for transfers between devices, along_depth(): return [lax.ppermute(mine, 'wide', shift(by)) for by in AROUND]  19.9 us
    all_to_all x2, waiting for transfers between devices, shards(): received = lax.all_to_all(outgoing, 'wide', 0, 0, tiled=True)  19.7 us
    unnamed x64, local copies, waits for them, and re-layouts  15.2 us
    ppermute x10, starting transfers between devices, swap(): lax.ppermute(x, axis, [(i, i ^ 1 << bit) for i in range(lax.axis_size(axi...  15.1 us
    pallas_call x2, Pallas kernels, local_tiles(): pl.pallas_call(functools.partial(local_kernel, len(parts)), out_shape=plt...  10.8 us
    ppermute x4, starting transfers between devices, along_depth(): return [lax.ppermute(mine, 'wide', shift(by)) for by in AROUND]  10.7 us
  transfers between devices with their start and end apart: 22, of which 12 were waited for; matrix products, arithmetic and copies ran while one was open for 1% of the time, Pallas kernels for 18%

profile of v4, /device:TPU:1, one launch (start us, length us, event | category | flops | bytes accessed | tf_op | source)
XLA Modules:
  0.0 228.0 jit_solution(13903287818902017107)
XLA Ops:
  0.0 4.0 %project_send.1 = (bf16[16,128,256]{2,1,0:T(8,128)(2,1)}, bf16[64,128,256]{2,1,0:T(8,128)(2,1)}) custom-call(s32[1,64]{1,0:T(1,128)} %send.3, bf16[2048,256]{1,0:T(8,128)(2,1)} %x.5, bf16[256,256]{1,0:T(8,128)(2,1)} %weight.1), custom_call_target="tpu_custom_call" | custom-call | tf_op jit(solution)/shard_map/project_send/pallas_call | solution.py:124
  4.1 13.3 %all-to-all-start = ((bf16[64,128,256]{2,1,0:T(8,128)(2,1)}), bf16[64,128,256]{2,1,0:T(8,128)(2,1)}, u32[]{:S(2)}, u32[]{:S(2)}) async-start(bf16[64,128,256]{2,1,0:T(8,128)(2,1)} %get-tuple-element.21), calls=%async_computation | async-start | bytes 8388608 | tf_op jit(solution)/shard_map/all_to_all | solution.py:590
  26.7 5.8 %attention_sums.1.mine = f32[264,256]{1,0:T(8,128)S(1)} custom-call(bf16[2048,256]{1,0:T(8,128)(2,1)S(1)} %copy-done.3, bf16[256,256]{1,0:T(8,128)(2,1)S(1)} %copy-done.18, bf16[256,256]{1,0:T(8,128)(2,1)S(1)} %copy-done.17, bf16[256,256]{1,0:T(8,128)(2,1)S(1)} %copy-done.20, bf16[16,128,256]{2,1,0:T(8,128)(2,1)S(1)} %copy-done.1), custom_call_target="tpu_custom_call" | custom-call | flops 2415919104 | bytes 2097152 | tf_op jit(solution)/shard_map/attention_sums/pallas_call | solution.py:192
  38.4 6.6 %collective-permute-done.4.other = f32[136,256]{1,0:T(8,128)S(1)} collective-permute-done((f32[136,256]{1,0:T(8,128)}, f32[136,256]{1,0:T(8,128)S(1)}, u32[]{:S(2)}, u32[]{:S(2)}) %collective-permute-start.4) | collective-permute-done | bytes 139296 | tf_op jit(solution)/shard_map/ppermute | solution.py:273
  47.4 2.9 %collective-permute-start.5 = (f32[72,256]{1,0:T(8,128)}, f32[72,256]{1,0:T(8,128)S(1)}, u32[]{:S(2)}, u32[]{:S(2)}) collective-permute-start(f32[72,256]{1,0:T(8,128)} %get-tuple-element.26), channel_id=1, source_target_pairs={{0,128},{4,132},{8,136},{12,140},{16,144},{20,148},{24,152},{28,15... | collective-permute-start | bytes 221192 | tf_op jit(solution)/shard_map/ppermute | solution.py:273
  50.2 3.0 %collective-permute-done.5.other = f32[72,256]{1,0:T(8,128)S(1)} collective-permute-done((f32[72,256]{1,0:T(8,128)}, f32[72,256]{1,0:T(8,128)S(1)}, u32[]{:S(2)}, u32[]{:S(2)}) %collective-permute-start.5) | collective-permute-done | bytes 73760 | tf_op jit(solution)/shard_map/ppermute | solution.py:273
  56.0 11.1 %collective-permute-done.6.other = f32[40,256]{1,0:T(8,128)S(1)} collective-permute-done((f32[40,256]{1,0:T(8,128)}, f32[40,256]{1,0:T(8,128)S(1)}, u32[]{:S(2)}, u32[]{:S(2)}) %collective-permute-start.6) | collective-permute-done | bytes 40992 | tf_op jit(solution)/shard_map/ppermute | solution.py:273
  69.1 2.7 %collective-permute-start.7 = (f32[24,256]{1,0:T(8,128)}, f32[24,256]{1,0:T(8,128)S(1)}, u32[]{:S(2)}, u32[]{:S(2)}) collective-permute-start(f32[24,256]{1,0:T(8,128)} %get-tuple-element.30), channel_id=1, source_target_pairs={{0,2},{1,3},{2,0},{3,1},{4,6},{5,7},{6,4},{7,5},{8,10},{9,11},{10,... | collective-permute-start | bytes 73736 | tf_op jit(solution)/shard_map/ppermute | solution.py:273
  72.5 2.8 %plan_tiles.1 = (s32[8,60]{1,0:T(8,128)}, s32[8,60]{1,0:T(8,128)}) custom-call(s32[1,96]{1,0:T(1,128)} %rows.1, s32[1,96]{1,0:T(1,128)} %cols.1, s32[1]{0:T(128)S(6)} %copy.12.count, bf16[16,128,256]{2,1,0:T(8,128)(2,1)} %get-tuple-element.19.after.refs_0_), custom_call_target="tpu_custom_call" | custom-call | tf_op jit(solution)/shard_map/plan_tiles/pallas_call | solution.py:357
  77.3 5.5 %collective-permute-start.8 = (f32[24,256]{1,0:T(8,128)}, f32[24,256]{1,0:T(8,128)S(1)}, u32[]{:S(2)}, u32[]{:S(2)}) collective-permute-start(f32[24,256]{1,0:T(8,128)} %merge_sums.3.refs_4_.refs_0_), channel_id=1, source_target_pairs={{0,16},{4,36},{8,24},{12,44},{16,32},{20,52},{24,40},{28,60},{32,4... | collective-permute-start | bytes 73736 | tf_op jit(solution)/shard_map/ppermute | solution.py:293
  83.4 3.9 %collective-permute-start.10 = (f32[24,256]{1,0:T(8,128)}, f32[24,256]{1,0:T(8,128)S(1)}, u32[]{:S(2)}, u32[]{:S(2)}) collective-permute-start(f32[24,256]{1,0:T(8,128)} %merge_sums.3.refs_4_.refs_0_), channel_id=1, source_target_pairs={{0,8},{4,44},{8,16},{12,52},{16,24},{20,60},{24,32},{28,4},{32,40}... | collective-permute-start | bytes 73736 | tf_op jit(solution)/shard_map/ppermute | solution.py:293
  88.7 5.0 %local_tiles.2.part = f32[16,128,256]{2,1,0:T(8,128)} custom-call(s32[8,60]{1,0:T(8,128)S(1)} %copy-done.13, bf16[96,128,128]{2,1,0:T(8,128)(2,1)S(1)} %copy-done, bf16[16,128,256]{2,1,0:T(8,128)(2,1)} %get-tuple-element.19.after.refs_0_, bf16[16,128,256]{2,1,0:T(8,128)(2,1)} %collective-permute-done.refs_1_, ...), custom_call_target="tpu_custom_call" | custom-call | flops 402653184 | bytes 9437184 | tf_op jit(solution)/shard_map/local_tiles/pallas_call | solution.py:416
  93.7 19.9 %collective-permute-done.8.refs_0_.refs_1_ = f32[24,256]{1,0:T(8,128)S(1)} collective-permute-done((f32[24,256]{1,0:T(8,128)}, f32[24,256]{1,0:T(8,128)S(1)}, u32[]{:S(2)}, u32[]{:S(2)}) %collective-permute-start.8) | collective-permute-done | bytes 24608 | tf_op jit(solution)/shard_map/ppermute | solution.py:293
  114.1 5.2 %halo_tiles_send.1 = (bf16[16,128,256]{2,1,0:T(8,128)(2,1)}, bf16[64,128,256]{2,1,0:T(8,128)(2,1)}) custom-call(s32[1,64]{1,0:T(1,128)S(1)} %copy-done.15, s32[8,60]{1,0:T(8,128)S(1)} %copy-done.12, bf16[96,128,128]{2,1,0:T(8,128)(2,1)S(1)} %copy-done, bf16[64,128,256]{2,1,0:T(8,128)(2,1)} %all-to-all-done.blocks, f32[16,128,256]{2,1,0:T(8,128)} %local_tiles.2.part, ...), custom_call_target="tpu_custom_call" | custom-call | tf_op jit(solution)/shard_map/halo_tiles_send/pallas_call | solution.py:485
  119.3 8.2 %all-to-all-start.1 = ((bf16[64,128,256]{2,1,0:T(8,128)(2,1)}), bf16[64,128,256]{2,1,0:T(8,128)(2,1)}, u32[]{:S(2)}, u32[]{:S(2)}) async-start(bf16[64,128,256]{2,1,0:T(8,128)(2,1)} %get-tuple-element.31), calls=%async_computation.1 | async-start | bytes 8388608 | tf_op jit(solution)/shard_map/all_to_all | solution.py:597
  129.2 2.8 %collective-permute-start.13 = (bf16[16,128,256]{2,1,0:T(8,128)(2,1)}, bf16[16,128,256]{2,1,0:T(8,128)(2,1)}, u32[]{:S(2)}, u32[]{:S(2)}) collective-permute-start(bf16[16,128,256]{2,1,0:T(8,128)(2,1)} %get-tuple-element.32.refs_0_), channel_id=1, source_target_pairs={{0,2},{1,3},{2,0},{3,1},{4,6},{5,7},{6,4},{7,5},{8,10},{9,11},{10,... | collective-permute-start | bytes 3145736 | tf_op jit(solution)/shard_map/ppermute | solution.py:577
  139.3 2.8 %collective-permute-start.16 = (f32[16,256]{1,0:T(8,128)S(1)}, f32[16,256]{1,0:T(8,128)S(1)}, u32[]{:S(2)}, u32[]{:S(2)}) collective-permute-start(f32[16,256]{1,0:T(8,128)S(1)} %slice.8.mine), channel_id=1, source_target_pairs={{0,128},{4,132},{8,136},{12,140},{16,144},{20,148},{24,152},{28,15... | collective-permute-start | bytes 49160 | tf_op jit(solution)/shard_map/ppermute | solution.py:273
  147.3 2.9 %collective-permute-done.17.other = f32[32,256]{1,0:T(8,128)S(1)} collective-permute-done((f32[32,256]{1,0:T(8,128)}, f32[32,256]{1,0:T(8,128)S(1)}, u32[]{:S(2)}, u32[]{:S(2)}) %collective-permute-start.17) | collective-permute-done | bytes 32800 | tf_op jit(solution)/shard_map/ppermute | solution.py:273
  152.2 26.7 %collective-permute-done.18.other = f32[64,256]{1,0:T(8,128)S(1)} collective-permute-done((f32[64,256]{1,0:T(8,128)}, f32[64,256]{1,0:T(8,128)S(1)}, u32[]{:S(2)}, u32[]{:S(2)}) %collective-permute-start.18) | collective-permute-done | bytes 65568 | tf_op jit(solution)/shard_map/ppermute | solution.py:273
  182.8 2.6 %collective-permute-done.19.other = f32[128,256]{1,0:T(8,128)S(1)} collective-permute-done((f32[128,256]{1,0:T(8,128)}, f32[128,256]{1,0:T(8,128)S(1)}, u32[]{:S(2)}, u32[]{:S(2)}) %collective-permute-start.19) | collective-permute-done | bytes 131104 | tf_op jit(solution)/shard_map/ppermute | solution.py:273
  192.4 5.8 %attention.1 = f32[2048,256]{1,0:T(8,128)} custom-call(bf16[2048,256]{1,0:T(8,128)(2,1)S(1)} %copy-done.4, bf16[256,256]{1,0:T(8,128)(2,1)S(1)} %copy-done.19, bf16[256,256]{1,0:T(8,128)(2,1)S(1)} %copy-done.21, f32[256,256]{1,0:T(8,128)S(1)} %copy-done.7, f32[8,256]{1,0:T(8,128)S(1)} %slice.9.extra, bf16[2048,256]{1,0:T(8,128)(2,1)S(1)} %bitcast.5, ...), custom_call_target="tpu_custom_call" | custom-call | flops 2415919104 | bytes 6291456 | tf_op jit(solution)/shard_map/attention/pallas_call | solution.py:523
  198.2 5.8 %local_tiles.3.base = f32[16,128,256]{2,1,0:T(8,128)} custom-call(s32[8,60]{1,0:T(8,128)S(1)} %copy-done.14, bf16[96,128,128]{2,1,0:T(8,128)(2,1)S(1)} %copy-done, bf16[16,128,256]{2,1,0:T(8,128)(2,1)} %get-tuple-element.32.refs_0_, bf16[16,128,256]{2,1,0:T(8,128)(2,1)} %collective-permute-done.12.refs_1_, ...), custom_call_target="tpu_custom_call" | custom-call | flops 402653184 | bytes 9437184 | tf_op jit(solution)/shard_map/local_tiles/pallas_call | solution.py:416
  204.1 19.3 %all-to-all-done.1.blocks = bf16[64,128,256]{2,1,0:T(8,128)(2,1)} async-done(((bf16[64,128,256]{2,1,0:T(8,128)(2,1)}), bf16[64,128,256]{2,1,0:T(8,128)(2,1)}, u32[]{:S(2)}, u32[]{:S(2)}) %all-to-all-start.1) | async-done | bytes 4194336 | tf_op jit(solution)/shard_map/all_to_all | solution.py:597
  223.4 4.5 %halo_tiles_norm.1 = bf16[16,128,256]{2,1,0:T(8,128)(2,1)} custom-call(s32[8,60]{1,0:T(8,128)S(1)} %copy-done.12, bf16[96,128,128]{2,1,0:T(8,128)(2,1)S(1)} %copy-done, bf16[64,128,256]{2,1,0:T(8,128)(2,1)} %all-to-all-done.1.blocks, f32[16,128,256]{2,1,0:T(8,128)} %local_tiles.3.base, f32[1,256]{1,0:T(1,128)S(1)} %bitcast.7), custom_call_target="tpu_custom_call" | custom-call | tf_op jit(solution)/shard_map/halo_tiles_norm/pallas_call | solution.py:561
  (105 shorter events, 53.8 us)
Async XLA Ops:
  4.1 110.0 %all-to-all-start = ((bf16[64,128,256]{2,1,0:T(8,128)(2,1)}), bf16[64,128,256]{2,1,0:T(8,128)(2,1)}, u32[]{:S(2)}, u32[]{:S(2)}) async-start(bf16[64,128,256]{2,1,0:T(8,128)(2,1)} %get-tuple-element.21), calls=%async_computation | async-start | bytes 8388608 | tf_op jit(solution)/shard_map/all_to_all | solution.py:590
  17.4 70.6 %copy-start = (bf16[96,128,128]{2,1,0:T(8,128)(2,1)S(1)}, bf16[96,128,128]{2,1,0:T(8,128)(2,1)}, u32[]{:S(2)}) copy-start(bf16[96,128,128]{2,1,0:T(8,128)(2,1)} %tiles.7) | copy-start | bytes 9437188
  17.4 66.1 %collective-permute-start = (bf16[16,128,256]{2,1,0:T(8,128)(2,1)}, bf16[16,128,256]{2,1,0:T(8,128)(2,1)}, u32[]{:S(2)}, u32[]{:S(2)}) collective-permute-start(bf16[16,128,256]{2,1,0:T(8,128)(2,1)} %get-tuple-element.19.after.refs_0_), channel_id=1, source_target_pairs={{0,1},{1,2},{2,3},{3,0},{4,5},{5,6},{6,7},{7,4},{8,9},{9,10},{10,1... | collective-permute-start | bytes 3145736 | tf_op jit(solution)/shard_map/ppermute | solution.py:577
  18.9 68.5 %collective-permute-start.1 = (bf16[16,128,256]{2,1,0:T(8,128)(2,1)}, bf16[16,128,256]{2,1,0:T(8,128)(2,1)}, u32[]{:S(2)}, u32[]{:S(2)}) collective-permute-start(bf16[16,128,256]{2,1,0:T(8,128)(2,1)} %get-tuple-element.19.after.refs_0_), channel_id=1, source_target_pairs={{0,2},{1,3},{2,0},{3,1},{4,6},{5,7},{6,4},{7,5},{8,10},{9,11},{10,... | collective-permute-start | bytes 3145736 | tf_op jit(solution)/shard_map/ppermute | solution.py:577
  21.3 66.7 %collective-permute-start.2 = (bf16[16,128,256]{2,1,0:T(8,128)(2,1)}, bf16[16,128,256]{2,1,0:T(8,128)(2,1)}, u32[]{:S(2)}, u32[]{:S(2)}) collective-permute-start(bf16[16,128,256]{2,1,0:T(8,128)(2,1)} %get-tuple-element.19.after.refs_0_), channel_id=1, source_target_pairs={{0,3},{1,0},{2,1},{3,2},{4,7},{5,4},{6,5},{7,6},{8,11},{9,8},{10,9... | collective-permute-start | bytes 3145736 | tf_op jit(solution)/shard_map/ppermute | solution.py:577
  32.6 2.8 %collective-permute-start.3 = (f32[264,256]{1,0:T(8,128)S(1)}, f32[264,256]{1,0:T(8,128)}, u32[]{:S(2)}, u32[]{:S(2)}) collective-permute-start(f32[264,256]{1,0:T(8,128)S(1)} %attention_sums.1.mine), channel_id=1, source_target_pairs={{0,4},{4,0},{8,12},{12,8},{16,20},{20,16},{24,28},{28,24},{32,36},... | collective-permute-start | bytes 811016 | tf_op jit(solution)/shard_map/ppermute | solution.py:273
  37.2 7.9 %collective-permute-start.4 = (f32[136,256]{1,0:T(8,128)}, f32[136,256]{1,0:T(8,128)S(1)}, u32[]{:S(2)}, u32[]{:S(2)}) collective-permute-start(f32[136,256]{1,0:T(8,128)} %get-tuple-element.24), channel_id=1, source_target_pairs={{0,64},{4,68},{8,72},{12,76},{16,80},{20,84},{24,88},{28,92},{32,9... | collective-permute-start | bytes 417800 | tf_op jit(solution)/shard_map/ppermute | solution.py:273
  47.4 5.9 %collective-permute-start.5 = (f32[72,256]{1,0:T(8,128)}, f32[72,256]{1,0:T(8,128)S(1)}, u32[]{:S(2)}, u32[]{:S(2)}) collective-permute-start(f32[72,256]{1,0:T(8,128)} %get-tuple-element.26), channel_id=1, source_target_pairs={{0,128},{4,132},{8,136},{12,140},{16,144},{20,148},{24,152},{28,15... | collective-permute-start | bytes 221192 | tf_op jit(solution)/shard_map/ppermute | solution.py:273
  55.5 11.6 %collective-permute-start.6 = (f32[40,256]{1,0:T(8,128)}, f32[40,256]{1,0:T(8,128)S(1)}, u32[]{:S(2)}, u32[]{:S(2)}) collective-permute-start(f32[40,256]{1,0:T(8,128)} %get-tuple-element.28), channel_id=1, source_target_pairs={{0,1},{1,0},{2,3},{3,2},{4,5},{5,4},{6,7},{7,6},{8,9},{9,8},{10,11... | collective-permute-start | bytes 122888 | tf_op jit(solution)/shard_map/ppermute | solution.py:273
  69.1 6.2 %collective-permute-start.7 = (f32[24,256]{1,0:T(8,128)}, f32[24,256]{1,0:T(8,128)S(1)}, u32[]{:S(2)}, u32[]{:S(2)}) collective-permute-start(f32[24,256]{1,0:T(8,128)} %get-tuple-element.30), channel_id=1, source_target_pairs={{0,2},{1,3},{2,0},{3,1},{4,6},{5,7},{6,4},{7,5},{8,10},{9,11},{10,... | collective-permute-start | bytes 73736 | tf_op jit(solution)/shard_map/ppermute | solution.py:273
  77.3 36.3 %collective-permute-start.8 = (f32[24,256]{1,0:T(8,128)}, f32[24,256]{1,0:T(8,128)S(1)}, u32[]{:S(2)}, u32[]{:S(2)}) collective-permute-start(f32[24,256]{1,0:T(8,128)} %merge_sums.3.refs_4_.refs_0_), channel_id=1, source_target_pairs={{0,16},{4,36},{8,24},{12,44},{16,32},{20,52},{24,40},{28,60},{32,4... | collective-permute-start | bytes 73736 | tf_op jit(solution)/shard_map/ppermute | solution.py:293
  82.9 30.8 %collective-permute-start.9 = (f32[24,256]{1,0:T(8,128)}, f32[24,256]{1,0:T(8,128)S(1)}, u32[]{:S(2)}, u32[]{:S(2)}) collective-permute-start(f32[24,256]{1,0:T(8,128)} %merge_sums.3.refs_4_.refs_0_), channel_id=1, source_target_pairs={{0,48},{4,28},{8,56},{12,36},{16,0},{20,44},{24,8},{28,52},{32,16}... | collective-permute-start | bytes 73736 | tf_op jit(solution)/shard_map/ppermute | solution.py:293
  83.4 30.2 %collective-permute-start.10 = (f32[24,256]{1,0:T(8,128)}, f32[24,256]{1,0:T(8,128)S(1)}, u32[]{:S(2)}, u32[]{:S(2)}) collective-permute-start(f32[24,256]{1,0:T(8,128)} %merge_sums.3.refs_4_.refs_0_), channel_id=1, source_target_pairs={{0,8},{4,44},{8,16},{12,52},{16,24},{20,60},{24,32},{28,4},{32,40}... | collective-permute-start | bytes 73736 | tf_op jit(solution)/shard_map/ppermute | solution.py:293
  87.3 26.3 %collective-permute-start.11 = (f32[24,256]{1,0:T(8,128)}, f32[24,256]{1,0:T(8,128)S(1)}, u32[]{:S(2)}, u32[]{:S(2)}) collective-permute-start(f32[24,256]{1,0:T(8,128)} %merge_sums.3.refs_4_.refs_0_), channel_id=1, source_target_pairs={{0,56},{8,0},{16,8},{24,16},{32,24},{40,32},{48,40},{56,48},{64,12... | collective-permute-start | bytes 73736 | tf_op jit(solution)/shard_map/ppermute | solution.py:293
  119.3 68.5 %copy-start.19 = (bf16[256,256]{1,0:T(8,128)(2,1)S(1)}, bf16[256,256]{1,0:T(8,128)(2,1)}, u32[]{:S(2)}) copy-start(bf16[256,256]{1,0:T(8,128)(2,1)} %qw.3) | copy-start | bytes 393220
  119.3 104.1 %all-to-all-start.1 = ((bf16[64,128,256]{2,1,0:T(8,128)(2,1)}), bf16[64,128,256]{2,1,0:T(8,128)(2,1)}, u32[]{:S(2)}, u32[]{:S(2)}) async-start(bf16[64,128,256]{2,1,0:T(8,128)(2,1)} %get-tuple-element.31), calls=%async_computation.1 | async-start | bytes 8388608 | tf_op jit(solution)/shard_map/all_to_all | solution.py:597
  127.5 70.7 %collective-permute-start.12 = (bf16[16,128,256]{2,1,0:T(8,128)(2,1)}, bf16[16,128,256]{2,1,0:T(8,128)(2,1)}, u32[]{:S(2)}, u32[]{:S(2)}) collective-permute-start(bf16[16,128,256]{2,1,0:T(8,128)(2,1)} %get-tuple-element.32.refs_0_), channel_id=1, source_target_pairs={{0,1},{1,2},{2,3},{3,0},{4,5},{5,6},{6,7},{7,4},{8,9},{9,10},{10,1... | collective-permute-start | bytes 3145736 | tf_op jit(solution)/shard_map/ppermute | solution.py:577
  129.2 69.0 %collective-permute-start.13 = (bf16[16,128,256]{2,1,0:T(8,128)(2,1)}, bf16[16,128,256]{2,1,0:T(8,128)(2,1)}, u32[]{:S(2)}, u32[]{:S(2)}) collective-permute-start(bf16[16,128,256]{2,1,0:T(8,128)(2,1)} %get-tuple-element.32.refs_0_), channel_id=1, source_target_pairs={{0,2},{1,3},{2,0},{3,1},{4,6},{5,7},{6,4},{7,5},{8,10},{9,11},{10,... | collective-permute-start | bytes 3145736 | tf_op jit(solution)/shard_map/ppermute | solution.py:577
  131.9 66.3 %collective-permute-start.14 = (bf16[16,128,256]{2,1,0:T(8,128)(2,1)}, bf16[16,128,256]{2,1,0:T(8,128)(2,1)}, u32[]{:S(2)}, u32[]{:S(2)}) collective-permute-start(bf16[16,128,256]{2,1,0:T(8,128)(2,1)} %get-tuple-element.32.refs_0_), channel_id=1, source_target_pairs={{0,3},{1,0},{2,1},{3,2},{4,7},{5,4},{6,5},{7,6},{8,11},{9,8},{10,9... | collective-permute-start | bytes 3145736 | tf_op jit(solution)/shard_map/ppermute | solution.py:577
  134.2 2.4 %collective-permute-start.15 = (f32[24,256]{1,0:T(8,128)}, f32[24,256]{1,0:T(8,128)S(1)}, u32[]{:S(2)}, u32[]{:S(2)}) collective-permute-start(f32[24,256]{1,0:T(8,128)} %merge_sums.4.refs_0_), channel_id=1, source_target_pairs={{0,4},{4,0},{8,12},{12,8},{16,20},{20,16},{24,28},{28,24},{32,36},... | collective-permute-start | bytes 73736 | tf_op jit(solution)/shard_map/ppermute | solution.py:273
  139.3 5.0 %collective-permute-start.16 = (f32[16,256]{1,0:T(8,128)S(1)}, f32[16,256]{1,0:T(8,128)S(1)}, u32[]{:S(2)}, u32[]{:S(2)}) collective-permute-start(f32[16,256]{1,0:T(8,128)S(1)} %slice.8.mine), channel_id=1, source_target_pairs={{0,128},{4,132},{8,136},{12,140},{16,144},{20,148},{24,152},{28,15... | collective-permute-start | bytes 49160 | tf_op jit(solution)/shard_map/ppermute | solution.py:273
  146.2 3.9 %collective-permute-start.17 = (f32[32,256]{1,0:T(8,128)}, f32[32,256]{1,0:T(8,128)S(1)}, u32[]{:S(2)}, u32[]{:S(2)}) collective-permute-start(f32[32,256]{1,0:T(8,128)} %join_sums.4.mine), channel_id=1, source_target_pairs={{0,64},{4,68},{8,72},{12,76},{16,80},{20,84},{24,88},{28,92},{32,9... | collective-permute-start | bytes 98312 | tf_op jit(solution)/shard_map/ppermute | solution.py:273
  152.1 26.7 %collective-permute-start.18 = (f32[64,256]{1,0:T(8,128)}, f32[64,256]{1,0:T(8,128)S(1)}, u32[]{:S(2)}, u32[]{:S(2)}) collective-permute-start(f32[64,256]{1,0:T(8,128)} %join_sums.5.mine), channel_id=1, source_target_pairs={{0,2},{1,3},{2,0},{3,1},{4,6},{5,7},{6,4},{7,5},{8,10},{9,11},{10,... | collective-permute-start | bytes 196616 | tf_op jit(solution)/shard_map/ppermute | solution.py:273
  181.0 4.4 %collective-permute-start.19 = (f32[128,256]{1,0:T(8,128)}, f32[128,256]{1,0:T(8,128)S(1)}, u32[]{:S(2)}, u32[]{:S(2)}) collective-permute-start(f32[128,256]{1,0:T(8,128)} %join_sums.6.mine), channel_id=1, source_target_pairs={{0,1},{1,0},{2,3},{3,2},{4,5},{5,4},{6,7},{7,6},{8,9},{9,8},{10,11... | collective-permute-start | bytes 393224 | tf_op jit(solution)/shard_map/ppermute | solution.py:273
  (30 other events, 214.1 us)

commit v5 on v4

--- a/solution.py
+++ b/solution.py
@@ -66,7 +66,8 @@
 
 
 def send_block(b, src, heads, nexts, h_out, out, sems):
-    pltpu.make_async_copy(src.at[b], h_out.at[b], sems.at[0]).start()
+    if h_out is not None:
+        pltpu.make_async_copy(src.at[b], h_out.at[b], sems.at[0]).start()
 
     def one(w):
         pltpu.make_async_copy(src.at[b], out.at[w], sems.at[1]).start()
@@ -76,7 +77,8 @@
 
 
 def wait_sent(src, h_out, out, sems):
-    pltpu.make_async_copy(src, h_out, sems.at[0]).wait()
+    if h_out is not None:
+        pltpu.make_async_copy(src, h_out, sems.at[0]).wait()
     pltpu.make_async_copy(out, out, sems.at[1]).wait()
 
 
@@ -90,7 +92,7 @@
     ]
 
 
-def start_kernel(send, x, weight, h_out, out, h_own, zeros, heads, nexts, sems, send_own, x_own, weight_own, loads):
+def start_kernel(send, x, weight, out, h_own, zeros, heads, nexts, sems, send_own, x_own, weight_own, loads):
     pieces = loads.shape[0] - 2
     rows = x.shape[0] // pieces
     per = rows // BLOCK
@@ -114,8 +116,8 @@
                 x_own[b * BLOCK:(b + 1) * BLOCK, :], weight_own[...], preferred_element_type=F32
             ).astype(BF16)
         for b in range(p * per, (p + 1) * per):
-            send_block(b, h_own, heads, nexts, h_out, out, sems)
-    wait_sent(h_own, h_out, out, sems)
+            send_block(b, h_own, heads, nexts, None, out, sems)
+    wait_sent(h_own, None, out, sems)
 
 
 def start(send, x, weight, peers):
@@ -123,9 +125,9 @@
     pieces = 4
     return pl.pallas_call(
         start_kernel,
-        out_shape=(pltpu.HBM((nblocks, BLOCK, D), BF16), pltpu.HBM((peers, BLOCK, D), BF16)),
+        out_shape=pltpu.HBM((peers, BLOCK, D), BF16),
         in_specs=[HBM] * 3,
-        out_specs=(HBM, HBM),
+        out_specs=HBM,
         scratch_shapes=send_scratch(nblocks, peers) + [
             pltpu.SMEM(send.shape, jnp.int32),
             pltpu.VMEM(x.shape, BF16),
@@ -135,6 +137,26 @@
         compiler_params=params(16),
         name="project_send",
     )(in_hbm(send), in_hbm(x), in_hbm(weight))
+
+
+def own_kernel(x, weight, after, out):
+    def one(b, _):
+        rows = pl.ds(pl.multiple_of(b * BLOCK, BLOCK), BLOCK)
+        out[b] = jnp.dot(x[rows, :], weight[...], preferred_element_type=F32).astype(BF16)
+        return 0
+
+    lax.fori_loop(0, out.shape[0], one, 0)
+
+
+def own_blocks(x, weight, after):
+    return pl.pallas_call(
+        own_kernel,
+        out_shape=pltpu.HBM((x.shape[0] // BLOCK, BLOCK, D), BF16),
+        in_specs=[VMEM, VMEM, HBM],
+        out_specs=VMEM,
+        compiler_params=params(16),
+        name="project_own",
+    )(x, weight, after)
 
 
 def stats_kernel(x, qw, kw, vw, after, out, keys_sq, values, sums):
@@ -456,27 +478,41 @@
         pltpu.VMEM((steps.shape[1], 2 * BLOCK, D), BF16),
         pltpu.VMEM((nblocks + 1, BLOCK, D), F32),
         pltpu.VMEM(part.shape, F32),
-        pltpu.SemaphoreType.DMA((steps.shape[1] // PAIRS + 1,)),
+        pltpu.SemaphoreType.DMA((steps.shape[1] // PAIRS + nblocks // NORM,)),
     ]
+
+
+def pieces_of(source, target, sems):
+    count = source.shape[0] // NORM
+
+    def piece(i):
+        at = pl.ds(i * NORM, NORM)
+        return pltpu.make_async_copy(source.at[at], target.at[at], sems.at[sems.shape[0] - count + i])
+
+    return piece, count
 
 
 def hop_kernel(send, steps, tiles, blocks, part, *refs):
     h_out, out, got, acc, local, loads, h_own, zeros, heads, nexts, sems = refs[len(AROUND):]
     nblocks = h_own.shape[0]
     load_halo(steps, blocks, got, loads)
-    load = pltpu.make_async_copy(part, local, loads.at[loads.shape[0] - 1])
-    load.start()
+    piece, count = pieces_of(part, local, loads)
+    for i in range(count):
+        piece(i).start()
     send_order(send, heads, nexts, zeros, out, sems.at[1])
     acc[...] = jnp.zeros_like(acc)
     add_halo(steps, tiles, got, acc, loads)
-    load.wait()
-
-    def one(b, _):
-        h_own[b] = (acc[b] + local[b]).astype(BF16)
-        send_block(b, h_own, heads, nexts, h_out, out, sems)
-        return 0
-
-    lax.fori_loop(0, nblocks, one, 0)
+
+    def some(i, _):
+        piece(i).wait()
+        for u in range(NORM):
+            b = i * NORM + u
+            h_own[b] = (acc[b] + local[b]).astype(BF16)
+        for u in range(NORM):
+            send_block(i * NORM + u, h_own, heads, nexts, h_out, out, sems)
+        return 0
+
+    lax.fori_loop(0, count, some, 0)
     wait_sent(h_own, h_out, out, sems)
 
 
@@ -535,13 +571,14 @@
 def finish_kernel(steps, tiles, blocks, base, gain, out, got, acc, mixing, loads, done, sem):
     nblocks = base.shape[0]
     load_halo(steps, blocks, got, loads)
-    load = pltpu.make_async_copy(base, mixing, loads.at[loads.shape[0] - 1])
-    load.start()
+    piece, count = pieces_of(base, mixing, loads)
+    for i in range(count):
+        piece(i).start()
     acc[...] = jnp.zeros_like(acc)
     add_halo(steps, tiles, got, acc, loads)
-    load.wait()
 
     def some(i, _):
+        piece(i).wait()
         for u in range(NORM):
             b = i * NORM + u
             mixed = mixing[b] + acc[b] / 3.0
@@ -552,7 +589,7 @@
         pltpu.make_async_copy(done.at[at], out.at[at], sem).start()
         return 0
 
-    lax.fori_loop(0, nblocks // NORM, some, 0)
+    lax.fori_loop(0, count, some, 0)
     pltpu.make_async_copy(done, out, sem).wait()
 
 
@@ -586,7 +623,8 @@
     total = float(rows_dev * peers * groups)
     first = groups * nblocks
 
-    hop_zero, outgoing = start(send_list, x, gw, peers)
+    outgoing = start(send_list, x, gw, peers)
+    hop_zero = own_blocks(x, gw, outgoing)
     received = lax.all_to_all(outgoing, "wide", 0, 0, tiled=True)
     group = group_blocks(hop_zero)
     mine = partial_sums(stats(x, qw, kw, vw, hop_zero))

time: 230 us -> 230 us (level)
  waiting for transfers between devices: 97.1 us -> 92.6 us
  Pallas kernels: 55.6 us -> 59.8 us
    ppermute x4, waiting for transfers between devices: 19.9 us -> 14 us  [along_depth(): return [lax.ppermute(mine, 'wide', shift(by)) for by in AROUND]]
    pallas_call x1 -> x2, Pallas kernels: 4.05 us -> 7.7 us  [the longest x1 4.04 us: start(): pl.pallas_call(start_kernel, out_shape=pltpu.HBM((peers, BLOCK, D), BF16)...]
    unnamed x64 -> x68, local copies, waits for them, and re-layouts: 15.2 us -> 14.4 us
  transfers between devices with their start and end apart: 22 -> 22, of which waited for: 12 -> 12; matrix products, arithmetic and copies ran while one was open for 1% -> 1% of each run, Pallas kernels for 18% -> 20%
where the time goes in v5:
time: 230 us; the launch traced here: 228 us
  waiting for transfers between devices  92.6 us (40%)
  Pallas kernels  59.8 us (26%)
  starting transfers between devices  58.7 us (26%)
  local copies, waits for them, and re-layouts  15.8 us (7%)
    ppermute x10, waiting for transfers between devices, swap(): lax.ppermute(x, axis, [(i, i ^ 1 << bit) for i in range(lax.axis_size(axi...  59.3 us
    all_to_all x2, starting transfers between devices, shards(): received = lax.all_to_all(outgoing, 'wide', 0, 0, tiled=True)  21 us
    all_to_all x2, waiting for transfers between devices, shards(): received = lax.all_to_all(outgoing, 'wide', 0, 0, tiled=True)  19.2 us
    ppermute x10, starting transfers between devices, swap(): lax.ppermute(x, axis, [(i, i ^ 1 << bit) for i in range(lax.axis_size(axi...  16.3 us
    unnamed x68, local copies, waits for them, and re-layouts  14.4 us
    ppermute x4, waiting for transfers between devices, along_depth(): return [lax.ppermute(mine, 'wide', shift(by)) for by in AROUND]  14 us
    ppermute x6, starting transfers between devices, group_blocks(): lax.ppermute(own, 'narrow', [(i, (i + by) % groups) for i in range(groups)])  10.9 us
    pallas_call x2, Pallas kernels, local_tiles(): pl.pallas_call(functools.partial(local_kernel, len(parts)), out_shape=plt...  10.8 us
  transfers between devices with their start and end apart: 22, of which 12 were waited for; matrix products, arithmetic and copies ran while one was open for 1% of the time, Pallas kernels for 20%

profile of v5, /device:TPU:1, one launch (start us, length us, event | category | flops | bytes accessed | tf_op | source)
XLA Modules:
  0.0 228.0 jit_solution(1149804703399415392)
XLA Ops:
  0.0 4.0 %project_send.1.after = bf16[64,128,256]{2,1,0:T(8,128)(2,1)} custom-call(s32[1,64]{1,0:T(1,128)} %send.3, bf16[2048,256]{1,0:T(8,128)(2,1)} %x.7, bf16[256,256]{1,0:T(8,128)(2,1)} %weight.3), custom_call_target="tpu_custom_call" | custom-call | tf_op jit(solution)/shard_map/project_send/pallas_call | solution.py:126
  4.1 13.2 %all-to-all-start = ((bf16[64,128,256]{2,1,0:T(8,128)(2,1)}), bf16[64,128,256]{2,1,0:T(8,128)(2,1)}, u32[]{:S(2)}, u32[]{:S(2)}) async-start(bf16[64,128,256]{2,1,0:T(8,128)(2,1)} %project_send.1.after), calls=%async_computation | async-start | bytes 8388608 | tf_op jit(solution)/shard_map/all_to_all | solution.py:628
  19.5 3.7 %project_own.1.after.refs_0_ = bf16[16,128,256]{2,1,0:T(8,128)(2,1)} custom-call(bf16[2048,256]{1,0:T(8,128)(2,1)S(1)} %copy-done.4, bf16[256,256]{1,0:T(8,128)(2,1)S(1)} %copy-done.8, bf16[64,128,256]{2,1,0:T(8,128)(2,1)S(1)} %copy-done.1), custom_call_target="tpu_custom_call" | custom-call | tf_op jit(solution)/shard_map/project_own/pallas_call | solution.py:152
  24.6 2.7 %collective-permute-start.1 = (bf16[16,128,256]{2,1,0:T(8,128)(2,1)}, bf16[16,128,256]{2,1,0:T(8,128)(2,1)}, u32[]{:S(2)}, u32[]{:S(2)}) collective-permute-start(bf16[16,128,256]{2,1,0:T(8,128)(2,1)} %project_own.1.after.refs_0_), channel_id=1, source_target_pairs={{0,2},{1,3},{2,0},{3,1},{4,6},{5,7},{6,4},{7,5},{8,10},{9,11},{10,... | collective-permute-start | bytes 3145736 | tf_op jit(solution)/shard_map/ppermute | solution.py:614
  29.6 5.8 %attention_sums.1.mine = f32[264,256]{1,0:T(8,128)S(1)} custom-call(bf16[2048,256]{1,0:T(8,128)(2,1)S(1)} %copy-done.5, bf16[256,256]{1,0:T(8,128)(2,1)S(1)} %copy-done.21, bf16[256,256]{1,0:T(8,128)(2,1)S(1)} %copy-done.20, bf16[256,256]{1,0:T(8,128)(2,1)S(1)} %copy-done.22, bf16[16,128,256]{2,1,0:T(8,128)(2,1)S(1)} %copy-done.2), custom_call_target="tpu_custom_call" | custom-call | flops 2415919104 | bytes 2097152 | tf_op jit(solution)/shard_map/attention_sums/pallas_call | solution.py:214
  41.2 5.2 %collective-permute-done.4.other = f32[136,256]{1,0:T(8,128)S(1)} collective-permute-done((f32[136,256]{1,0:T(8,128)}, f32[136,256]{1,0:T(8,128)S(1)}, u32[]{:S(2)}, u32[]{:S(2)}) %collective-permute-start.4) | collective-permute-done | bytes 139296 | tf_op jit(solution)/shard_map/ppermute | solution.py:295
  48.7 2.8 %collective-permute-start.5 = (f32[72,256]{1,0:T(8,128)}, f32[72,256]{1,0:T(8,128)S(1)}, u32[]{:S(2)}, u32[]{:S(2)}) collective-permute-start(f32[72,256]{1,0:T(8,128)} %get-tuple-element.22), channel_id=1, source_target_pairs={{0,128},{4,132},{8,136},{12,140},{16,144},{20,148},{24,152},{28,15... | collective-permute-start | bytes 221192 | tf_op jit(solution)/shard_map/ppermute | solution.py:295
  51.6 2.9 %collective-permute-done.5.other = f32[72,256]{1,0:T(8,128)S(1)} collective-permute-done((f32[72,256]{1,0:T(8,128)}, f32[72,256]{1,0:T(8,128)S(1)}, u32[]{:S(2)}, u32[]{:S(2)}) %collective-permute-start.5) | collective-permute-done | bytes 73760 | tf_op jit(solution)/shard_map/ppermute | solution.py:295
  57.7 15.2 %collective-permute-done.6.other = f32[40,256]{1,0:T(8,128)S(1)} collective-permute-done((f32[40,256]{1,0:T(8,128)}, f32[40,256]{1,0:T(8,128)S(1)}, u32[]{:S(2)}, u32[]{:S(2)}) %collective-permute-start.6) | collective-permute-done | bytes 40992 | tf_op jit(solution)/shard_map/ppermute | solution.py:295
  75.0 2.7 %collective-permute-start.7 = (f32[24,256]{1,0:T(8,128)}, f32[24,256]{1,0:T(8,128)S(1)}, u32[]{:S(2)}, u32[]{:S(2)}) collective-permute-start(f32[24,256]{1,0:T(8,128)} %get-tuple-element.26), channel_id=1, source_target_pairs={{0,2},{1,3},{2,0},{3,1},{4,6},{5,7},{6,4},{7,5},{8,10},{9,11},{10,... | collective-permute-start | bytes 73736 | tf_op jit(solution)/shard_map/ppermute | solution.py:295
  78.4 2.9 %plan_tiles.1 = (s32[8,60]{1,0:T(8,128)}, s32[8,60]{1,0:T(8,128)}) custom-call(s32[1,96]{1,0:T(1,128)} %rows.1, s32[1,96]{1,0:T(1,128)} %cols.1, s32[1]{0:T(128)S(6)} %copy.12.count, bf16[16,128,256]{2,1,0:T(8,128)(2,1)} %project_own.1.after.refs_0_), custom_call_target="tpu_custom_call" | custom-call | tf_op jit(solution)/shard_map/plan_tiles/pallas_call | solution.py:379
  83.2 5.5 %collective-permute-start.8 = (f32[24,256]{1,0:T(8,128)}, f32[24,256]{1,0:T(8,128)S(1)}, u32[]{:S(2)}, u32[]{:S(2)}) collective-permute-start(f32[24,256]{1,0:T(8,128)} %merge_sums.3.refs_4_.refs_0_), channel_id=1, source_target_pairs={{0,16},{4,36},{8,24},{12,44},{16,32},{20,52},{24,40},{28,60},{32,4... | collective-permute-start | bytes 73736 | tf_op jit(solution)/shard_map/ppermute | solution.py:315
  94.6 5.0 %local_tiles.2.part = f32[16,128,256]{2,1,0:T(8,128)} custom-call(s32[8,60]{1,0:T(8,128)S(1)} %copy-done.16, bf16[96,128,128]{2,1,0:T(8,128)(2,1)S(1)} %copy-done, bf16[16,128,256]{2,1,0:T(8,128)(2,1)} %project_own.1.after.refs_0_, bf16[16,128,256]{2,1,0:T(8,128)(2,1)} %collective-permute-done.refs_1_, bf16[16,128,256]{2,1,0:T(8,128)(2,1)} %collective-permute-done.1.refs_2_, ...), custom_call_target="tpu_custom_call" | custom-call | flops 402653184 | bytes 9437184 | tf_op jit(solution)/shard_map/local_tiles/pallas_call | solution.py:438
  99.6 14.0 %collective-permute-done.8.refs_0_.refs_1_ = f32[24,256]{1,0:T(8,128)S(1)} collective-permute-done((f32[24,256]{1,0:T(8,128)}, f32[24,256]{1,0:T(8,128)S(1)}, u32[]{:S(2)}, u32[]{:S(2)}) %collective-permute-start.8) | collective-permute-done | bytes 24608 | tf_op jit(solution)/shard_map/ppermute | solution.py:315
  114.0 5.4 %halo_tiles_send.1 = (bf16[16,128,256]{2,1,0:T(8,128)(2,1)}, bf16[64,128,256]{2,1,0:T(8,128)(2,1)}) custom-call(s32[1,64]{1,0:T(1,128)S(1)} %copy-done.18, s32[8,60]{1,0:T(8,128)S(1)} %copy-done.15, bf16[96,128,128]{2,1,0:T(8,128)(2,1)S(1)} %copy-done, bf16[64,128,256]{2,1,0:T(8,128)(2,1)} %all-to-all-done.blocks, f32[16,128,256]{2,1,0:T(8,128)} %local_tiles.2.part, ...), custom_call_target="tpu_custom_call" | custom-call | tf_op jit(solution)/shard_map/halo_tiles_send/pallas_call | solution.py:521
  119.5 7.8 %all-to-all-start.1 = ((bf16[64,128,256]{2,1,0:T(8,128)(2,1)}), bf16[64,128,256]{2,1,0:T(8,128)(2,1)}, u32[]{:S(2)}, u32[]{:S(2)}) async-start(bf16[64,128,256]{2,1,0:T(8,128)(2,1)} %get-tuple-element.27), calls=%async_computation.1 | async-start | bytes 8388608 | tf_op jit(solution)/shard_map/all_to_all | solution.py:635
  128.9 3.3 %collective-permute-start.13 = (bf16[16,128,256]{2,1,0:T(8,128)(2,1)}, bf16[16,128,256]{2,1,0:T(8,128)(2,1)}, u32[]{:S(2)}, u32[]{:S(2)}) collective-permute-start(bf16[16,128,256]{2,1,0:T(8,128)(2,1)} %get-tuple-element.28.refs_0_), channel_id=1, source_target_pairs={{0,2},{1,3},{2,0},{3,1},{4,6},{5,7},{6,4},{7,5},{8,10},{9,11},{10,... | collective-permute-start | bytes 3145736 | tf_op jit(solution)/shard_map/ppermute | solution.py:614
  139.6 2.8 %collective-permute-start.16 = (f32[16,256]{1,0:T(8,128)S(1)}, f32[16,256]{1,0:T(8,128)S(1)}, u32[]{:S(2)}, u32[]{:S(2)}) collective-permute-start(f32[16,256]{1,0:T(8,128)S(1)} %slice.8.mine), channel_id=1, source_target_pairs={{0,128},{4,132},{8,136},{12,140},{16,144},{20,148},{24,152},{28,15... | collective-permute-start | bytes 49160 | tf_op jit(solution)/shard_map/ppermute | solution.py:295
  152.2 26.9 %collective-permute-done.18.other = f32[64,256]{1,0:T(8,128)S(1)} collective-permute-done((f32[64,256]{1,0:T(8,128)}, f32[64,256]{1,0:T(8,128)S(1)}, u32[]{:S(2)}, u32[]{:S(2)}) %collective-permute-start.18) | collective-permute-done | bytes 65568 | tf_op jit(solution)/shard_map/ppermute | solution.py:295
  183.2 2.5 %collective-permute-done.19.other = f32[128,256]{1,0:T(8,128)S(1)} collective-permute-done((f32[128,256]{1,0:T(8,128)}, f32[128,256]{1,0:T(8,128)S(1)}, u32[]{:S(2)}, u32[]{:S(2)}) %collective-permute-start.19) | collective-permute-done | bytes 131104 | tf_op jit(solution)/shard_map/ppermute | solution.py:295
  192.7 5.8 %attention.1 = f32[2048,256]{1,0:T(8,128)} custom-call(bf16[2048,256]{1,0:T(8,128)(2,1)S(1)} %copy-done.6, bf16[256,256]{1,0:T(8,128)(2,1)S(1)} %copy-done.21, bf16[256,256]{1,0:T(8,128)(2,1)S(1)} %copy-done.23, f32[256,256]{1,0:T(8,128)S(1)} %copy-done.10, f32[8,256]{1,0:T(8,128)S(1)} %slice.9.extra, bf16[2048,256]{1,0:T(8,128)(2,1)S(1)} %bitcast.5, ...), custom_call_target="tpu_custom_call" | custom-call | flops 2415919104 | bytes 6291456 | tf_op jit(solution)/shard_map/attention/pallas_call | solution.py:559
  198.5 5.8 %local_tiles.3.base = f32[16,128,256]{2,1,0:T(8,128)} custom-call(s32[8,60]{1,0:T(8,128)S(1)} %copy-done.17, bf16[96,128,128]{2,1,0:T(8,128)(2,1)S(1)} %copy-done, bf16[16,128,256]{2,1,0:T(8,128)(2,1)} %get-tuple-element.28.refs_0_, bf16[16,128,256]{2,1,0:T(8,128)(2,1)} %collective-permute-done.12.refs_1_, ...), custom_call_target="tpu_custom_call" | custom-call | flops 402653184 | bytes 9437184 | tf_op jit(solution)/shard_map/local_tiles/pallas_call | solution.py:438
  204.3 18.8 %all-to-all-done.1.blocks = bf16[64,128,256]{2,1,0:T(8,128)(2,1)} async-done(((bf16[64,128,256]{2,1,0:T(8,128)(2,1)}), bf16[64,128,256]{2,1,0:T(8,128)(2,1)}, u32[]{:S(2)}, u32[]{:S(2)}) %all-to-all-start.1) | async-done | bytes 4194336 | tf_op jit(solution)/shard_map/all_to_all | solution.py:635
  223.2 4.7 %halo_tiles_norm.1 = bf16[16,128,256]{2,1,0:T(8,128)(2,1)} custom-call(s32[8,60]{1,0:T(8,128)S(1)} %copy-done.15, bf16[96,128,128]{2,1,0:T(8,128)(2,1)S(1)} %copy-done, bf16[64,128,256]{2,1,0:T(8,128)(2,1)} %all-to-all-done.1.blocks, f32[16,128,256]{2,1,0:T(8,128)} %local_tiles.3.base, f32[1,256]{1,0:T(1,128)S(1)} %bitcast.7), custom_call_target="tpu_custom_call" | custom-call | tf_op jit(solution)/shard_map/halo_tiles_norm/pallas_call | solution.py:598
  (110 shorter events, 57.5 us)
Async XLA Ops:
  4.1 109.9 %all-to-all-start = ((bf16[64,128,256]{2,1,0:T(8,128)(2,1)}), bf16[64,128,256]{2,1,0:T(8,128)(2,1)}, u32[]{:S(2)}, u32[]{:S(2)}) async-start(bf16[64,128,256]{2,1,0:T(8,128)(2,1)} %project_send.1.after), calls=%async_computation | async-start | bytes 8388608 | tf_op jit(solution)/shard_map/all_to_all | solution.py:628
  23.2 70.7 %copy-start = (bf16[96,128,128]{2,1,0:T(8,128)(2,1)S(1)}, bf16[96,128,128]{2,1,0:T(8,128)(2,1)}, u32[]{:S(2)}) copy-start(bf16[96,128,128]{2,1,0:T(8,128)(2,1)} %tiles.7) | copy-start | bytes 9437188
  23.2 67.7 %collective-permute-start = (bf16[16,128,256]{2,1,0:T(8,128)(2,1)}, bf16[16,128,256]{2,1,0:T(8,128)(2,1)}, u32[]{:S(2)}, u32[]{:S(2)}) collective-permute-start(bf16[16,128,256]{2,1,0:T(8,128)(2,1)} %project_own.1.after.refs_0_), channel_id=1, source_target_pairs={{0,1},{1,2},{2,3},{3,0},{4,5},{5,6},{6,7},{7,4},{8,9},{9,10},{10,1... | collective-permute-start | bytes 3145736 | tf_op jit(solution)/shard_map/ppermute | solution.py:614
  24.6 68.6 %collective-permute-start.1 = (bf16[16,128,256]{2,1,0:T(8,128)(2,1)}, bf16[16,128,256]{2,1,0:T(8,128)(2,1)}, u32[]{:S(2)}, u32[]{:S(2)}) collective-permute-start(bf16[16,128,256]{2,1,0:T(8,128)(2,1)} %project_own.1.after.refs_0_), channel_id=1, source_target_pairs={{0,2},{1,3},{2,0},{3,1},{4,6},{5,7},{6,4},{7,5},{8,10},{9,11},{10,... | collective-permute-start | bytes 3145736 | tf_op jit(solution)/shard_map/ppermute | solution.py:614
  27.2 66.6 %collective-permute-start.2 = (bf16[16,128,256]{2,1,0:T(8,128)(2,1)}, bf16[16,128,256]{2,1,0:T(8,128)(2,1)}, u32[]{:S(2)}, u32[]{:S(2)}) collective-permute-start(bf16[16,128,256]{2,1,0:T(8,128)(2,1)} %project_own.1.after.refs_0_), channel_id=1, source_target_pairs={{0,3},{1,0},{2,1},{3,2},{4,7},{5,4},{6,5},{7,6},{8,11},{9,8},{10,9... | collective-permute-start | bytes 3145736 | tf_op jit(solution)/shard_map/ppermute | solution.py:614
  35.4 2.8 %collective-permute-start.3 = (f32[264,256]{1,0:T(8,128)S(1)}, f32[264,256]{1,0:T(8,128)}, u32[]{:S(2)}, u32[]{:S(2)}) collective-permute-start(f32[264,256]{1,0:T(8,128)S(1)} %attention_sums.1.mine), channel_id=1, source_target_pairs={{0,4},{4,0},{8,12},{12,8},{16,20},{20,16},{24,28},{28,24},{32,36},... | collective-permute-start | bytes 811016 | tf_op jit(solution)/shard_map/ppermute | solution.py:295
  40.0 6.4 %collective-permute-start.4 = (f32[136,256]{1,0:T(8,128)}, f32[136,256]{1,0:T(8,128)S(1)}, u32[]{:S(2)}, u32[]{:S(2)}) collective-permute-start(f32[136,256]{1,0:T(8,128)} %get-tuple-element.20), channel_id=1, source_target_pairs={{0,64},{4,68},{8,72},{12,76},{16,80},{20,84},{24,88},{28,92},{32,9... | collective-permute-start | bytes 417800 | tf_op jit(solution)/shard_map/ppermute | solution.py:295
  48.7 5.7 %collective-permute-start.5 = (f32[72,256]{1,0:T(8,128)}, f32[72,256]{1,0:T(8,128)S(1)}, u32[]{:S(2)}, u32[]{:S(2)}) collective-permute-start(f32[72,256]{1,0:T(8,128)} %get-tuple-element.22), channel_id=1, source_target_pairs={{0,128},{4,132},{8,136},{12,140},{16,144},{20,148},{24,152},{28,15... | collective-permute-start | bytes 221192 | tf_op jit(solution)/shard_map/ppermute | solution.py:295
  56.6 16.3 %collective-permute-start.6 = (f32[40,256]{1,0:T(8,128)}, f32[40,256]{1,0:T(8,128)S(1)}, u32[]{:S(2)}, u32[]{:S(2)}) collective-permute-start(f32[40,256]{1,0:T(8,128)} %get-tuple-element.24), channel_id=1, source_target_pairs={{0,1},{1,0},{2,3},{3,2},{4,5},{5,4},{6,7},{7,6},{8,9},{9,8},{10,11... | collective-permute-start | bytes 122888 | tf_op jit(solution)/shard_map/ppermute | solution.py:295
  75.0 6.2 %collective-permute-start.7 = (f32[24,256]{1,0:T(8,128)}, f32[24,256]{1,0:T(8,128)S(1)}, u32[]{:S(2)}, u32[]{:S(2)}) collective-permute-start(f32[24,256]{1,0:T(8,128)} %get-tuple-element.26), channel_id=1, source_target_pairs={{0,2},{1,3},{2,0},{3,1},{4,6},{5,7},{6,4},{7,5},{8,10},{9,11},{10,... | collective-permute-start | bytes 73736 | tf_op jit(solution)/shard_map/ppermute | solution.py:295
  83.2 30.3 %collective-permute-start.8 = (f32[24,256]{1,0:T(8,128)}, f32[24,256]{1,0:T(8,128)S(1)}, u32[]{:S(2)}, u32[]{:S(2)}) collective-permute-start(f32[24,256]{1,0:T(8,128)} %merge_sums.3.refs_4_.refs_0_), channel_id=1, source_target_pairs={{0,16},{4,36},{8,24},{12,44},{16,32},{20,52},{24,40},{28,60},{32,4... | collective-permute-start | bytes 73736 | tf_op jit(solution)/shard_map/ppermute | solution.py:315
  88.7 24.8 %collective-permute-start.9 = (f32[24,256]{1,0:T(8,128)}, f32[24,256]{1,0:T(8,128)S(1)}, u32[]{:S(2)}, u32[]{:S(2)}) collective-permute-start(f32[24,256]{1,0:T(8,128)} %merge_sums.3.refs_4_.refs_0_), channel_id=1, source_target_pairs={{0,48},{4,28},{8,56},{12,36},{16,0},{20,44},{24,8},{28,52},{32,16}... | collective-permute-start | bytes 73736 | tf_op jit(solution)/shard_map/ppermute | solution.py:315
  91.0 22.6 %collective-permute-start.10 = (f32[24,256]{1,0:T(8,128)}, f32[24,256]{1,0:T(8,128)S(1)}, u32[]{:S(2)}, u32[]{:S(2)}) collective-permute-start(f32[24,256]{1,0:T(8,128)} %merge_sums.3.refs_4_.refs_0_), channel_id=1, source_target_pairs={{0,8},{4,44},{8,16},{12,52},{16,24},{20,60},{24,32},{28,4},{32,40}... | collective-permute-start | bytes 73736 | tf_op jit(solution)/shard_map/ppermute | solution.py:315
  93.2 20.4 %collective-permute-start.11 = (f32[24,256]{1,0:T(8,128)}, f32[24,256]{1,0:T(8,128)S(1)}, u32[]{:S(2)}, u32[]{:S(2)}) collective-permute-start(f32[24,256]{1,0:T(8,128)} %merge_sums.3.refs_4_.refs_0_), channel_id=1, source_target_pairs={{0,56},{8,0},{16,8},{24,16},{32,24},{40,32},{48,40},{56,48},{64,12... | collective-permute-start | bytes 73736 | tf_op jit(solution)/shard_map/ppermute | solution.py:315
  119.5 68.6 %copy-start.23 = (bf16[256,256]{1,0:T(8,128)(2,1)S(1)}, bf16[256,256]{1,0:T(8,128)(2,1)}, u32[]{:S(2)}) copy-start(bf16[256,256]{1,0:T(8,128)(2,1)} %vw.3) | copy-start | bytes 393220
  119.5 103.7 %all-to-all-start.1 = ((bf16[64,128,256]{2,1,0:T(8,128)(2,1)}), bf16[64,128,256]{2,1,0:T(8,128)(2,1)}, u32[]{:S(2)}, u32[]{:S(2)}) async-start(bf16[64,128,256]{2,1,0:T(8,128)(2,1)} %get-tuple-element.27), calls=%async_computation.1 | async-start | bytes 8388608 | tf_op jit(solution)/shard_map/all_to_all | solution.py:635
  127.3 71.2 %collective-permute-start.12 = (bf16[16,128,256]{2,1,0:T(8,128)(2,1)}, bf16[16,128,256]{2,1,0:T(8,128)(2,1)}, u32[]{:S(2)}, u32[]{:S(2)}) collective-permute-start(bf16[16,128,256]{2,1,0:T(8,128)(2,1)} %get-tuple-element.28.refs_0_), channel_id=1, source_target_pairs={{0,1},{1,2},{2,3},{3,0},{4,5},{5,6},{6,7},{7,4},{8,9},{9,10},{10,1... | collective-permute-start | bytes 3145736 | tf_op jit(solution)/shard_map/ppermute | solution.py:614
  128.9 69.6 %collective-permute-start.13 = (bf16[16,128,256]{2,1,0:T(8,128)(2,1)}, bf16[16,128,256]{2,1,0:T(8,128)(2,1)}, u32[]{:S(2)}, u32[]{:S(2)}) collective-permute-start(bf16[16,128,256]{2,1,0:T(8,128)(2,1)} %get-tuple-element.28.refs_0_), channel_id=1, source_target_pairs={{0,2},{1,3},{2,0},{3,1},{4,6},{5,7},{6,4},{7,5},{8,10},{9,11},{10,... | collective-permute-start | bytes 3145736 | tf_op jit(solution)/shard_map/ppermute | solution.py:614
  132.2 66.3 %collective-permute-start.14 = (bf16[16,128,256]{2,1,0:T(8,128)(2,1)}, bf16[16,128,256]{2,1,0:T(8,128)(2,1)}, u32[]{:S(2)}, u32[]{:S(2)}) collective-permute-start(bf16[16,128,256]{2,1,0:T(8,128)(2,1)} %get-tuple-element.28.refs_0_), channel_id=1, source_target_pairs={{0,3},{1,0},{2,1},{3,2},{4,7},{5,4},{6,5},{7,6},{8,11},{9,8},{10,9... | collective-permute-start | bytes 3145736 | tf_op jit(solution)/shard_map/ppermute | solution.py:614
  134.5 2.4 %collective-permute-start.15 = (f32[24,256]{1,0:T(8,128)}, f32[24,256]{1,0:T(8,128)S(1)}, u32[]{:S(2)}, u32[]{:S(2)}) collective-permute-start(f32[24,256]{1,0:T(8,128)} %merge_sums.4.refs_0_), channel_id=1, source_target_pairs={{0,4},{4,0},{8,12},{12,8},{16,20},{20,16},{24,28},{28,24},{32,36},... | collective-permute-start | bytes 73736 | tf_op jit(solution)/shard_map/ppermute | solution.py:295
  139.6 4.8 %collective-permute-start.16 = (f32[16,256]{1,0:T(8,128)S(1)}, f32[16,256]{1,0:T(8,128)S(1)}, u32[]{:S(2)}, u32[]{:S(2)}) collective-permute-start(f32[16,256]{1,0:T(8,128)S(1)} %slice.8.mine), channel_id=1, source_target_pairs={{0,128},{4,132},{8,136},{12,140},{16,144},{20,148},{24,152},{28,15... | collective-permute-start | bytes 49160 | tf_op jit(solution)/shard_map/ppermute | solution.py:295
  146.4 3.8 %collective-permute-start.17 = (f32[32,256]{1,0:T(8,128)}, f32[32,256]{1,0:T(8,128)S(1)}, u32[]{:S(2)}, u32[]{:S(2)}) collective-permute-start(f32[32,256]{1,0:T(8,128)} %join_sums.4.mine), channel_id=1, source_target_pairs={{0,64},{4,68},{8,72},{12,76},{16,80},{20,84},{24,88},{28,92},{32,9... | collective-permute-start | bytes 98312 | tf_op jit(solution)/shard_map/ppermute | solution.py:295
  152.2 26.9 %collective-permute-start.18 = (f32[64,256]{1,0:T(8,128)}, f32[64,256]{1,0:T(8,128)S(1)}, u32[]{:S(2)}, u32[]{:S(2)}) collective-permute-start(f32[64,256]{1,0:T(8,128)} %join_sums.5.mine), channel_id=1, source_target_pairs={{0,2},{1,3},{2,0},{3,1},{4,6},{5,7},{6,4},{7,5},{8,10},{9,11},{10,... | collective-permute-start | bytes 196616 | tf_op jit(solution)/shard_map/ppermute | solution.py:295
  181.3 4.4 %collective-permute-start.19 = (f32[128,256]{1,0:T(8,128)}, f32[128,256]{1,0:T(8,128)S(1)}, u32[]{:S(2)}, u32[]{:S(2)}) collective-permute-start(f32[128,256]{1,0:T(8,128)} %join_sums.6.mine), channel_id=1, source_target_pairs={{0,1},{1,0},{2,3},{3,2},{4,5},{5,4},{6,7},{7,6},{8,9},{9,8},{10,11... | collective-permute-start | bytes 393224 | tf_op jit(solution)/shard_map/ppermute | solution.py:295
  (32 other events, 176.4 us)

commit v6 on v5

--- a/solution.py
+++ b/solution.py
@@ -9,7 +9,7 @@
 
 D = 256
 BLOCK = 128
-PAIRS = 4
+PAIRS = 8
 CHUNK = 256
 NORM = 4
 EXTRA = 8
@@ -446,7 +446,7 @@
             pltpu.VMEM((nblocks, BLOCK, D), F32),
             pltpu.SemaphoreType.DMA((len(parts) + 2,)),
         ],
-        compiler_params=params(20),
+        compiler_params=params(24),
         cost_estimate=cost(48 * BLOCK * BLOCK * D * 2, 9 << 20),
         name="local_tiles",
     )(steps, tiles, *map(in_hbm, parts), in_hbm(base))
@@ -524,7 +524,7 @@
         in_specs=[SMEM, SMEM, VMEM, HBM, HBM] + [HBM] * len(after),
         out_specs=(HBM, HBM),
         scratch_shapes=halo_scratch(steps, part) + send_scratch(nblocks, blocks.shape[0]),
-        compiler_params=params(20),
+        compiler_params=params(24),
         name="halo_tiles_send",
     )(send, steps, tiles, in_hbm(blocks), in_hbm(part), *after)
 
@@ -603,7 +603,7 @@
         scratch_shapes=halo_scratch(steps, base) + [
             pltpu.VMEM((nblocks, BLOCK, D), BF16), pltpu.SemaphoreType.DMA,
         ],
-        compiler_params=params(20),
+        compiler_params=params(24),
         name="halo_tiles_norm",
     )(steps, tiles, in_hbm(blocks), in_hbm(base), gain)
 

time: 230 us -> 230 us (level)
  no operation moved by 1% of the time
where the time goes in v6:
time: 230 us; the launch traced here: 229 us
  waiting for transfers between devices  91.2 us (40%)
  Pallas kernels  60.3 us (26%)
  starting transfers between devices  60.1 us (26%)
  local copies, waits for them, and re-layouts  15.8 us (7%)
    ppermute x10, waiting for transfers between devices, swap(): lax.ppermute(x, axis, [(i, i ^ 1 << bit) for i in range(lax.axis_size(axi...  58.9 us
    all_to_all x2, starting transfers between devices, shards(): received = lax.all_to_all(outgoing, 'wide', 0, 0, tiled=True)  21.2 us
    all_to_all x2, waiting for transfers between devices, shards(): received = lax.all_to_all(outgoing, 'wide', 0, 0, tiled=True)  20.2 us
    ppermute x10, starting transfers between devices, swap(): lax.ppermute(x, axis, [(i, i ^ 1 << bit) for i in range(lax.axis_size(axi...  16.4 us
    unnamed x68, local copies, waits for them, and re-layouts  14.4 us
    ppermute x4, starting transfers between devices, along_depth(): return [lax.ppermute(mine, 'wide', shift(by)) for by in AROUND]  12.2 us
    ppermute x4, waiting for transfers between devices, along_depth(): return [lax.ppermute(mine, 'wide', shift(by)) for by in AROUND]  12.1 us
    pallas_call x2, Pallas kernels, local_tiles(): pl.pallas_call(functools.partial(local_kernel, len(parts)), out_shape=plt...  10.6 us
  transfers between devices with their start and end apart: 22, of which 12 were waited for; matrix products, arithmetic and copies ran while one was open for 1% of the time, Pallas kernels for 20%

profile of v6, /device:TPU:1, one launch (start us, length us, event | category | flops | bytes accessed | tf_op | source)
XLA Modules:
  0.0 228.5 jit_solution(1094444061145625531)
XLA Ops:
  0.0 4.0 %project_send.1.after = bf16[64,128,256]{2,1,0:T(8,128)(2,1)} custom-call(s32[1,64]{1,0:T(1,128)} %send.3, bf16[2048,256]{1,0:T(8,128)(2,1)} %x.7, bf16[256,256]{1,0:T(8,128)(2,1)} %weight.3), custom_call_target="tpu_custom_call" | custom-call | tf_op jit(solution)/shard_map/project_send/pallas_call | solution.py:126
  4.0 13.3 %all-to-all-start = ((bf16[64,128,256]{2,1,0:T(8,128)(2,1)}), bf16[64,128,256]{2,1,0:T(8,128)(2,1)}, u32[]{:S(2)}, u32[]{:S(2)}) async-start(bf16[64,128,256]{2,1,0:T(8,128)(2,1)} %project_send.1.after), calls=%async_computation | async-start | bytes 8388608 | tf_op jit(solution)/shard_map/all_to_all | solution.py:628
  19.5 3.7 %project_own.1.after.refs_0_ = bf16[16,128,256]{2,1,0:T(8,128)(2,1)} custom-call(bf16[2048,256]{1,0:T(8,128)(2,1)S(1)} %copy-done.4, bf16[256,256]{1,0:T(8,128)(2,1)S(1)} %copy-done.8, bf16[64,128,256]{2,1,0:T(8,128)(2,1)S(1)} %copy-done.1), custom_call_target="tpu_custom_call" | custom-call | tf_op jit(solution)/shard_map/project_own/pallas_call | solution.py:152
  24.6 2.5 %collective-permute-start.1 = (bf16[16,128,256]{2,1,0:T(8,128)(2,1)}, bf16[16,128,256]{2,1,0:T(8,128)(2,1)}, u32[]{:S(2)}, u32[]{:S(2)}) collective-permute-start(bf16[16,128,256]{2,1,0:T(8,128)(2,1)} %project_own.1.after.refs_0_), channel_id=1, source_target_pairs={{0,2},{1,3},{2,0},{3,1},{4,6},{5,7},{6,4},{7,5},{8,10},{9,11},{10,... | collective-permute-start | bytes 3145736 | tf_op jit(solution)/shard_map/ppermute | solution.py:614
  29.5 5.8 %attention_sums.1.mine = f32[264,256]{1,0:T(8,128)S(1)} custom-call(bf16[2048,256]{1,0:T(8,128)(2,1)S(1)} %copy-done.5, bf16[256,256]{1,0:T(8,128)(2,1)S(1)} %copy-done.21, bf16[256,256]{1,0:T(8,128)(2,1)S(1)} %copy-done.20, bf16[256,256]{1,0:T(8,128)(2,1)S(1)} %copy-done.22, bf16[16,128,256]{2,1,0:T(8,128)(2,1)S(1)} %copy-done.2), custom_call_target="tpu_custom_call" | custom-call | flops 2415919104 | bytes 2097152 | tf_op jit(solution)/shard_map/attention_sums/pallas_call | solution.py:214
  41.2 5.1 %collective-permute-done.4.other = f32[136,256]{1,0:T(8,128)S(1)} collective-permute-done((f32[136,256]{1,0:T(8,128)}, f32[136,256]{1,0:T(8,128)S(1)}, u32[]{:S(2)}, u32[]{:S(2)}) %collective-permute-start.4) | collective-permute-done | bytes 139296 | tf_op jit(solution)/shard_map/ppermute | solution.py:295
  48.6 2.9 %collective-permute-start.5 = (f32[72,256]{1,0:T(8,128)}, f32[72,256]{1,0:T(8,128)S(1)}, u32[]{:S(2)}, u32[]{:S(2)}) collective-permute-start(f32[72,256]{1,0:T(8,128)} %get-tuple-element.22), channel_id=1, source_target_pairs={{0,128},{4,132},{8,136},{12,140},{16,144},{20,148},{24,152},{28,15... | collective-permute-start | bytes 221192 | tf_op jit(solution)/shard_map/ppermute | solution.py:295
  51.5 2.9 %collective-permute-done.5.other = f32[72,256]{1,0:T(8,128)S(1)} collective-permute-done((f32[72,256]{1,0:T(8,128)}, f32[72,256]{1,0:T(8,128)S(1)}, u32[]{:S(2)}, u32[]{:S(2)}) %collective-permute-start.5) | collective-permute-done | bytes 73760 | tf_op jit(solution)/shard_map/ppermute | solution.py:295
  57.8 14.8 %collective-permute-done.6.other = f32[40,256]{1,0:T(8,128)S(1)} collective-permute-done((f32[40,256]{1,0:T(8,128)}, f32[40,256]{1,0:T(8,128)S(1)}, u32[]{:S(2)}, u32[]{:S(2)}) %collective-permute-start.6) | collective-permute-done | bytes 40992 | tf_op jit(solution)/shard_map/ppermute | solution.py:295
  74.7 3.0 %collective-permute-start.7 = (f32[24,256]{1,0:T(8,128)}, f32[24,256]{1,0:T(8,128)S(1)}, u32[]{:S(2)}, u32[]{:S(2)}) collective-permute-start(f32[24,256]{1,0:T(8,128)} %get-tuple-element.26), channel_id=1, source_target_pairs={{0,2},{1,3},{2,0},{3,1},{4,6},{5,7},{6,4},{7,5},{8,10},{9,11},{10,... | collective-permute-start | bytes 73736 | tf_op jit(solution)/shard_map/ppermute | solution.py:295
  78.3 3.3 %plan_tiles.1 = (s32[8,64]{1,0:T(8,128)}, s32[8,64]{1,0:T(8,128)}) custom-call(s32[1,96]{1,0:T(1,128)} %rows.1, s32[1,96]{1,0:T(1,128)} %cols.1, s32[1]{0:T(128)S(6)} %copy.12.count, bf16[16,128,256]{2,1,0:T(8,128)(2,1)} %project_own.1.after.refs_0_), custom_call_target="tpu_custom_call" | custom-call | tf_op jit(solution)/shard_map/plan_tiles/pallas_call | solution.py:379
  83.6 7.1 %collective-permute-start.8 = (f32[24,256]{1,0:T(8,128)}, f32[24,256]{1,0:T(8,128)S(1)}, u32[]{:S(2)}, u32[]{:S(2)}) collective-permute-start(f32[24,256]{1,0:T(8,128)} %merge_sums.3.refs_4_.refs_0_), channel_id=1, source_target_pairs={{0,16},{4,36},{8,24},{12,44},{16,32},{20,52},{24,40},{28,60},{32,4... | collective-permute-start | bytes 73736 | tf_op jit(solution)/shard_map/ppermute | solution.py:315
  90.7 4.5 %collective-permute-start.10 = (f32[24,256]{1,0:T(8,128)}, f32[24,256]{1,0:T(8,128)S(1)}, u32[]{:S(2)}, u32[]{:S(2)}) collective-permute-start(f32[24,256]{1,0:T(8,128)} %merge_sums.3.refs_4_.refs_0_), channel_id=1, source_target_pairs={{0,8},{4,44},{8,16},{12,52},{16,24},{20,60},{24,32},{28,4},{32,40}... | collective-permute-start | bytes 73736 | tf_op jit(solution)/shard_map/ppermute | solution.py:315
  96.5 4.9 %local_tiles.2.part = f32[16,128,256]{2,1,0:T(8,128)} custom-call(s32[8,64]{1,0:T(8,128)S(1)} %copy-done.16, bf16[96,128,128]{2,1,0:T(8,128)(2,1)S(1)} %copy-done, bf16[16,128,256]{2,1,0:T(8,128)(2,1)} %project_own.1.after.refs_0_, bf16[16,128,256]{2,1,0:T(8,128)(2,1)} %collective-permute-done.refs_1_, bf16[16,128,256]{2,1,0:T(8,128)(2,1)} %collective-permute-done.1.refs_2_, ...), custom_call_target="tpu_custom_call" | custom-call | flops 402653184 | bytes 9437184 | tf_op jit(solution)/shard_map/local_tiles/pallas_call | solution.py:438
  101.4 12.1 %collective-permute-done.8.refs_0_.refs_1_ = f32[24,256]{1,0:T(8,128)S(1)} collective-permute-done((f32[24,256]{1,0:T(8,128)}, f32[24,256]{1,0:T(8,128)S(1)}, u32[]{:S(2)}, u32[]{:S(2)}) %collective-permute-start.8) | collective-permute-done | bytes 24608 | tf_op jit(solution)/shard_map/ppermute | solution.py:315
  114.0 5.6 %halo_tiles_send.1 = (bf16[16,128,256]{2,1,0:T(8,128)(2,1)}, bf16[64,128,256]{2,1,0:T(8,128)(2,1)}) custom-call(s32[1,64]{1,0:T(1,128)S(1)} %copy-done.18, s32[8,64]{1,0:T(8,128)S(1)} %copy-done.15, bf16[96,128,128]{2,1,0:T(8,128)(2,1)S(1)} %copy-done, bf16[64,128,256]{2,1,0:T(8,128)(2,1)} %all-to-all-done.blocks, f32[16,128,256]{2,1,0:T(8,128)} %local_tiles.2.part, ...), custom_call_target="tpu_custom_call" | custom-call | tf_op jit(solution)/shard_map/halo_tiles_send/pallas_call | solution.py:521
  119.7 8.0 %all-to-all-start.1 = ((bf16[64,128,256]{2,1,0:T(8,128)(2,1)}), bf16[64,128,256]{2,1,0:T(8,128)(2,1)}, u32[]{:S(2)}, u32[]{:S(2)}) async-start(bf16[64,128,256]{2,1,0:T(8,128)(2,1)} %get-tuple-element.27), calls=%async_computation.1 | async-start | bytes 8388608 | tf_op jit(solution)/shard_map/all_to_all | solution.py:635
  139.3 2.8 %collective-permute-start.16 = (f32[16,256]{1,0:T(8,128)S(1)}, f32[16,256]{1,0:T(8,128)S(1)}, u32[]{:S(2)}, u32[]{:S(2)}) collective-permute-start(f32[16,256]{1,0:T(8,128)S(1)} %slice.8.mine), channel_id=1, source_target_pairs={{0,128},{4,132},{8,136},{12,140},{16,144},{20,148},{24,152},{28,15... | collective-permute-start | bytes 49160 | tf_op jit(solution)/shard_map/ppermute | solution.py:295
  147.4 2.9 %collective-permute-done.17.other = f32[32,256]{1,0:T(8,128)S(1)} collective-permute-done((f32[32,256]{1,0:T(8,128)}, f32[32,256]{1,0:T(8,128)S(1)}, u32[]{:S(2)}, u32[]{:S(2)}) %collective-permute-start.17) | collective-permute-done | bytes 32800 | tf_op jit(solution)/shard_map/ppermute | solution.py:295
  152.3 26.3 %collective-permute-done.18.other = f32[64,256]{1,0:T(8,128)S(1)} collective-permute-done((f32[64,256]{1,0:T(8,128)}, f32[64,256]{1,0:T(8,128)S(1)}, u32[]{:S(2)}, u32[]{:S(2)}) %collective-permute-start.18) | collective-permute-done | bytes 65568 | tf_op jit(solution)/shard_map/ppermute | solution.py:295
  192.2 5.8 %attention.1 = f32[2048,256]{1,0:T(8,128)} custom-call(bf16[2048,256]{1,0:T(8,128)(2,1)S(1)} %copy-done.6, bf16[256,256]{1,0:T(8,128)(2,1)S(1)} %copy-done.21, bf16[256,256]{1,0:T(8,128)(2,1)S(1)} %copy-done.23, f32[256,256]{1,0:T(8,128)S(1)} %copy-done.10, f32[8,256]{1,0:T(8,128)S(1)} %slice.9.extra, bf16[2048,256]{1,0:T(8,128)(2,1)S(1)} %bitcast.5, ...), custom_call_target="tpu_custom_call" | custom-call | flops 2415919104 | bytes 6291456 | tf_op jit(solution)/shard_map/attention/pallas_call | solution.py:559
  198.0 5.7 %local_tiles.3.base = f32[16,128,256]{2,1,0:T(8,128)} custom-call(s32[8,64]{1,0:T(8,128)S(1)} %copy-done.17, bf16[96,128,128]{2,1,0:T(8,128)(2,1)S(1)} %copy-done, bf16[16,128,256]{2,1,0:T(8,128)(2,1)} %get-tuple-element.28.refs_0_, bf16[16,128,256]{2,1,0:T(8,128)(2,1)} %collective-permute-done.12.refs_1_, ...), custom_call_target="tpu_custom_call" | custom-call | flops 402653184 | bytes 9437184 | tf_op jit(solution)/shard_map/local_tiles/pallas_call | solution.py:438
  203.7 19.8 %all-to-all-done.1.blocks = bf16[64,128,256]{2,1,0:T(8,128)(2,1)} async-done(((bf16[64,128,256]{2,1,0:T(8,128)(2,1)}), bf16[64,128,256]{2,1,0:T(8,128)(2,1)}, u32[]{:S(2)}, u32[]{:S(2)}) %all-to-all-start.1) | async-done | bytes 4194336 | tf_op jit(solution)/shard_map/all_to_all | solution.py:635
  223.5 4.8 %halo_tiles_norm.1 = bf16[16,128,256]{2,1,0:T(8,128)(2,1)} custom-call(s32[8,64]{1,0:T(8,128)S(1)} %copy-done.15, bf16[96,128,128]{2,1,0:T(8,128)(2,1)S(1)} %copy-done, bf16[64,128,256]{2,1,0:T(8,128)(2,1)} %all-to-all-done.1.blocks, f32[16,128,256]{2,1,0:T(8,128)} %local_tiles.3.base, f32[1,256]{1,0:T(1,128)S(1)} %bitcast.7), custom_call_target="tpu_custom_call" | custom-call | tf_op jit(solution)/shard_map/halo_tiles_norm/pallas_call | solution.py:598
  (110 shorter events, 55.9 us)
Async XLA Ops:
  4.0 110.0 %all-to-all-start = ((bf16[64,128,256]{2,1,0:T(8,128)(2,1)}), bf16[64,128,256]{2,1,0:T(8,128)(2,1)}, u32[]{:S(2)}, u32[]{:S(2)}) async-start(bf16[64,128,256]{2,1,0:T(8,128)(2,1)} %project_send.1.after), calls=%async_computation | async-start | bytes 8388608 | tf_op jit(solution)/shard_map/all_to_all | solution.py:628
  23.2 72.6 %copy-start = (bf16[96,128,128]{2,1,0:T(8,128)(2,1)S(1)}, bf16[96,128,128]{2,1,0:T(8,128)(2,1)}, u32[]{:S(2)}) copy-start(bf16[96,128,128]{2,1,0:T(8,128)(2,1)} %tiles.7) | copy-start | bytes 9437188
  23.2 67.5 %collective-permute-start = (bf16[16,128,256]{2,1,0:T(8,128)(2,1)}, bf16[16,128,256]{2,1,0:T(8,128)(2,1)}, u32[]{:S(2)}, u32[]{:S(2)}) collective-permute-start(bf16[16,128,256]{2,1,0:T(8,128)(2,1)} %project_own.1.after.refs_0_), channel_id=1, source_target_pairs={{0,1},{1,2},{2,3},{3,0},{4,5},{5,6},{6,7},{7,4},{8,9},{9,10},{10,1... | collective-permute-start | bytes 3145736 | tf_op jit(solution)/shard_map/ppermute | solution.py:614
  24.6 70.6 %collective-permute-start.1 = (bf16[16,128,256]{2,1,0:T(8,128)(2,1)}, bf16[16,128,256]{2,1,0:T(8,128)(2,1)}, u32[]{:S(2)}, u32[]{:S(2)}) collective-permute-start(bf16[16,128,256]{2,1,0:T(8,128)(2,1)} %project_own.1.after.refs_0_), channel_id=1, source_target_pairs={{0,2},{1,3},{2,0},{3,1},{4,6},{5,7},{6,4},{7,5},{8,10},{9,11},{10,... | collective-permute-start | bytes 3145736 | tf_op jit(solution)/shard_map/ppermute | solution.py:614
  27.1 68.8 %collective-permute-start.2 = (bf16[16,128,256]{2,1,0:T(8,128)(2,1)}, bf16[16,128,256]{2,1,0:T(8,128)(2,1)}, u32[]{:S(2)}, u32[]{:S(2)}) collective-permute-start(bf16[16,128,256]{2,1,0:T(8,128)(2,1)} %project_own.1.after.refs_0_), channel_id=1, source_target_pairs={{0,3},{1,0},{2,1},{3,2},{4,7},{5,4},{6,5},{7,6},{8,11},{9,8},{10,9... | collective-permute-start | bytes 3145736 | tf_op jit(solution)/shard_map/ppermute | solution.py:614
  35.4 2.8 %collective-permute-start.3 = (f32[264,256]{1,0:T(8,128)S(1)}, f32[264,256]{1,0:T(8,128)}, u32[]{:S(2)}, u32[]{:S(2)}) collective-permute-start(f32[264,256]{1,0:T(8,128)S(1)} %attention_sums.1.mine), channel_id=1, source_target_pairs={{0,4},{4,0},{8,12},{12,8},{16,20},{20,16},{24,28},{28,24},{32,36},... | collective-permute-start | bytes 811016 | tf_op jit(solution)/shard_map/ppermute | solution.py:295
  39.9 6.3 %collective-permute-start.4 = (f32[136,256]{1,0:T(8,128)}, f32[136,256]{1,0:T(8,128)S(1)}, u32[]{:S(2)}, u32[]{:S(2)}) collective-permute-start(f32[136,256]{1,0:T(8,128)} %get-tuple-element.20), channel_id=1, source_target_pairs={{0,64},{4,68},{8,72},{12,76},{16,80},{20,84},{24,88},{28,92},{32,9... | collective-permute-start | bytes 417800 | tf_op jit(solution)/shard_map/ppermute | solution.py:295
  48.6 5.7 %collective-permute-start.5 = (f32[72,256]{1,0:T(8,128)}, f32[72,256]{1,0:T(8,128)S(1)}, u32[]{:S(2)}, u32[]{:S(2)}) collective-permute-start(f32[72,256]{1,0:T(8,128)} %get-tuple-element.22), channel_id=1, source_target_pairs={{0,128},{4,132},{8,136},{12,140},{16,144},{20,148},{24,152},{28,15... | collective-permute-start | bytes 221192 | tf_op jit(solution)/shard_map/ppermute | solution.py:295
  56.6 16.0 %collective-permute-start.6 = (f32[40,256]{1,0:T(8,128)}, f32[40,256]{1,0:T(8,128)S(1)}, u32[]{:S(2)}, u32[]{:S(2)}) collective-permute-start(f32[40,256]{1,0:T(8,128)} %get-tuple-element.24), channel_id=1, source_target_pairs={{0,1},{1,0},{2,3},{3,2},{4,5},{5,4},{6,7},{7,6},{8,9},{9,8},{10,11... | collective-permute-start | bytes 122888 | tf_op jit(solution)/shard_map/ppermute | solution.py:295
  74.7 7.0 %collective-permute-start.7 = (f32[24,256]{1,0:T(8,128)}, f32[24,256]{1,0:T(8,128)S(1)}, u32[]{:S(2)}, u32[]{:S(2)}) collective-permute-start(f32[24,256]{1,0:T(8,128)} %get-tuple-element.26), channel_id=1, source_target_pairs={{0,2},{1,3},{2,0},{3,1},{4,6},{5,7},{6,4},{7,5},{8,10},{9,11},{10,... | collective-permute-start | bytes 73736 | tf_op jit(solution)/shard_map/ppermute | solution.py:295
  83.6 30.0 %collective-permute-start.8 = (f32[24,256]{1,0:T(8,128)}, f32[24,256]{1,0:T(8,128)S(1)}, u32[]{:S(2)}, u32[]{:S(2)}) collective-permute-start(f32[24,256]{1,0:T(8,128)} %merge_sums.3.refs_4_.refs_0_), channel_id=1, source_target_pairs={{0,16},{4,36},{8,24},{12,44},{16,32},{20,52},{24,40},{28,60},{32,4... | collective-permute-start | bytes 73736 | tf_op jit(solution)/shard_map/ppermute | solution.py:315
  90.7 22.9 %collective-permute-start.9 = (f32[24,256]{1,0:T(8,128)}, f32[24,256]{1,0:T(8,128)S(1)}, u32[]{:S(2)}, u32[]{:S(2)}) collective-permute-start(f32[24,256]{1,0:T(8,128)} %merge_sums.3.refs_4_.refs_0_), channel_id=1, source_target_pairs={{0,48},{4,28},{8,56},{12,36},{16,0},{20,44},{24,8},{28,52},{32,16}... | collective-permute-start | bytes 73736 | tf_op jit(solution)/shard_map/ppermute | solution.py:315
  90.7 22.9 %collective-permute-start.10 = (f32[24,256]{1,0:T(8,128)}, f32[24,256]{1,0:T(8,128)S(1)}, u32[]{:S(2)}, u32[]{:S(2)}) collective-permute-start(f32[24,256]{1,0:T(8,128)} %merge_sums.3.refs_4_.refs_0_), channel_id=1, source_target_pairs={{0,8},{4,44},{8,16},{12,52},{16,24},{20,60},{24,32},{28,4},{32,40}... | collective-permute-start | bytes 73736 | tf_op jit(solution)/shard_map/ppermute | solution.py:315
  95.2 18.4 %collective-permute-start.11 = (f32[24,256]{1,0:T(8,128)}, f32[24,256]{1,0:T(8,128)S(1)}, u32[]{:S(2)}, u32[]{:S(2)}) collective-permute-start(f32[24,256]{1,0:T(8,128)} %merge_sums.3.refs_4_.refs_0_), channel_id=1, source_target_pairs={{0,56},{8,0},{16,8},{24,16},{32,24},{40,32},{48,40},{56,48},{64,12... | collective-permute-start | bytes 73736 | tf_op jit(solution)/shard_map/ppermute | solution.py:315
  119.7 67.9 %copy-start.23 = (bf16[256,256]{1,0:T(8,128)(2,1)S(1)}, bf16[256,256]{1,0:T(8,128)(2,1)}, u32[]{:S(2)}) copy-start(bf16[256,256]{1,0:T(8,128)(2,1)} %vw.3) | copy-start | bytes 393220
  119.7 103.9 %all-to-all-start.1 = ((bf16[64,128,256]{2,1,0:T(8,128)(2,1)}), bf16[64,128,256]{2,1,0:T(8,128)(2,1)}, u32[]{:S(2)}, u32[]{:S(2)}) async-start(bf16[64,128,256]{2,1,0:T(8,128)(2,1)} %get-tuple-element.27), calls=%async_computation.1 | async-start | bytes 8388608 | tf_op jit(solution)/shard_map/all_to_all | solution.py:635
  127.7 70.3 %collective-permute-start.12 = (bf16[16,128,256]{2,1,0:T(8,128)(2,1)}, bf16[16,128,256]{2,1,0:T(8,128)(2,1)}, u32[]{:S(2)}, u32[]{:S(2)}) collective-permute-start(bf16[16,128,256]{2,1,0:T(8,128)(2,1)} %get-tuple-element.28.refs_0_), channel_id=1, source_target_pairs={{0,1},{1,2},{2,3},{3,0},{4,5},{5,6},{6,7},{7,4},{8,9},{9,10},{10,1... | collective-permute-start | bytes 3145736 | tf_op jit(solution)/shard_map/ppermute | solution.py:614
  129.5 68.5 %collective-permute-start.13 = (bf16[16,128,256]{2,1,0:T(8,128)(2,1)}, bf16[16,128,256]{2,1,0:T(8,128)(2,1)}, u32[]{:S(2)}, u32[]{:S(2)}) collective-permute-start(bf16[16,128,256]{2,1,0:T(8,128)(2,1)} %get-tuple-element.28.refs_0_), channel_id=1, source_target_pairs={{0,2},{1,3},{2,0},{3,1},{4,6},{5,7},{6,4},{7,5},{8,10},{9,11},{10,... | collective-permute-start | bytes 3145736 | tf_op jit(solution)/shard_map/ppermute | solution.py:614
  131.7 66.3 %collective-permute-start.14 = (bf16[16,128,256]{2,1,0:T(8,128)(2,1)}, bf16[16,128,256]{2,1,0:T(8,128)(2,1)}, u32[]{:S(2)}, u32[]{:S(2)}) collective-permute-start(bf16[16,128,256]{2,1,0:T(8,128)(2,1)} %get-tuple-element.28.refs_0_), channel_id=1, source_target_pairs={{0,3},{1,0},{2,1},{3,2},{4,7},{5,4},{6,5},{7,6},{8,11},{9,8},{10,9... | collective-permute-start | bytes 3145736 | tf_op jit(solution)/shard_map/ppermute | solution.py:614
  134.2 2.4 %collective-permute-start.15 = (f32[24,256]{1,0:T(8,128)}, f32[24,256]{1,0:T(8,128)S(1)}, u32[]{:S(2)}, u32[]{:S(2)}) collective-permute-start(f32[24,256]{1,0:T(8,128)} %merge_sums.4.refs_0_), channel_id=1, source_target_pairs={{0,4},{4,0},{8,12},{12,8},{16,20},{20,16},{24,28},{28,24},{32,36},... | collective-permute-start | bytes 73736 | tf_op jit(solution)/shard_map/ppermute | solution.py:295
  139.3 5.1 %collective-permute-start.16 = (f32[16,256]{1,0:T(8,128)S(1)}, f32[16,256]{1,0:T(8,128)S(1)}, u32[]{:S(2)}, u32[]{:S(2)}) collective-permute-start(f32[16,256]{1,0:T(8,128)S(1)} %slice.8.mine), channel_id=1, source_target_pairs={{0,128},{4,132},{8,136},{12,140},{16,144},{20,148},{24,152},{28,15... | collective-permute-start | bytes 49160 | tf_op jit(solution)/shard_map/ppermute | solution.py:295
  146.4 3.9 %collective-permute-start.17 = (f32[32,256]{1,0:T(8,128)}, f32[32,256]{1,0:T(8,128)S(1)}, u32[]{:S(2)}, u32[]{:S(2)}) collective-permute-start(f32[32,256]{1,0:T(8,128)} %join_sums.4.mine), channel_id=1, source_target_pairs={{0,64},{4,68},{8,72},{12,76},{16,80},{20,84},{24,88},{28,92},{32,9... | collective-permute-start | bytes 98312 | tf_op jit(solution)/shard_map/ppermute | solution.py:295
  152.3 26.3 %collective-permute-start.18 = (f32[64,256]{1,0:T(8,128)}, f32[64,256]{1,0:T(8,128)S(1)}, u32[]{:S(2)}, u32[]{:S(2)}) collective-permute-start(f32[64,256]{1,0:T(8,128)} %join_sums.5.mine), channel_id=1, source_target_pairs={{0,2},{1,3},{2,0},{3,1},{4,6},{5,7},{6,4},{7,5},{8,10},{9,11},{10,... | collective-permute-start | bytes 196616 | tf_op jit(solution)/shard_map/ppermute | solution.py:295
  180.7 4.4 %collective-permute-start.19 = (f32[128,256]{1,0:T(8,128)}, f32[128,256]{1,0:T(8,128)S(1)}, u32[]{:S(2)}, u32[]{:S(2)}) collective-permute-start(f32[128,256]{1,0:T(8,128)} %join_sums.6.mine), channel_id=1, source_target_pairs={{0,1},{1,0},{2,3},{3,2},{4,5},{5,4},{6,7},{7,6},{8,9},{9,8},{10,11... | collective-permute-start | bytes 393224 | tf_op jit(solution)/shard_map/ppermute | solution.py:295
  (32 other events, 174.2 us)
